TPU v7x, 32 devices: a whole 2x2x4 slice. The times are simulated.
32 devices in a mesh: section: 4 (over z), expert: 8 (over y, x, core).
Axes of the slice: x: 2, y: 2, z: 4, core: 2. Of those that a mesh axis runs over, the one named last changes fastest.
Arguments:
- acts: bfloat16 [4, 2048, 2048], P('section', 'expert'), may hold values from -6 to 6
- expert_ids: int32 [4, 2048, 2], P('section', 'expert'), may hold values from 0 to 7, all different within a row; in each aligned block of 256 rows (0 to 255, 256 to 511, ..., all dimensions but the last counted through in order) at most 96 rows name the same one
- router: bfloat16 [4, 2048, 8], P('section'), may hold values from -0.125 to 0.125
- skip_gain: float32 [4, 2048], P('section'), may hold values from 0.5 to 1.5
- skip_rows: bfloat16 [4, 2048, 2048], P('section', 'expert'), may hold values from -6 to 6
- w_in: bfloat16 [4, 8, 2048, 1024], P('section', 'expert'), may hold values from -0.125 to 0.125
- w_out: bfloat16 [4, 8, 1024, 2048], P('section', 'expert'), may hold values from -0.1875 to 0.1875
Outputs:
- handed: bfloat16 [4, 2048, 2048], P('section', 'expert')
- mirrored: bfloat16 [4, 2048, 2048], P('section', 'expert')
Inputs may be any that keep to these rules, and one draw needn't show every extreme that they name: `expert_ids`: each token names 2 different experts. Among the 256 tokens of one group no expert is named more than 96 times, a bound that some block reaches.
All inputs are finite; a program needn't handle non-finite values.
Results may differ from a plain program's by a relative error of at most 0.0041.
Values may be sent and summed in bfloat16 or wider, within the bound.
No kernel may reach another device: no remote copies, remote signals or barrier semaphores. Data moves between devices by JAX's collectives and lax.ppermute only.
A program may use at most 64 MiB of HBM per device.

v0:
```python
import jax
import jax.numpy as jnp
from jax import lax
from jax.sharding import PartitionSpec as P


def shifted(shard, axis, by):
    peers = lax.axis_size(axis)
    return lax.ppermute(shard, axis, [(i, (i + by) % peers) for i in range(peers)])


def rms(values):
    return values * lax.rsqrt(jnp.mean(values * values, axis=-1, keepdims=True) + 1e-06)


def slots_of(group_ids, experts):
    flat = group_ids.reshape(-1)
    onehot = (flat[:, None] == jnp.arange(experts, dtype=jnp.int32)[None, :]).astype(jnp.int32)
    before = jnp.cumsum(onehot, axis=0) - onehot
    return jnp.sum(before * onehot, axis=1)


def expert_apply(rows, first, second):
    width = rows.shape[-1]
    flat = rows.reshape(-1, width)
    hidden = jax.nn.gelu(
        jnp.dot(flat, first, preferred_element_type=jnp.float32), approximate=True
    ).astype(jnp.bfloat16)
    result = jnp.dot(hidden, second, preferred_element_type=jnp.float32).astype(jnp.bfloat16)
    return result.reshape(rows.shape)


def local(acts, expert_ids, router, skip_gain, skip_rows, w_in, w_out):
    section_pos = lax.axis_index("section")
    section_count = lax.axis_size("section")
    tokens = acts[0]
    group_ids = expert_ids[0]
    tok_count = tokens.shape[0]
    width = tokens.shape[1]
    topk = group_ids.shape[1]
    experts = router.shape[2]
    capacity = 3 * tok_count * topk // (2 * experts)
    decoder = section_pos >= section_count // 2
    skip_term = skip_gain[0][None, :] * rms(skip_rows[0].astype(jnp.float32))
    h_rows = tokens.astype(jnp.float32) + jnp.where(decoder, skip_term, jnp.zeros_like(skip_term))
    normed = rms(h_rows).astype(jnp.bfloat16)
    logits = jnp.dot(normed, router[0], preferred_element_type=jnp.float32)
    chosen = jnp.take_along_axis(logits, group_ids, axis=1)
    gates = jax.nn.softmax(chosen, axis=-1)
    slot = slots_of(group_ids, experts)
    target = group_ids.reshape(-1) * capacity + slot
    repeated = jnp.repeat(normed, topk, axis=0)
    buffer = jnp.zeros((experts * capacity, width), jnp.bfloat16).at[target].set(repeated)
    send_rows = buffer.reshape(experts, capacity, width)
    first = w_in[0, 0]
    second = w_out[0, 0]
    arrived = lax.all_to_all(send_rows, "expert", split_axis=0, concat_axis=0, tiled=True)
    worked = expert_apply(arrived, first, second)
    back_rows = lax.all_to_all(worked, "expert", split_axis=0, concat_axis=0, tiled=True)
    fetched = back_rows.reshape(experts * capacity, width)[target].reshape(tok_count, topk, width)
    combined = jnp.sum(gates[:, :, None] * fetched.astype(jnp.float32), axis=1)
    output_rows = (h_rows + combined).astype(jnp.bfloat16)
    handed = shifted(output_rows, "section", 1)
    pieces = output_rows.reshape(section_count, tok_count // section_count, width)
    spread = lax.all_to_all(pieces, "section", split_axis=0, concat_axis=0, tiled=True)
    collected = lax.all_to_all(spread[::-1], "section", split_axis=0, concat_axis=0, tiled=True)
    mirror_rows = collected.reshape(tok_count, width)
    return (handed[None], mirror_rows[None])


def solution(mesh):
    placed = (
        P("section", "expert", None),
        P("section", "expert", None),
        P("section", None, None),
        P("section", None),
        P("section", "expert", None),
        P("section", "expert", None, None),
        P("section", "expert", None, None),
    )
    return jax.shard_map(
        local,
        mesh=mesh,
        in_specs=placed,
        out_specs=(P("section", "expert", None), P("section", "expert", None)),
        check_vma=False,
    )
```

profile of v0, /device:TPU:0, one launch (start us, length us, event | category | flops | bytes accessed | tf_op | source)
XLA Modules:
  0.0 213.7 jit_solution(8084735192607474264)
XLA Ops:
  0.6 0.0 copy-start
  0.6 0.0 copy-start.1
  0.7 0.0 copy-start.6
  0.7 0.0 copy-start.3
  0.7 1.0 copy.10
  1.6 0.1 eq.29
  1.8 0.1 eq.25
  1.9 0.7 broadcast_multiply_fusion
  2.6 1.5 fusion.15
  4.1 0.0 copy-done.1
  4.2 1.9 multiply_reduce_fusion.1
  6.1 0.0 copy-done.6
  6.1 0.0 copy-done.3
  6.1 0.6 multiply_convert_fusion
  6.7 1.3 broadcast_in_dim.32
  8.0 2.2 %reshape.243 = bf16[512,2048]{1,0:T(8,128)(2,1)} reshape(bf16[256,2,2048]{2,1,0:T(2,128)(2,1)S(1)} %broadcast_in_dim.32) | data formatting | bytes 4194304 | tf_op jit(solution)/shard_map/reshape | solution.py:52
  10.2 1.1 reduce-window.6
  11.4 0.2 slice_reduce_fusion
  11.6 0.1 copy.12
  11.8 0.1 mul.121
  11.9 0.1 fusion.30
  12.0 5.7 %scatter_custom_fusion = bf16[768,2048]{1,0:T(8,128)(2,1)S(1)} fusion(s32[512]{0:T(512)S(1)} %bitcast.92, bf16[512,2048]{1,0:T(8,128)(2,1)} %reshape.243, bf16[]{:T(256)} %constant.16.clone.1), kind=kCustom, calls=%fused_computation.29 | custom fusion | bytes 3146240 | tf_op jit(solution)/shard_map/scatter | solution.py:53
  17.7 0.0 copy-start.8
  17.7 43.1 %all_to_all.20 = bf16[8,96,2048]{2,1,0:T(8,128)(2,1)S(1)} all-to-all(bf16[8,96,2048]{2,1,0:T(8,128)(2,1)S(1)} %bitcast.83), channel_id=1, replica_groups=mesh['section'=4,'expert'=8] {'expert'}, dimensions={0} | all-to-all | bytes 6291456 | tf_op jit(solution)/shard_map/all_to_all | solution.py:57
  60.8 0.0 copy-done.8
  60.8 0.0 copy-start.9
  60.8 4.0 %fusion.14 = bf16[768,1024]{1,0:T(8,128)(2,1)S(1)} fusion(bf16[768,2048]{1,0:T(8,128)(2,1)S(1)} %bitcast.85, bf16[1,1,2048,1024]{3,2,1,0:T(8,128)(2,1)S(1)} %copy-done.8), kind=kOutput, calls=%fused_computation.17 | convolution fusion | flops 3228303360 | bytes 8912896 | tf_op jit(solution)/shard_map/dot_general | solution.py:27
  64.7 0.0 copy-done.9
  64.7 4.8 %fusion.4 = bf16[768,2048]{1,0:T(8,128)(2,1)} fusion(bf16[768,1024]{1,0:T(8,128)(2,1)S(1)} %fusion.14, bf16[1,1,1024,2048]{3,2,1,0:T(8,128)(2,1)S(1)} %copy-done.9), kind=kOutput, calls=%fused_computation.9 | convolution fusion | flops 3222798336 | bytes 8912896 | tf_op jit(solution)/shard_map/dot_general | solution.py:29
  69.6 0.0 copy-start.7
  69.6 3.8 %all-to-all-start.1 = ((bf16[8,96,2048]{2,1,0:T(8,128)(2,1)}), bf16[8,96,2048]{2,1,0:T(8,128)(2,1)S(1)}, u32[]{:S(2)}, u32[]{:S(2)}) async-start(bf16[8,96,2048]{2,1,0:T(8,128)(2,1)} %bitcast.84), calls=%async_computation.1 | async-start | bytes 6291456 | tf_op jit(solution)/shard_map/all_to_all | solution.py:59
  73.4 0.1 rsqrt.22
  73.4 0.0 copy-done.7
  73.5 0.1 copy.11
  73.6 0.1 reshape.233
  73.7 0.0 copy-done
  73.7 2.2 %fusion.24 = f32[256,8]{0,1:T(8,128)S(1)} fusion(bf16[1,256,2048]{2,1,0:T(8,128)(2,1)} %param.11, bf16[1,256,2048]{2,1,0:T(8,128)(2,1)} %param.7, f32[256]{0:T(256)S(1)} %add_rsqrt_fusion, f32[256]{0:T(256)S(1)} %add_rsqrt_fusion.1, f32[2048]{0:T(1024)S(1)} %bitcast.89, pred[]{:T(512)S(6)} %ge.16, bf16[1,2048,8]{1,2,0:T(8,128)(2,1)S(1)} %copy-done), kind=kOutput, calls=%fused_computation.32 | convolution fusion | flops 12582912 | bytes 2148353 | tf_op jit(solution)/shard_map/dot_general | solution.py:47
  76.0 3.5 %gather_fusion.1 = f32[512]{0:T(512)S(1)} fusion(f32[256,8]{0,1:T(8,128)S(1)} %fusion.24, s32[512]{0:T(512)S(1)} %reshape.233), kind=kCustom, calls=%fused_computation.1 | custom fusion | bytes 8192 | tf_op jit(solution)/shard_map/jit(take_along_axis)/gather | solution.py:48
  79.5 0.1 reshape.236
  79.6 0.1 fusion.36
  79.8 0.2 fusion.27
  79.9 0.8 fusion.26
  80.8 30.4 %all-to-all-done.1 = bf16[8,96,2048]{2,1,0:T(8,128)(2,1)S(1)} async-done(((bf16[8,96,2048]{2,1,0:T(8,128)(2,1)}), bf16[8,96,2048]{2,1,0:T(8,128)(2,1)S(1)}, u32[]{:S(2)}, u32[]{:S(2)}) %all-to-all-start.1) | async-done | bytes 3145760 | tf_op jit(solution)/shard_map/all_to_all | solution.py:59
  111.2 3.3 %gather_fusion = bf16[512,2048]{1,0:T(8,128)(2,1)} fusion(bf16[768,2048]{1,0:T(8,128)(2,1)S(1)} %bitcast.79, s32[1024]{0:T(1024)S(1)} %pad_clamp_fusion), kind=kCustom, calls=%fused_computation | custom fusion | bytes 4196352 | tf_op jit(solution)/shard_map/gather | solution.py:60
  114.5 0.0 copy-start.5
  114.5 5.5 %reshape.222 = f32[256,2,2048]{2,1,0:T(2,128)} reshape(bf16[512,2048]{1,0:T(8,128)(2,1)} %gather_fusion) | data formatting | bytes 6291456 | tf_op jit(solution)/shard_map/convert_element_type | solution.py:61
  120.0 0.0 copy-done.5
  120.0 0.0 copy-start.2
  120.0 0.0 copy-start.4
  120.0 8.9 %multiply_reduce_fusion = f32[256,2048]{1,0:T(8,128)S(1)} fusion(f32[256,2,2048]{2,1,0:T(2,128)} %reshape.222, f32[256,2]{1,0:T(8,128)S(1)} %copy-done.5), kind=kLoop, calls=%fused_computation.8 | loop fusion | flops 1572864 | bytes 6293504 | tf_op jit(solution)/shard_map/reduce_sum | solution.py:61
  128.9 0.0 copy-done.2
  128.9 0.0 copy-done.4
  128.9 0.7 add_convert_fusion
  129.6 27.6 %all_to_all.21 = bf16[4,64,2048]{2,1,0:T(8,128)(2,1)} all-to-all(bf16[4,64,2048]{2,1,0:T(8,128)(2,1)S(1)} %add_convert_fusion), channel_id=1, replica_groups=mesh['section'=4,'expert'=8] {'section'}, dimensions={0} | all-to-all | bytes 2097152 | tf_op jit(solution)/shard_map/all_to_all | solution.py:65
  157.2 2.3 %rev.3 = bf16[4,64,2048]{2,1,0:T(8,128)(2,1)} reverse(bf16[4,64,2048]{2,1,0:T(8,128)(2,1)} %all_to_all.21), dimensions={0} | reverse | bytes 2097152 | tf_op jit(solution)/shard_map/rev | solution.py:66
  159.5 4.2 %all-to-all-start.3 = ((bf16[4,64,2048]{2,1,0:T(8,128)(2,1)}), bf16[4,64,2048]{2,1,0:T(8,128)(2,1)}, u32[]{:S(2)}, u32[]{:S(2)}) async-start(bf16[4,64,2048]{2,1,0:T(8,128)(2,1)} %rev.3), calls=%async_computation.3 | async-start | bytes 2097152 | tf_op jit(solution)/shard_map/all_to_all | solution.py:66
  163.8 1.8 add_convert_fusion.1
  165.6 2.0 collective-permute-start
  167.6 38.0 %collective-permute-done = bf16[256,2048]{1,0:T(8,128)(2,1)S(1)} collective-permute-done((bf16[256,2048]{1,0:T(8,128)(2,1)S(1)}, bf16[256,2048]{1,0:T(8,128)(2,1)S(1)}, u32[]{:S(2)}, u32[]{:S(2)}) %collective-permute-start) | collective-permute-done | bytes 1048608 | tf_op jit(solution)/shard_map/ppermute | solution.py:9
  205.6 4.8 %all-to-all-done.3 = bf16[4,64,2048]{2,1,0:T(8,128)(2,1)} async-done(((bf16[4,64,2048]{2,1,0:T(8,128)(2,1)}), bf16[4,64,2048]{2,1,0:T(8,128)(2,1)}, u32[]{:S(2)}, u32[]{:S(2)}) %all-to-all-start.3) | async-done | bytes 1048608 | tf_op jit(solution)/shard_map/all_to_all | solution.py:66
  210.4 1.0 copy.17
  211.4 2.3 %copy.18 = bf16[1,256,2048]{2,1,0:T(8,128)(2,1)} copy(bf16[1,256,2048]{2,1,0:T(8,128)(2,1)} %bitcast.21) | data formatting | bytes 2097152
  (8 shorter events, 0.1 us)
Async XLA Ops:
  0.6 73.1 %copy-start = (bf16[1,2048,8]{1,2,0:T(8,128)(2,1)S(1)}, bf16[1,2048,8]{1,2,0:T(8,128)(2,1)}, u32[]{:S(2)}) copy-start(bf16[1,2048,8]{1,2,0:T(8,128)(2,1)} %param.9) | copy-start | bytes 98308
  0.6 3.5 %copy-start.1 = (bf16[1,256,2048]{2,1,0:T(8,128)(2,1)S(1)}, bf16[1,256,2048]{2,1,0:T(8,128)(2,1)}, u32[]{:S(2)}) copy-start(bf16[1,256,2048]{2,1,0:T(8,128)(2,1)} %param.11) | copy-start | bytes 3145732
  0.7 5.4 %copy-start.6 = (f32[1,2048]{1,0:T(1,128)S(1)}, f32[1,2048]{1,0:T(1,128)}, u32[]{:S(2)}) copy-start(f32[1,2048]{1,0:T(1,128)} %param.10) | copy-start | bytes 24580
  0.7 5.4 %copy-start.3 = (bf16[1,256,2048]{2,1,0:T(8,128)(2,1)S(1)}, bf16[1,256,2048]{2,1,0:T(8,128)(2,1)}, u32[]{:S(2)}) copy-start(bf16[1,256,2048]{2,1,0:T(8,128)(2,1)} %param.7) | copy-start | bytes 3145732
  17.7 43.1 %copy-start.8 = (bf16[1,1,2048,1024]{3,2,1,0:T(8,128)(2,1)S(1)}, bf16[1,1,2048,1024]{3,2,1,0:T(8,128)(2,1)}, u32[]{:S(2)}) copy-start(bf16[1,1,2048,1024]{3,2,1,0:T(8,128)(2,1)} %param.12) | copy-start | bytes 12582916
  60.8 4.0 %copy-start.9 = (bf16[1,1,1024,2048]{3,2,1,0:T(8,128)(2,1)S(1)}, bf16[1,1,1024,2048]{3,2,1,0:T(8,128)(2,1)}, u32[]{:S(2)}) copy-start(bf16[1,1,1024,2048]{3,2,1,0:T(8,128)(2,1)} %param.13) | copy-start | bytes 12582916
  69.6 3.9 %copy-start.7 = (s32[1,256,2]{1,2,0:T(2,128)S(1)}, s32[1,256,2]{1,2,0:T(2,128)}, u32[]{:S(2)}) copy-start(s32[1,256,2]{1,2,0:T(2,128)} %param.8) | copy-start | bytes 6148
  69.6 41.6 %all-to-all-start.1 = ((bf16[8,96,2048]{2,1,0:T(8,128)(2,1)}), bf16[8,96,2048]{2,1,0:T(8,128)(2,1)S(1)}, u32[]{:S(2)}, u32[]{:S(2)}) async-start(bf16[8,96,2048]{2,1,0:T(8,128)(2,1)} %bitcast.84), calls=%async_computation.1 | async-start | bytes 6291456 | tf_op jit(solution)/shard_map/all_to_all | solution.py:59
  114.5 5.5 %copy-start.5 = (f32[256,2]{1,0:T(8,128)S(1)}, f32[256,2]{1,0:T(8,128)}, u32[]{:S(2)}) copy-start(f32[256,2]{1,0:T(8,128)} %fusion.26) | copy-start | bytes 6148
  120.0 8.9 %copy-start.2 = (bf16[1,256,2048]{2,1,0:T(8,128)(2,1)S(1)}, bf16[1,256,2048]{2,1,0:T(8,128)(2,1)}, u32[]{:S(2)}) copy-start(bf16[1,256,2048]{2,1,0:T(8,128)(2,1)} %param.11) | copy-start | bytes 3145732
  120.0 8.9 %copy-start.4 = (bf16[1,256,2048]{2,1,0:T(8,128)(2,1)S(1)}, bf16[1,256,2048]{2,1,0:T(8,128)(2,1)}, u32[]{:S(2)}) copy-start(bf16[1,256,2048]{2,1,0:T(8,128)(2,1)} %param.7) | copy-start | bytes 3145732
  159.5 50.9 %all-to-all-start.3 = ((bf16[4,64,2048]{2,1,0:T(8,128)(2,1)}), bf16[4,64,2048]{2,1,0:T(8,128)(2,1)}, u32[]{:S(2)}, u32[]{:S(2)}) async-start(bf16[4,64,2048]{2,1,0:T(8,128)(2,1)} %rev.3), calls=%async_computation.3 | async-start | bytes 2097152 | tf_op jit(solution)/shard_map/all_to_all | solution.py:66
  165.6 40.0 %collective-permute-start = (bf16[256,2048]{1,0:T(8,128)(2,1)S(1)}, bf16[256,2048]{1,0:T(8,128)(2,1)S(1)}, u32[]{:S(2)}, u32[]{:S(2)}) collective-permute-start(bf16[256,2048]{1,0:T(8,128)(2,1)S(1)} %add_convert_fusion.1), channel_id=1, source_target_pairs={{0,8},{8,16},{16,24},{24,0},{1,9},{9,17},{17,25},{25,1},{2,10},{10... | collective-permute-start | bytes 3145736 | tf_op jit(solution)/shard_map/ppermute | solution.py:9
where the time goes:
time: 216 us; the launch traced here: 214 us
  waiting for transfers between devices  73.2 us (34%)
  blocking collectives  70.7 us (33%)
  local copies, waits for them, and re-layouts  29.3 us (14%)
  other arithmetic  18.5 us (9%)
  matrix products  11 us (5%)
  starting transfers between devices  10 us (5%)
    all_to_all x1, blocking collectives, local(): lax.all_to_all(send_rows, 'expert', split_axis=0, concat_axis=0, tiled=True)  43.1 us
    ppermute x1, waiting for transfers between devices, shifted(): lax.ppermute(shard, axis, [(i, (i + by) % peers) for i in range(peers)])  38 us
    all_to_all x1, waiting for transfers between devices, local(): lax.all_to_all(worked, 'expert', split_axis=0, concat_axis=0, tiled=True)  30.4 us
    all_to_all x1, blocking collectives, local(): lax.all_to_all(pieces, 'section', split_axis=0, concat_axis=0, tiled=True)  27.6 us
    reduce_sum x1, other arithmetic, local(): combined = jnp.sum(gates[:, :, None] * fetched.astype(jnp.float32), axis=1)  8.91 us
    scatter x1, local copies, waits for them, and re-layouts, local(): jnp.zeros((experts * capacity, width), jnp.bfloat16).at[target]  5.65 us
    convert_element_type x1, local copies, waits for them, and re-layouts, local(): combined = jnp.sum(gates[:, :, None] * fetched.astype(jnp.float32), axis=1)  5.47 us
    dot_general x1, matrix products, expert_apply(): jnp.dot(hidden, second, preferred_element_type=jnp.float32)  4.83 us
  transfers between devices with their start and end apart: 3, of which 3 were waited for; matrix products, arithmetic and copies ran while one was open for 4% of the time, Pallas kernels for 0%

commit v1 on v0

v1 whole, which is shorter than its diff:
```python
import jax
import jax.numpy as jnp
from jax import lax
from jax.experimental import pallas as pl
from jax.experimental.pallas import tpu as pltpu
from jax.sharding import PartitionSpec as P

OUT_CHUNKS = 4
IN_CHUNKS = 1


def inverse_rms(values):
    return lax.rsqrt(jnp.mean(values * values, axis=-1, keepdims=True) + 1e-06)


def slot_table(ids, experts, capacity):
    tokens = ids.shape[0]
    rows = experts * capacity
    named = jnp.zeros((tokens, experts), jnp.float32)
    lane = lax.broadcasted_iota(jnp.int32, (tokens, experts), 1)
    for k in range(ids.shape[1]):
        named = named + jnp.where(ids[:, k : k + 1] == lane, 1.0, 0.0)
    before = lax.broadcasted_iota(jnp.int32, (tokens, tokens), 0)
    after = lax.broadcasted_iota(jnp.int32, (tokens, tokens), 1)
    weight = jnp.where(before < after, 1.0, jnp.where(before == after, 512.0, 0.0))
    tally = lax.dot_general(
        named.astype(jnp.bfloat16),
        weight.astype(jnp.bfloat16),
        (((0,), (0,)), ((), ())),
        preferred_element_type=jnp.float32,
    )
    slot = jnp.where(tally >= 512.0, tally - 512.0, -1.0)
    row = lax.broadcasted_iota(jnp.int32, (rows, experts), 0)
    column = lax.broadcasted_iota(jnp.int32, (rows, experts), 1)
    low = column * capacity
    spread = jnp.where((row >= low) & (row < low + capacity), 1.0, 0.0)
    wanted = jnp.dot(
        spread.astype(jnp.bfloat16), slot.astype(jnp.bfloat16), preferred_element_type=jnp.float32
    )
    first = jnp.sum(spread * low.astype(jnp.float32), axis=1, keepdims=True)
    place = lax.broadcasted_iota(jnp.int32, (rows, 1), 0).astype(jnp.float32) - first
    return wanted == place, spread, named


def dispatch_kernel(experts, capacity, late_ref, acts_ref, ids_ref, gain_ref, skip_ref, buffer_ref, h_ref, normed_ref):
    skip = skip_ref[...].astype(jnp.float32)
    term = gain_ref[...] * (skip * inverse_rms(skip))
    h = acts_ref[...].astype(jnp.float32) + jnp.where(late_ref[0] > 0, term, jnp.zeros_like(term))
    h_ref[...] = h
    normed = (h * inverse_rms(h)).astype(jnp.bfloat16)
    normed_ref[...] = normed
    taken, _, _ = slot_table(ids_ref[...], experts, capacity)
    pick = jnp.where(taken, 1.0, 0.0).astype(jnp.bfloat16)
    buffer_ref[...] = jnp.dot(pick, normed, preferred_element_type=jnp.float32).astype(jnp.bfloat16)


def gate_kernel(experts, capacity, normed_ref, ids_ref, router_ref, mix_ref):
    logits = jnp.dot(normed_ref[...], router_ref[...], preferred_element_type=jnp.float32)
    taken, spread, named = slot_table(ids_ref[...], experts, capacity)
    chosen = named > 0.0
    peak = jnp.max(jnp.where(chosen, logits, -jnp.inf), axis=1, keepdims=True)
    mass = jnp.where(chosen, jnp.exp(logits - peak), 0.0)
    gates = mass / jnp.sum(mass, axis=1, keepdims=True)
    wide = lax.dot_general(
        spread.astype(jnp.bfloat16),
        gates.astype(jnp.bfloat16),
        (((1,), (1,)), ((), ())),
        preferred_element_type=jnp.float32,
    )
    mix_ref[...] = jnp.where(taken, wide, 0.0).T.astype(jnp.bfloat16)


def local(acts, expert_ids, router, skip_gain, skip_rows, w_in, w_out):
    section_pos = lax.axis_index("section")
    sections = lax.axis_size("section")
    tokens, width = acts.shape[1:]
    topk = expert_ids.shape[2]
    experts = router.shape[2]
    capacity = 3 * tokens * topk // (2 * experts)
    rows = experts * capacity
    late = (section_pos >= sections // 2).astype(jnp.int32).reshape(1)
    ids = expert_ids[0]
    whole = pl.BlockSpec(memory_space=pltpu.VMEM)
    buffer, h_rows, normed = pl.pallas_call(
        lambda *refs: dispatch_kernel(experts, capacity, *refs),
        out_shape=(
            jax.ShapeDtypeStruct((rows, width), jnp.bfloat16),
            jax.ShapeDtypeStruct((tokens, width), jnp.float32),
            jax.ShapeDtypeStruct((tokens, width), jnp.bfloat16),
        ),
        in_specs=[pl.BlockSpec(memory_space=pltpu.SMEM)] + [whole] * 4,
        out_specs=(whole,) * 3,
        compiler_params=pltpu.CompilerParams(vmem_limit_bytes=48 * 2**20),
        name="dispatch",
    )(late, acts[0], ids, skip_gain, skip_rows[0])

    def exchange(block):
        return lax.all_to_all(block, "expert", split_axis=0, concat_axis=0, tiled=True)

    send = buffer.reshape(experts, capacity, width)
    step = width // IN_CHUNKS
    summed = None
    for c in range(IN_CHUNKS):
        part = exchange(send[:, :, c * step : (c + 1) * step]).reshape(rows, step)
        term = jnp.dot(part, w_in[0, 0, c * step : (c + 1) * step], preferred_element_type=jnp.float32)
        summed = term if summed is None else summed + term
    hidden = jax.nn.gelu(summed, approximate=True).astype(jnp.bfloat16)

    mix = pl.pallas_call(
        lambda *refs: gate_kernel(experts, capacity, *refs),
        out_shape=jax.ShapeDtypeStruct((tokens, rows), jnp.bfloat16),
        in_specs=[whole] * 3,
        out_specs=whole,
        compiler_params=pltpu.CompilerParams(vmem_limit_bytes=48 * 2**20),
        name="gates",
    )(normed, ids, router[0])

    mirror = [(s, sections - 1 - s) for s in range(sections)]
    same = [s for s in range(sections) if (s - 1) % sections == sections - 1 - s]
    onward = [((s - 1) % sections, s) for s in range(sections) if s not in same]
    shared = jnp.zeros((), jnp.bool_)
    for s in same:
        shared = shared | (section_pos == s)
    step = width // OUT_CHUNKS
    mirrored, handed = [], []
    for c in range(OUT_CHUNKS):
        columns = slice(c * step, (c + 1) * step)
        worked = jnp.dot(hidden, w_out[0, 0][:, columns], preferred_element_type=jnp.float32).astype(jnp.bfloat16)
        back = exchange(worked.reshape(experts, capacity, step)).reshape(rows, step)
        y = (h_rows[:, columns] + jnp.dot(mix, back, preferred_element_type=jnp.float32)).astype(jnp.bfloat16)
        across = lax.ppermute(y, "section", mirror)
        mirrored.append(across)
        if onward:
            handed.append(jnp.where(shared, across, lax.ppermute(y, "section", onward)))
        else:
            handed.append(across)
    return (jnp.concatenate(handed, axis=1)[None], jnp.concatenate(mirrored, axis=1)[None])


def solution(mesh):
    placed = (
        P("section", "expert", None),
        P("section", "expert", None),
        P("section", None, None),
        P("section", None),
        P("section", "expert", None),
        P("section", "expert", None, None),
        P("section", "expert", None, None),
    )
    return jax.shard_map(
        local,
        mesh=mesh,
        in_specs=placed,
        out_specs=(P("section", "expert", None), P("section", "expert", None)),
        check_vma=False,
    )
```

time: 216 us -> 168 us (0.78)
  starting transfers between devices: 10 us -> 44.5 us
  waiting for transfers between devices: 73.2 us -> 40.1 us
  blocking collectives: 70.7 us -> 43.3 us
  local copies, waits for them, and re-layouts: 29.3 us -> 5.88 us
  other arithmetic: 18.5 us -> 2.36 us
  matrix products: 11 us -> 24.2 us
  Pallas kernels: 0 us -> 4.68 us
    all_to_all x2 -> x1, blocking collectives: 70.7 us -> 43.3 us  [exchange(): lax.all_to_all(block, 'expert', split_axis=0, concat_axis=0, tiled=True)]
    ppermute x1 -> x8, starting transfers between devices: 2.02 us -> 28.3 us  [the longest x4 25.9 us: local(): handed.append(jnp.where(shared, across, lax.ppermute(y, 'section', onward)))]
    ppermute x1 -> x8, waiting for transfers between devices: 38 us -> 15.6 us  [the longest x4 10 us: local(): across = lax.ppermute(y, 'section', mirror)]
    dot_general x3 -> x9, matrix products: 11 us -> 24.2 us  [the longest x4 14 us: local(): jnp.dot(hidden, w_out[0, 0][:, columns], preferred_element_type=jnp.float32)]
    reduce_sum x5 -> x0, other arithmetic: 12.6 us -> none  [the longest x1 8.91 us: local(): combined = jnp.sum(gates[:, :, None] * fetched.astype(jnp.float32), axis=1)]
    all_to_all x2 -> x4, waiting for transfers between devices: 35.2 us -> 24.5 us  [exchange(): lax.all_to_all(block, 'expert', split_axis=0, concat_axis=0, tiled=True)]
    all_to_all x2 -> x4, starting transfers between devices: 8.02 us -> 16.2 us  [exchange(): lax.all_to_all(block, 'expert', split_axis=0, concat_axis=0, tiled=True)]
    gather x5 -> x0, local copies, waits for them, and re-layouts: 7.23 us -> none  [the longest x4 3.9 us: local(): chosen = jnp.take_along_axis(logits, group_ids, axis=1)]
  transfers between devices with their start and end apart: 3 -> 12, of which waited for: 3 -> 6; matrix products, arithmetic and copies ran while one was open for 4% -> 10% of each run, Pallas kernels for 0% -> 1%
where the time goes in v1:
time: 168 us; the launch traced here: 166 us
  starting transfers between devices  44.5 us (26%)
  blocking collectives  43.3 us (26%)
  waiting for transfers between devices  40.1 us (24%)
  matrix products  24.2 us (14%)
  local copies, waits for them, and re-layouts  5.88 us (4%)
  Pallas kernels  4.68 us (3%)
  other arithmetic  2.36 us (1%)
    all_to_all x1, blocking collectives, exchange(): lax.all_to_all(block, 'expert', split_axis=0, concat_axis=0, tiled=True)  43.3 us
    ppermute x4, starting transfers between devices, local(): handed.append(jnp.where(shared, across, lax.ppermute(y, 'section', onward)))  25.9 us
    all_to_all x4, waiting for transfers between devices, exchange(): lax.all_to_all(block, 'expert', split_axis=0, concat_axis=0, tiled=True)  24.5 us
    all_to_all x4, starting transfers between devices, exchange(): lax.all_to_all(block, 'expert', split_axis=0, concat_axis=0, tiled=True)  16.2 us
    dot_general x4, matrix products, local(): jnp.dot(hidden, w_out[0, 0][:, columns], preferred_element_type=jnp.float32)  14 us
    ppermute x4, waiting for transfers between devices, local(): across = lax.ppermute(y, 'section', mirror)  10 us
    dot_general x4, matrix products, local(): jnp.dot(mix, back, preferred_element_type=jnp.float32)  6.27 us
    unnamed x24, local copies, waits for them, and re-layouts  5.88 us
  transfers between devices with their start and end apart: 12, of which 6 were waited for; matrix products, arithmetic and copies ran while one was open for 10% of the time, Pallas kernels for 1%

profile of v1, /device:TPU:0, one launch (start us, length us, event | category | flops | bytes accessed | tf_op | source)
XLA Modules:
  0.0 165.8 jit_solution(12035793742790535346)
XLA Ops:
  0.6 0.8 copy.9
  1.5 0.0 copy-start
  1.5 1.2 copy-done
  2.7 0.0 copy-start.1
  2.7 1.2 copy-done.1
  3.9 0.0 copy-start.4
  3.9 0.7 copy-done.4
  4.6 3.7 %dispatch.1 = (bf16[768,2048]{1,0:T(8,128)(2,1)}, f32[256,2048]{1,0:T(8,128)S(1)}, bf16[256,2048]{1,0:T(8,128)(2,1)S(1)}) custom-call(s32[1]{0:T(128)} %bitcast.refs_0_, bf16[256,2048]{1,0:T(8,128)(2,1)S(1)} %bitcast.41, s32[256,2]{1,0:T(8,128)S(1)} %bitcast.39, f32[1,2048]{1,0:T(1,128)S(1)} %copy-done.4, bf16[256,2048]{1,0:T(8,128)(2,1)S(1)} %bitcast.42), custom_call_target="tpu_custom_call" | custom-call | tf_op jit(solution)/shard_map/dispatch/pallas_call | solution.py:84
  8.3 0.0 copy-start.2
  8.3 0.0 copy-start.8
  8.3 43.3 %all_to_all.25 = bf16[8,96,2048]{2,1,0:T(8,128)(2,1)S(1)} all-to-all(bf16[8,96,2048]{2,1,0:T(8,128)(2,1)} %bitcast.43), channel_id=1, replica_groups=mesh['section'=4,'expert'=8] {'expert'}, dimensions={0} | all-to-all | bytes 6291456 | tf_op jit(solution)/shard_map/all_to_all | solution.py:98
  51.6 0.0 copy-done.2
  51.6 0.0 copy-done.8
  51.6 3.9 %fusion.9 = bf16[768,1024]{1,0:T(8,128)(2,1)S(1)} fusion(bf16[768,2048]{1,0:T(8,128)(2,1)S(1)} %bitcast.44, bf16[1,1,2048,1024]{3,2,1,0:T(8,128)(2,1)S(1)} %copy-done.8), kind=kOutput, calls=%fused_computation.10 | convolution fusion | flops 3228303360 | bytes 8912896 | tf_op jit(solution)/shard_map/dot_general | solution.py:105
  55.5 0.0 copy-start.9
  55.5 3.6 %convolution_convert_fusion = bf16[768,512]{1,0:T(8,128)(2,1)} fusion(bf16[768,1024]{1,0:T(8,128)(2,1)S(1)} %fusion.9, bf16[1024,2048]{1,0:T(8,128)(2,1)} %bitcast.50), kind=kOutput, calls=%fused_computation.11 | convolution fusion | flops 805699584 | bytes 3407872 | tf_op jit(solution)/shard_map/dot_general | solution.py:128
  59.2 0.0 copy-done.9
  59.2 3.5 %all-to-all-start.4 = ((bf16[8,96,512]{2,1,0:T(8,128)(2,1)}), bf16[8,96,512]{2,1,0:T(8,128)(2,1)S(1)}, u32[]{:S(2)}, u32[]{:S(2)}) async-start(bf16[8,96,512]{2,1,0:T(8,128)(2,1)} %bitcast.49), calls=%async_computation.4 | async-start | bytes 1572864 | tf_op jit(solution)/shard_map/all_to_all | solution.py:98
  62.7 3.6 %convolution_convert_fusion.1 = bf16[768,512]{1,0:T(8,128)(2,1)} fusion(bf16[768,1024]{1,0:T(8,128)(2,1)} %copy-done.9, bf16[1024,2048]{1,0:T(8,128)(2,1)} %bitcast.51), kind=kOutput, calls=%fused_computation.12 | convolution fusion | flops 805699584 | bytes 3407872 | tf_op jit(solution)/shard_map/dot_general | solution.py:128
  66.3 8.9 %all-to-all-done.4 = bf16[8,96,512]{2,1,0:T(8,128)(2,1)S(1)} async-done(((bf16[8,96,512]{2,1,0:T(8,128)(2,1)}), bf16[8,96,512]{2,1,0:T(8,128)(2,1)S(1)}, u32[]{:S(2)}, u32[]{:S(2)}) %all-to-all-start.4) | async-done | bytes 786464 | tf_op jit(solution)/shard_map/all_to_all | solution.py:98
  75.3 0.0 copy-start.5
  75.3 4.2 %all-to-all-start.3 = ((bf16[8,96,512]{2,1,0:T(8,128)(2,1)}), bf16[8,96,512]{2,1,0:T(8,128)(2,1)}, u32[]{:S(2)}, u32[]{:S(2)}) async-start(bf16[8,96,512]{2,1,0:T(8,128)(2,1)} %bitcast.48), calls=%async_computation.3 | async-start | bytes 1572864 | tf_op jit(solution)/shard_map/all_to_all | solution.py:98
  79.5 0.0 copy-start.7
  79.5 3.6 %convolution_convert_fusion.2 = bf16[768,512]{1,0:T(8,128)(2,1)} fusion(bf16[768,1024]{1,0:T(8,128)(2,1)} %copy-done.9, bf16[1024,2048]{1,0:T(8,128)(2,1)} %bitcast.52), kind=kOutput, calls=%fused_computation.13 | convolution fusion | flops 805699584 | bytes 3407872 | tf_op jit(solution)/shard_map/dot_general | solution.py:128
  83.1 0.0 copy-done.5
  83.1 9.0 %all-to-all-done.3 = bf16[8,96,512]{2,1,0:T(8,128)(2,1)} async-done(((bf16[8,96,512]{2,1,0:T(8,128)(2,1)}), bf16[8,96,512]{2,1,0:T(8,128)(2,1)}, u32[]{:S(2)}, u32[]{:S(2)}) %all-to-all-start.3) | async-done | bytes 786464 | tf_op jit(solution)/shard_map/all_to_all | solution.py:98
  92.1 4.2 %all-to-all-start.2 = ((bf16[8,96,512]{2,1,0:T(8,128)(2,1)}), bf16[8,96,512]{2,1,0:T(8,128)(2,1)}, u32[]{:S(2)}, u32[]{:S(2)}) async-start(bf16[8,96,512]{2,1,0:T(8,128)(2,1)} %bitcast.47), calls=%async_computation.2 | async-start | bytes 1572864 | tf_op jit(solution)/shard_map/all_to_all | solution.py:98
  96.4 0.0 copy-done.7
  96.4 0.3 copy.10
  96.6 0.0 copy-start.3
  96.7 1.2 copy-done.3
  97.9 0.0 copy-start.10
  97.9 1.0 gates.1
  98.9 0.4 copy-done.10
  99.3 0.0 copy-start.6
  99.3 3.2 %convolution_convert_fusion.3 = bf16[768,512]{1,0:T(8,128)(2,1)} fusion(bf16[768,1024]{1,0:T(8,128)(2,1)S(1)} %copy-done.10, bf16[1024,2048]{1,0:T(8,128)(2,1)} %bitcast.53), kind=kOutput, calls=%fused_computation.14 | convolution fusion | flops 805699584 | bytes 3407872 | tf_op jit(solution)/shard_map/dot_general | solution.py:128
  102.4 6.5 %all-to-all-done.2 = bf16[8,96,512]{2,1,0:T(8,128)(2,1)} async-done(((bf16[8,96,512]{2,1,0:T(8,128)(2,1)}), bf16[8,96,512]{2,1,0:T(8,128)(2,1)}, u32[]{:S(2)}, u32[]{:S(2)}) %all-to-all-start.2) | async-done | bytes 786464 | tf_op jit(solution)/shard_map/all_to_all | solution.py:98
  109.0 4.2 %all-to-all-start.1 = ((bf16[8,96,512]{2,1,0:T(8,128)(2,1)}), bf16[8,96,512]{2,1,0:T(8,128)(2,1)}, u32[]{:S(2)}, u32[]{:S(2)}) async-start(bf16[8,96,512]{2,1,0:T(8,128)(2,1)} %bitcast.46), calls=%async_computation.1 | async-start | bytes 1572864 | tf_op jit(solution)/shard_map/all_to_all | solution.py:98
  113.2 0.0 copy-done.6
  113.2 1.1 fusion.15
  114.3 4.2 %collective-permute-start.7 = (bf16[256,512]{1,0:T(8,128)(2,1)}, bf16[256,512]{1,0:T(8,128)(2,1)}, u32[]{:S(2)}, u32[]{:S(2)}) collective-permute-start(bf16[256,512]{1,0:T(8,128)(2,1)} %fusion.15), channel_id=1, source_target_pairs={{0,8},{16,24},{1,9},{17,25},{2,10},{18,26},{3,11},{19,27},{4,12},{... | collective-permute-start | bytes 786440 | tf_op jit(solution)/shard_map/ppermute | solution.py:134
  118.5 0.8 collective-permute-start.6
  119.2 2.2 %fusion.14 = bf16[256,512]{1,0:T(8,128)(2,1)} fusion(bf16[256,768]{1,0:T(8,128)(2,1)S(1)} %gates.1, bf16[768,512]{1,0:T(8,128)(2,1)} %bitcast.14, f32[256,2048]{1,0:T(8,128)S(1)} %get-tuple-element.5), kind=kOutput, calls=%fused_computation.21 | convolution fusion | flops 201588736 | bytes 1966080 | tf_op jit(solution)/shard_map/dot_general | solution.py:130
  121.4 5.0 %collective-permute-start.5 = (bf16[256,512]{1,0:T(8,128)(2,1)}, bf16[256,512]{1,0:T(8,128)(2,1)}, u32[]{:S(2)}, u32[]{:S(2)}) collective-permute-start(bf16[256,512]{1,0:T(8,128)(2,1)} %fusion.14), channel_id=1, source_target_pairs={{0,8},{16,24},{1,9},{17,25},{2,10},{18,26},{3,11},{19,27},{4,12},{... | collective-permute-start | bytes 786440 | tf_op jit(solution)/shard_map/ppermute | solution.py:134
  126.4 0.0 collective-permute-start.4
  126.4 1.5 fusion.13
  127.9 0.0 all-to-all-done.1
  127.9 1.5 fusion.12
  129.4 3.7 %collective-permute-start.1 = (bf16[256,512]{1,0:T(8,128)(2,1)S(1)}, bf16[256,512]{1,0:T(8,128)(2,1)S(1)}, u32[]{:S(2)}, u32[]{:S(2)}) collective-permute-start(bf16[256,512]{1,0:T(8,128)(2,1)S(1)} %fusion.12), channel_id=1, source_target_pairs={{0,8},{16,24},{1,9},{17,25},{2,10},{18,26},{3,11},{19,27},{4,12},{... | collective-permute-start | bytes 786440 | tf_op jit(solution)/shard_map/ppermute | solution.py:134
  133.2 0.0 collective-permute-done.7
  133.2 1.5 collective-permute-start
  134.6 0.0 collective-permute-done.6
  134.6 13.1 %collective-permute-start.3 = (bf16[256,512]{1,0:T(8,128)(2,1)S(1)}, bf16[256,512]{1,0:T(8,128)(2,1)S(1)}, u32[]{:S(2)}, u32[]{:S(2)}) collective-permute-start(bf16[256,512]{1,0:T(8,128)(2,1)S(1)} %fusion.13), channel_id=1, source_target_pairs={{0,8},{16,24},{1,9},{17,25},{2,10},{18,26},{3,11},{19,27},{4,12},{... | collective-permute-start | bytes 786440 | tf_op jit(solution)/shard_map/ppermute | solution.py:134
  147.7 0.0 collective-permute-done.5
  147.8 0.1 collective-permute-start.2
  147.8 0.0 collective-permute-done.4
  147.9 0.0 collective-permute-done.1
  147.9 4.9 %collective-permute-done = bf16[256,512]{1,0:T(8,128)(2,1)S(1)} collective-permute-done((bf16[256,512]{1,0:T(8,128)(2,1)S(1)}, bf16[256,512]{1,0:T(8,128)(2,1)S(1)}, u32[]{:S(2)}, u32[]{:S(2)}) %collective-permute-start) | collective-permute-done | bytes 262176 | tf_op jit(solution)/shard_map/ppermute | solution.py:131
  152.8 5.6 %collective-permute-done.3 = bf16[256,512]{1,0:T(8,128)(2,1)S(1)} collective-permute-done((bf16[256,512]{1,0:T(8,128)(2,1)S(1)}, bf16[256,512]{1,0:T(8,128)(2,1)S(1)}, u32[]{:S(2)}, u32[]{:S(2)}) %collective-permute-start.3) | collective-permute-done | bytes 262176 | tf_op jit(solution)/shard_map/ppermute | solution.py:134
  158.4 5.1 %collective-permute-done.2 = bf16[256,512]{1,0:T(8,128)(2,1)S(1)} collective-permute-done((bf16[256,512]{1,0:T(8,128)(2,1)S(1)}, bf16[256,512]{1,0:T(8,128)(2,1)S(1)}, u32[]{:S(2)}, u32[]{:S(2)}) %collective-permute-start.2) | collective-permute-done | bytes 262176 | tf_op jit(solution)/shard_map/ppermute | solution.py:131
  163.6 1.1 maximum_bitcast_fusion
  164.7 1.1 maximum_bitcast_fusion.1
  (4 shorter events, 0.1 us)
Async XLA Ops:
  1.5 1.2 copy-start
  2.7 1.2 copy-start.1
  3.9 0.7 copy-start.4
  8.3 43.3 %copy-start.2 = (bf16[256,2048]{1,0:T(8,128)(2,1)}, bf16[256,2048]{1,0:T(8,128)(2,1)S(1)}, u32[]{:S(2)}) copy-start(bf16[256,2048]{1,0:T(8,128)(2,1)S(1)} %get-tuple-element.6.refs_0_) | copy-start | bytes 3145732
  8.3 43.3 %copy-start.8 = (bf16[1,1,2048,1024]{3,2,1,0:T(8,128)(2,1)S(1)}, bf16[1,1,2048,1024]{3,2,1,0:T(8,128)(2,1)}, u32[]{:S(2)}) copy-start(bf16[1,1,2048,1024]{3,2,1,0:T(8,128)(2,1)} %param.12) | copy-start | bytes 12582916
  55.5 3.7 %copy-start.9 = (bf16[768,1024]{1,0:T(8,128)(2,1)}, bf16[768,1024]{1,0:T(8,128)(2,1)S(1)}, u32[]{:S(2)}) copy-start(bf16[768,1024]{1,0:T(8,128)(2,1)S(1)} %fusion.9) | copy-start | bytes 4718596
  59.2 16.1 %all-to-all-start.4 = ((bf16[8,96,512]{2,1,0:T(8,128)(2,1)}), bf16[8,96,512]{2,1,0:T(8,128)(2,1)S(1)}, u32[]{:S(2)}, u32[]{:S(2)}) async-start(bf16[8,96,512]{2,1,0:T(8,128)(2,1)} %bitcast.49), calls=%async_computation.4 | async-start | bytes 1572864 | tf_op jit(solution)/shard_map/all_to_all | solution.py:98
  75.3 7.8 %copy-start.5 = (bf16[8,96,512]{2,1,0:T(8,128)(2,1)}, bf16[8,96,512]{2,1,0:T(8,128)(2,1)S(1)}, u32[]{:S(2)}) copy-start(bf16[8,96,512]{2,1,0:T(8,128)(2,1)S(1)} %all-to-all-done.4) | copy-start | bytes 2359300
  75.3 16.8 %all-to-all-start.3 = ((bf16[8,96,512]{2,1,0:T(8,128)(2,1)}), bf16[8,96,512]{2,1,0:T(8,128)(2,1)}, u32[]{:S(2)}, u32[]{:S(2)}) async-start(bf16[8,96,512]{2,1,0:T(8,128)(2,1)} %bitcast.48), calls=%async_computation.3 | async-start | bytes 1572864 | tf_op jit(solution)/shard_map/all_to_all | solution.py:98
  79.5 16.9 %copy-start.7 = (bf16[1,2048,8]{1,2,0:T(8,128)(2,1)S(1)}, bf16[1,2048,8]{1,2,0:T(8,128)(2,1)}, u32[]{:S(2)}) copy-start(bf16[1,2048,8]{1,2,0:T(8,128)(2,1)} %param.9) | copy-start | bytes 98308
  92.1 16.8 %all-to-all-start.2 = ((bf16[8,96,512]{2,1,0:T(8,128)(2,1)}), bf16[8,96,512]{2,1,0:T(8,128)(2,1)}, u32[]{:S(2)}, u32[]{:S(2)}) async-start(bf16[8,96,512]{2,1,0:T(8,128)(2,1)} %bitcast.47), calls=%async_computation.2 | async-start | bytes 1572864 | tf_op jit(solution)/shard_map/all_to_all | solution.py:98
  96.6 1.2 copy-start.3
  97.9 1.4 copy-start.10
  99.3 13.9 %copy-start.6 = (bf16[8,96,512]{2,1,0:T(8,128)(2,1)S(1)}, bf16[8,96,512]{2,1,0:T(8,128)(2,1)}, u32[]{:S(2)}) copy-start(bf16[8,96,512]{2,1,0:T(8,128)(2,1)} %copy-done.5) | copy-start | bytes 2359300
  109.0 19.0 %all-to-all-start.1 = ((bf16[8,96,512]{2,1,0:T(8,128)(2,1)}), bf16[8,96,512]{2,1,0:T(8,128)(2,1)}, u32[]{:S(2)}, u32[]{:S(2)}) async-start(bf16[8,96,512]{2,1,0:T(8,128)(2,1)} %bitcast.46), calls=%async_computation.1 | async-start | bytes 1572864 | tf_op jit(solution)/shard_map/all_to_all | solution.py:98
  114.3 18.9 %collective-permute-start.7 = (bf16[256,512]{1,0:T(8,128)(2,1)}, bf16[256,512]{1,0:T(8,128)(2,1)}, u32[]{:S(2)}, u32[]{:S(2)}) collective-permute-start(bf16[256,512]{1,0:T(8,128)(2,1)} %fusion.15), channel_id=1, source_target_pairs={{0,8},{16,24},{1,9},{17,25},{2,10},{18,26},{3,11},{19,27},{4,12},{... | collective-permute-start | bytes 786440 | tf_op jit(solution)/shard_map/ppermute | solution.py:134
  118.5 16.2 %collective-permute-start.6 = (bf16[256,512]{1,0:T(8,128)(2,1)}, bf16[256,512]{1,0:T(8,128)(2,1)S(1)}, u32[]{:S(2)}, u32[]{:S(2)}) collective-permute-start(bf16[256,512]{1,0:T(8,128)(2,1)} %fusion.15), channel_id=1, source_target_pairs={{0,24},{8,16},{16,8},{24,0},{1,25},{9,17},{17,9},{25,1},{2,26},{10... | collective-permute-start | bytes 786440 | tf_op jit(solution)/shard_map/ppermute | solution.py:131
  121.4 26.3 %collective-permute-start.5 = (bf16[256,512]{1,0:T(8,128)(2,1)}, bf16[256,512]{1,0:T(8,128)(2,1)}, u32[]{:S(2)}, u32[]{:S(2)}) collective-permute-start(bf16[256,512]{1,0:T(8,128)(2,1)} %fusion.14), channel_id=1, source_target_pairs={{0,8},{16,24},{1,9},{17,25},{2,10},{18,26},{3,11},{19,27},{4,12},{... | collective-permute-start | bytes 786440 | tf_op jit(solution)/shard_map/ppermute | solution.py:134
  126.4 21.4 %collective-permute-start.4 = (bf16[256,512]{1,0:T(8,128)(2,1)}, bf16[256,512]{1,0:T(8,128)(2,1)S(1)}, u32[]{:S(2)}, u32[]{:S(2)}) collective-permute-start(bf16[256,512]{1,0:T(8,128)(2,1)} %fusion.14), channel_id=1, source_target_pairs={{0,24},{8,16},{16,8},{24,0},{1,25},{9,17},{17,9},{25,1},{2,26},{10... | collective-permute-start | bytes 786440 | tf_op jit(solution)/shard_map/ppermute | solution.py:131
  129.4 18.5 %collective-permute-start.1 = (bf16[256,512]{1,0:T(8,128)(2,1)S(1)}, bf16[256,512]{1,0:T(8,128)(2,1)S(1)}, u32[]{:S(2)}, u32[]{:S(2)}) collective-permute-start(bf16[256,512]{1,0:T(8,128)(2,1)S(1)} %fusion.12), channel_id=1, source_target_pairs={{0,8},{16,24},{1,9},{17,25},{2,10},{18,26},{3,11},{19,27},{4,12},{... | collective-permute-start | bytes 786440 | tf_op jit(solution)/shard_map/ppermute | solution.py:134
  133.2 19.6 %collective-permute-start = (bf16[256,512]{1,0:T(8,128)(2,1)S(1)}, bf16[256,512]{1,0:T(8,128)(2,1)S(1)}, u32[]{:S(2)}, u32[]{:S(2)}) collective-permute-start(bf16[256,512]{1,0:T(8,128)(2,1)S(1)} %fusion.12), channel_id=1, source_target_pairs={{0,24},{8,16},{16,8},{24,0},{1,25},{9,17},{17,9},{25,1},{2,26},{10... | collective-permute-start | bytes 786440 | tf_op jit(solution)/shard_map/ppermute | solution.py:131
  134.6 23.8 %collective-permute-start.3 = (bf16[256,512]{1,0:T(8,128)(2,1)S(1)}, bf16[256,512]{1,0:T(8,128)(2,1)S(1)}, u32[]{:S(2)}, u32[]{:S(2)}) collective-permute-start(bf16[256,512]{1,0:T(8,128)(2,1)S(1)} %fusion.13), channel_id=1, source_target_pairs={{0,8},{16,24},{1,9},{17,25},{2,10},{18,26},{3,11},{19,27},{4,12},{... | collective-permute-start | bytes 786440 | tf_op jit(solution)/shard_map/ppermute | solution.py:134
  147.8 15.8 %collective-permute-start.2 = (bf16[256,512]{1,0:T(8,128)(2,1)S(1)}, bf16[256,512]{1,0:T(8,128)(2,1)S(1)}, u32[]{:S(2)}, u32[]{:S(2)}) collective-permute-start(bf16[256,512]{1,0:T(8,128)(2,1)S(1)} %fusion.13), channel_id=1, source_target_pairs={{0,24},{8,16},{16,8},{24,0},{1,25},{9,17},{17,9},{25,1},{2,26},{10... | collective-permute-start | bytes 786440 | tf_op jit(solution)/shard_map/ppermute | solution.py:131

commit v2 on v0

v2 whole, which is shorter than its diff:
```python
import jax
import jax.numpy as jnp
from jax import lax
from jax.experimental import pallas as pl
from jax.experimental.pallas import tpu as pltpu
from jax.sharding import PartitionSpec as P

OUT_CHUNKS = 4
IN_CHUNKS = 2
VMEM = pl.BlockSpec(memory_space=pltpu.VMEM)
SMEM = pl.BlockSpec(memory_space=pltpu.SMEM)
HBM = pl.BlockSpec(memory_space=pl.ANY)
BF16 = jnp.bfloat16
F32 = jnp.float32


def inverse_rms(values):
    return lax.rsqrt(jnp.mean(values * values, axis=-1, keepdims=True) + 1e-06)


def matmul(a, b):
    return jnp.dot(a, b, preferred_element_type=F32)


def slot_table(me, ids, experts, slots):
    tokens = ids.shape[1]
    rows = experts * slots
    expert = lax.broadcasted_iota(jnp.int32, (experts, tokens), 0) ^ me
    named = jnp.zeros((experts, tokens), F32)
    for k in range(ids.shape[0]):
        named = named + jnp.where(ids[k : k + 1, :] == expert, 1.0, 0.0)
    before = lax.broadcasted_iota(jnp.int32, (tokens, tokens), 0)
    after = lax.broadcasted_iota(jnp.int32, (tokens, tokens), 1)
    earlier = jnp.where(before < after, 1.0, 0.0)
    tally = matmul(named.astype(BF16), earlier.astype(BF16))
    slot = jnp.where(named > 0.0, tally, -1.0)
    row = lax.broadcasted_iota(jnp.int32, (rows, experts), 0)
    low = lax.broadcasted_iota(jnp.int32, (rows, experts), 1) * slots
    spread = jnp.where((row >= low) & (row < low + slots), 1.0, 0.0)
    wanted = matmul(spread.astype(BF16), slot.astype(BF16))
    first = jnp.sum(spread * low.astype(F32), axis=1, keepdims=True)
    place = lax.broadcasted_iota(jnp.int32, (rows, 1), 0).astype(F32) - first
    return wanted == place, spread.astype(BF16), named, expert


def sum_rows(late, acts, skip, gain):
    skip = skip.astype(F32)
    term = gain * (skip * inverse_rms(skip))
    return acts.astype(F32) + jnp.where(late > 0, term, jnp.zeros_like(term))


def dispatch_kernel(experts, slots, pieces, late_ref, me_ref, ids_ref, gain_ref, acts_hbm, skip_hbm, *rest):
    out_refs, (acts_ref, skip_ref, normed_ref, sems) = rest[:-4], rest[-4:]
    tokens, width = acts_ref.shape
    size = tokens // pieces
    copies = []
    for r in range(pieces):
        part = pl.ds(r * size, size)
        pair = (
            pltpu.make_async_copy(skip_hbm.at[part], skip_ref.at[part], sems.at[0, r]),
            pltpu.make_async_copy(acts_hbm.at[part], acts_ref.at[part], sems.at[1, r]),
        )
        for copy in pair:
            copy.start()
        copies.append(pair)
    taken, _, _, _ = slot_table(me_ref[0], ids_ref[...], experts, slots)
    pick = jnp.where(taken, 1.0, 0.0).astype(BF16)
    for r in range(pieces):
        part = pl.ds(r * size, size)
        for copy in copies[r]:
            copy.wait()
        h = sum_rows(late_ref[0], acts_ref[part], skip_ref[part], gain_ref[...])
        normed_ref[part] = (h * inverse_rms(h)).astype(BF16)
    chips = experts // 2
    step = width // IN_CHUNKS
    for c in range(IN_CHUNKS):
        block = matmul(pick, normed_ref[:, c * step : (c + 1) * step]).astype(BF16)
        for k in range(chips):
            out_refs[c * chips + k][...] = block[k * 2 * slots : (k + 1) * 2 * slots]


def gate_kernel(experts, slots, late_ref, me_ref, ids_ref, gain_ref, acts_ref, skip_ref, router_ref, mix_ref, h_ref):
    h = sum_rows(late_ref[0], acts_ref[...], skip_ref[...], gain_ref[...])
    h_ref[...] = h
    normed = (h * inverse_rms(h)).astype(BF16)
    logits = lax.dot_general(
        router_ref[...], normed, (((1,), (1,)), ((), ())), preferred_element_type=F32
    )
    taken, spread, named, expert = slot_table(me_ref[0], ids_ref[...], experts, slots)
    natural = lax.broadcasted_iota(jnp.int32, (experts, ids_ref.shape[1]), 0)
    chosen = jnp.zeros(natural.shape, F32)
    for k in range(ids_ref.shape[0]):
        chosen = chosen + jnp.where(ids_ref[k : k + 1, :] == natural, 1.0, 0.0)
    peak = jnp.max(jnp.where(chosen > 0.0, logits, -jnp.inf), axis=0, keepdims=True)
    mass = jnp.where(chosen > 0.0, jnp.exp(logits - peak), 0.0)
    gates = (mass / jnp.sum(mass, axis=0, keepdims=True)).astype(BF16)
    order = lax.broadcasted_iota(jnp.int32, (experts, experts), 0) ^ me_ref[0]
    swap = jnp.where(order == lax.broadcasted_iota(jnp.int32, (experts, experts), 1), 1.0, 0.0)
    turned = matmul(swap.astype(BF16), gates).astype(BF16)
    wide = matmul(spread, turned)
    mix_ref[...] = jnp.where(taken, wide, 0.0).T.astype(BF16)


def first_kernel(chips, slots, last, *refs):
    blocks, (own_ref, other_ref) = refs[:chips], refs[chips : chips + 2]
    before_ref = None if len(refs) == chips + 4 else refs[chips + 2]
    out_ref, held = refs[-2:]

    @pl.when(pl.program_id(0) == 0)
    def _():
        for k in range(chips):
            for half in range(2):
                held[half, k * slots : (k + 1) * slots] = blocks[k][half * slots : (half + 1) * slots]

    size = chips * slots
    for half, weight in enumerate((own_ref, other_ref)):
        part = slice(half * size, (half + 1) * size)
        total = matmul(held[half], weight[...])
        if before_ref is not None:
            total = total + before_ref[part]
        out_ref[part] = jax.nn.gelu(total, approximate=True).astype(BF16) if last else total


def second_kernel(chips, slots, hidden_ref, own_ref, other_ref, *out_refs):
    size = chips * slots
    for half, weight in enumerate((own_ref, other_ref)):
        worked = matmul(hidden_ref[half * size : (half + 1) * size], weight[...]).astype(BF16)
        for k in range(chips):
            out_refs[k][half * slots : (half + 1) * slots] = worked[k * slots : (k + 1) * slots]


def combine_kernel(chips, h_ref, mix_ref, *refs):
    blocks, out_ref, held = refs[:chips], refs[-2], refs[-1]
    size = blocks[0].shape[0]
    for k in range(chips):
        held[k * size : (k + 1) * size] = blocks[k][...]
    out_ref[...] = (h_ref[...] + matmul(mix_ref[...], held[...])).astype(BF16)


def local(acts, expert_ids, router, skip_gain, skip_rows, w_in, w_out):
    section_pos = lax.axis_index("section")
    sections = lax.axis_size("section")
    devices = lax.axis_size("expert")
    tokens, width = acts.shape[1:]
    topk = expert_ids.shape[2]
    experts = router.shape[2]
    hidden_width = w_in.shape[3]
    capacity = 3 * tokens * topk // (2 * experts)
    slots = -(-capacity // 16) * 16
    rows = experts * slots
    chips = devices // 2
    params = pltpu.CompilerParams(vmem_limit_bytes=40 * 2**20)
    late = (section_pos >= sections // 2).astype(jnp.int32).reshape(1)
    me = lax.axis_index("expert").astype(jnp.int32).reshape(1)
    ids = expert_ids[0].T
    first, second = w_in[0, 0], w_out[0, 0]

    def across_core(block):
        return lax.ppermute(block, "expert", [(i, i ^ 1) for i in range(devices)])

    def exchange(blocks):
        return [blocks[0]] + [
            lax.ppermute(blocks[k], "expert", [(i, i ^ (2 * k)) for i in range(devices)])
            for k in range(1, chips)
        ]

    step = width // IN_CHUNKS
    pieces = 4
    sent = pl.pallas_call(
        lambda *refs: dispatch_kernel(experts, slots, pieces, *refs),
        out_shape=[jax.ShapeDtypeStruct((2 * slots, step), BF16)] * (chips * IN_CHUNKS),
        in_specs=[SMEM, SMEM, VMEM, VMEM, HBM, HBM],
        out_specs=[VMEM] * (chips * IN_CHUNKS),
        scratch_shapes=[
            pltpu.VMEM((tokens, width), BF16),
            pltpu.VMEM((tokens, width), BF16),
            pltpu.VMEM((tokens, width), BF16),
            pltpu.SemaphoreType.DMA((2, pieces)),
        ],
        compiler_params=params,
        name="dispatch",
    )(late, me, ids, skip_gain, acts[0], skip_rows[0])
    other_first = across_core(first)
    other_second = across_core(second)

    mix, h_rows = pl.pallas_call(
        lambda *refs: gate_kernel(experts, slots, *refs),
        out_shape=(
            jax.ShapeDtypeStruct((tokens, rows), BF16),
            jax.ShapeDtypeStruct((tokens, width), F32),
        ),
        in_specs=[SMEM, SMEM] + [VMEM] * 5,
        out_specs=(VMEM, VMEM),
        compiler_params=params,
        name="gates",
    )(late, me, ids, skip_gain, acts[0], skip_rows[0], router[0].T)

    steps = 4
    wide = hidden_width // steps
    total = None
    for c in range(IN_CHUNKS):
        arrived = exchange(sent[c * chips : (c + 1) * chips])
        last = c == IN_CHUNKS - 1
        weight = pl.BlockSpec((step, wide), lambda j, c=c: (c, j))
        column = pl.BlockSpec((rows, wide), lambda j: (0, j))
        total = pl.pallas_call(
            lambda *refs, last=last: first_kernel(chips, slots, last, *refs),
            grid=(steps,),
            out_shape=jax.ShapeDtypeStruct((rows, hidden_width), BF16 if last else F32),
            in_specs=[pl.BlockSpec((2 * slots, step), lambda j: (0, 0))] * chips
            + [weight, weight]
            + ([] if total is None else [column]),
            out_specs=column,
            scratch_shapes=[pltpu.VMEM((2, chips * slots, step), BF16)],
            compiler_params=params,
            name="first_matmul",
        )(*arrived, first, other_first, *([] if total is None else [total]))
    hidden = total

    mirror = [(s, sections - 1 - s) for s in range(sections)]
    same = [s for s in range(sections) if (s - 1) % sections == sections - 1 - s]
    onward = [((s - 1) % sections, s) for s in range(sections) if s not in same]
    shared = jnp.zeros((), jnp.bool_)
    for s in same:
        shared = shared | (section_pos == s)
    step = width // OUT_CHUNKS
    mirrored, handed = [], []
    for c in range(OUT_CHUNKS):
        weight = pl.BlockSpec((hidden_width, step), lambda j, c=c: (0, c))
        worked = pl.pallas_call(
            lambda *refs: second_kernel(chips, slots, *refs),
            grid=(1,),
            out_shape=[jax.ShapeDtypeStruct((2 * slots, step), BF16)] * chips,
            in_specs=[pl.BlockSpec((rows, hidden_width), lambda j: (0, 0)), weight, weight],
            out_specs=[pl.BlockSpec((2 * slots, step), lambda j: (0, 0))] * chips,
            compiler_params=params,
            name="second_matmul",
        )(hidden, second, other_second)
        back = exchange(worked)
        y = pl.pallas_call(
            lambda *refs: combine_kernel(chips, *refs),
            grid=(1,),
            out_shape=jax.ShapeDtypeStruct((tokens, step), BF16),
            in_specs=[
                pl.BlockSpec((tokens, step), lambda j, c=c: (0, c)),
                pl.BlockSpec((tokens, rows), lambda j: (0, 0)),
            ]
            + [pl.BlockSpec((2 * slots, step), lambda j: (0, 0))] * chips,
            out_specs=pl.BlockSpec((tokens, step), lambda j: (0, 0)),
            scratch_shapes=[pltpu.VMEM((rows, step), BF16)],
            compiler_params=params,
            name="combine",
        )(h_rows, mix, *back)
        across = lax.ppermute(y, "section", mirror)
        mirrored.append(across)
        handed.append(jnp.where(shared, across, lax.ppermute(y, "section", onward)) if onward else across)
    return (jnp.concatenate(handed, axis=1)[None], jnp.concatenate(mirrored, axis=1)[None])


def solution(mesh):
    placed = (
        P("section", "expert", None),
        P("section", "expert", None),
        P("section", None, None),
        P("section", None),
        P("section", "expert", None),
        P("section", "expert", None, None),
        P("section", "expert", None, None),
    )
    return jax.shard_map(
        local,
        mesh=mesh,
        in_specs=placed,
        out_specs=(P("section", "expert", None), P("section", "expert", None)),
        check_vma=False,
    )
```

time: 216 us -> 127 us (0.59)
  blocking collectives: 70.7 us -> 0 us
  waiting for transfers between devices: 73.2 us -> 42.9 us
  starting transfers between devices: 10 us -> 39 us
  Pallas kernels: 0 us -> 26.5 us
  local copies, waits for them, and re-layouts: 29.3 us -> 11.3 us
  other arithmetic: 18.5 us -> 5.27 us
  matrix products: 11 us -> 0 us
    all_to_all x2 -> x0, blocking collectives: 70.7 us -> none  [the longest x1 43.1 us: local(): lax.all_to_all(send_rows, 'expert', split_axis=0, concat_axis=0, tiled=True)]
    ppermute x1 -> x28, starting transfers between devices: 2.02 us -> 39 us  [the longest x18 20.4 us: exchange(): lax.ppermute(blocks[k], 'expert', [(i, i ^ 2 * k) for i in range(devices)])]
    all_to_all x2 -> x0, waiting for transfers between devices: 35.2 us -> none  [the longest x1 30.4 us: local(): lax.all_to_all(worked, 'expert', split_axis=0, concat_axis=0, tiled=True)]
    pallas_call x0 -> x12, Pallas kernels: none -> 26.5 us  [the longest x4 9.78 us: local(): pl.pallas_call(lambda *refs: second_kernel(chips, slots, *refs), grid=(1,...]
    reduce_sum x5 -> x0, other arithmetic: 12.6 us -> none  [the longest x1 8.91 us: local(): combined = jnp.sum(gates[:, :, None] * fetched.astype(jnp.float32), axis=1)]
    dot_general x3 -> x0, matrix products: 11 us -> none  [the longest x1 4.83 us: expert_apply(): jnp.dot(hidden, second, preferred_element_type=jnp.float32)]
    all_to_all x2 -> x0, starting transfers between devices: 8.02 us -> none  [the longest x1 4.24 us: local(): lax.all_to_all(spread[::-1], 'section', split_axis=0, concat_axis=0, tile...]
    gather x5 -> x0, local copies, waits for them, and re-layouts: 7.23 us -> none  [the longest x4 3.9 us: local(): chosen = jnp.take_along_axis(logits, group_ids, axis=1)]
  transfers between devices with their start and end apart: 3 -> 28, of which waited for: 3 -> 11; matrix products, arithmetic and copies ran while one was open for 4% -> 2% of each run, Pallas kernels for 0% -> 19%
where the time goes in v2:
time: 127 us; the launch traced here: 126 us
  waiting for transfers between devices  42.9 us (34%)
  starting transfers between devices  39 us (31%)
  Pallas kernels  26.5 us (21%)
  local copies, waits for them, and re-layouts  11.3 us (9%)
  other arithmetic  5.27 us (4%)
    ppermute x18, waiting for transfers between devices, exchange(): lax.ppermute(blocks[k], 'expert', [(i, i ^ 2 * k) for i in range(devices)])  31.8 us
    ppermute x18, starting transfers between devices, exchange(): lax.ppermute(blocks[k], 'expert', [(i, i ^ 2 * k) for i in range(devices)])  20.4 us
    ppermute x4, starting transfers between devices, local(): lax.ppermute(y, 'section', onward)  12.5 us
    unnamed x44, local copies, waits for them, and re-layouts  11.3 us
    pallas_call x4, Pallas kernels, local(): pl.pallas_call(lambda *refs: second_kernel(chips, slots, *refs), grid=(1,...  9.78 us
    pallas_call x2, Pallas kernels, local(): pl.pallas_call(lambda *refs, last=last: first_kernel(chips, slots, last,...  9.54 us
    ppermute x4, waiting for transfers between devices, local(): lax.ppermute(y, 'section', onward)  7.04 us
    ppermute x4, starting transfers between devices, local(): across = lax.ppermute(y, 'section', mirror)  5.52 us
  transfers between devices with their start and end apart: 28, of which 11 were waited for; matrix products, arithmetic and copies ran while one was open for 2% of the time, Pallas kernels for 19%

profile of v2, /device:TPU:0, one launch (start us, length us, event | category | flops | bytes accessed | tf_op | source)
XLA Modules:
  0.0 125.9 jit_solution(4443748561789616901)
XLA Ops:
  0.6 0.5 collective-permute-start.3
  1.2 1.2 copy-done.3
  2.5 1.2 copy-done.5
  3.7 0.7 copy-done.18
  4.4 0.7 copy-done.20
  5.1 2.9 %dispatch.1 = (bf16[192,1024]{1,0:T(8,128)(2,1)S(1)}, bf16[192,1024]{1,0:T(8,128)(2,1)S(1)}, bf16[192,1024]{1,0:T(8,128)(2,1)S(1)}, bf16[192,1024]{1,0:T(8,128)(...) custom-call(s32[1]{0:T(128)} %bitcast.refs_0_, ...), custom_call_target="tpu_custom_call" | custom-call | tf_op jit(solution)/shard_map/dispatch/pallas_call | solution.py:169
  7.9 3.0 %collective-permute-start.4 = (bf16[192,1024]{1,0:T(8,128)(2,1)S(1)}, bf16[192,1024]{1,0:T(8,128)(2,1)S(1)}, u32[]{:S(2)}, u32[]{:S(2)}) collective-permute-start(bf16[192,1024]{1,0:T(8,128)(2,1)S(1)} %get-tuple-element.35), channel_id=1, source_target_pairs={{0,2},{1,3},{2,0},{3,1},{4,6},{5,7},{6,4},{7,5},{8,10},{9,11},{10,... | collective-permute-start | bytes 1179656 | tf_op jit(solution)/shard_map/ppermute | solution.py:163
  10.9 1.5 %collective-permute-start.5 = (bf16[192,1024]{1,0:T(8,128)(2,1)S(1)}, bf16[192,1024]{1,0:T(8,128)(2,1)S(1)}, u32[]{:S(2)}, u32[]{:S(2)}) collective-permute-start(bf16[192,1024]{1,0:T(8,128)(2,1)S(1)} %get-tuple-element.36), channel_id=1, source_target_pairs={{0,4},{1,5},{2,6},{3,7},{4,0},{5,1},{6,2},{7,3},{8,12},{9,13},{10,... | collective-permute-start | bytes 1179656 | tf_op jit(solution)/shard_map/ppermute | solution.py:163
  12.4 8.4 %collective-permute-done.4.refs_1_ = bf16[192,1024]{1,0:T(8,128)(2,1)S(1)} collective-permute-done((bf16[192,1024]{1,0:T(8,128)(2,1)S(1)}, bf16[192,1024]{1,0:T(8,128)(2,1)S(1)}, u32[]{:S(2)}, u32[]{:S(2)}) %collective-permute-start.4) | collective-permute-done | bytes 393248 | tf_op jit(solution)/shard_map/ppermute | solution.py:163
  20.8 2.1 %collective-permute-start = (bf16[192,1024]{1,0:T(8,128)(2,1)S(1)}, bf16[192,1024]{1,0:T(8,128)(2,1)S(1)}, u32[]{:S(2)}, u32[]{:S(2)}) collective-permute-start(bf16[192,1024]{1,0:T(8,128)(2,1)S(1)} %get-tuple-element.31), channel_id=1, source_target_pairs={{0,2},{1,3},{2,0},{3,1},{4,6},{5,7},{6,4},{7,5},{8,10},{9,11},{10,... | collective-permute-start | bytes 1179656 | tf_op jit(solution)/shard_map/ppermute | solution.py:163
  22.9 6.6 %collective-permute-done.5.refs_2_ = bf16[192,1024]{1,0:T(8,128)(2,1)S(1)} collective-permute-done((bf16[192,1024]{1,0:T(8,128)(2,1)S(1)}, bf16[192,1024]{1,0:T(8,128)(2,1)S(1)}, u32[]{:S(2)}, u32[]{:S(2)}) %collective-permute-start.5) | collective-permute-done | bytes 393248 | tf_op jit(solution)/shard_map/ppermute | solution.py:163
  29.5 2.2 %collective-permute-start.1 = (bf16[192,1024]{1,0:T(8,128)(2,1)S(1)}, bf16[192,1024]{1,0:T(8,128)(2,1)S(1)}, u32[]{:S(2)}, u32[]{:S(2)}) collective-permute-start(bf16[192,1024]{1,0:T(8,128)(2,1)S(1)} %get-tuple-element.32), channel_id=1, source_target_pairs={{0,4},{1,5},{2,6},{3,7},{4,0},{5,1},{6,2},{7,3},{8,12},{9,13},{10,... | collective-permute-start | bytes 1179656 | tf_op jit(solution)/shard_map/ppermute | solution.py:163
  31.7 0.6 collective-permute-start.2
  32.3 2.2 %copy-done.1 = bf16[1,1,2048,1024]{3,2,1,0:T(8,128)(2,1)S(1)} copy-done((bf16[1,1,2048,1024]{3,2,1,0:T(8,128)(2,1)S(1)}, bf16[1,1,2048,1024]{3,2,1,0:T(8,128)(2,1)}, u32[]{:S(2)}) %copy-start.1) | copy-done | bytes 4194328
  34.4 4.5 %first_matmul.2.refs_6_ = f32[768,1024]{1,0:T(8,128)S(1)} custom-call(bf16[192,1024]{1,0:T(8,128)(2,1)S(1)} %get-tuple-element.34.refs_0_, bf16[192,1024]{1,0:T(8,128)(2,1)S(1)} %collective-permute-done.4.refs_1_, bf16[192,1024]{1,0:T(8,128)(2,1)S(1)} %collective-permute-done.5.refs_2_, bf16[192,1024]{1,0:T(8,128)(2,1)S(1)} %collective-permute-done.6.refs_3_, ...), custom_call_target="tpu_custom_call" | custom-call | tf_op jit(solution)/shard_map/first_matmul/pallas_call | solution.py:206
  39.0 9.1 %collective-permute-done.1.refs_2_ = bf16[192,1024]{1,0:T(8,128)(2,1)S(1)} collective-permute-done((bf16[192,1024]{1,0:T(8,128)(2,1)S(1)}, bf16[192,1024]{1,0:T(8,128)(2,1)S(1)}, u32[]{:S(2)}, u32[]{:S(2)}) %collective-permute-start.1) | collective-permute-done | bytes 393248 | tf_op jit(solution)/shard_map/ppermute | solution.py:163
  48.0 5.0 %first_matmul.3.refs_0_ = bf16[768,1024]{1,0:T(8,128)(2,1)S(1)} custom-call(bf16[192,1024]{1,0:T(8,128)(2,1)S(1)} %get-tuple-element.30.refs_0_, bf16[192,1024]{1,0:T(8,128)(2,1)S(1)} %collective-permute-done.refs_1_, bf16[192,1024]{1,0:T(8,128)(2,1)S(1)} %collective-permute-done.1.refs_2_, bf16[192,1024]{1,0:T(8,128)(2,1)S(1)} %collective-permute-done.2.refs_3_, ...), custom_call_target="tpu_custom_call" | custom-call | tf_op jit(solution)/shard_map/first_matmul/pallas_call | solution.py:206
  53.1 2.3 %second_matmul.4 = (bf16[192,512]{1,0:T(8,128)(2,1)S(1)}, bf16[192,512]{1,0:T(8,128)(2,1)S(1)}, bf16[192,512]{1,0:T(8,128)(2,1)S(1)}, bf16[192,512]{1,0:T(8,128)(2,1)S(1)}) custom-call(bf16[768,1024]{1,0:T(8,128)(2,1)S(1)} %first_matmul.3.refs_0_, bf16[1024,2048]{1,0:T(8,128)(2,1)S(1)} %bitcast.17, bf16[1024,2048]{1,0:T(8,128)(2,1)} %collective-permute-done.7.refs_2_), custom_call_target="tpu_custom_call" | custom-call | tf_op jit(solution)/shard_map/second_matmul/pallas_call | solution.py:230
  55.4 0.5 collective-permute-start.10
  55.9 2.7 %collective-permute-start.8 = (bf16[192,512]{1,0:T(8,128)(2,1)S(1)}, bf16[192,512]{1,0:T(8,128)(2,1)S(1)}, u32[]{:S(2)}, u32[]{:S(2)}) collective-permute-start(bf16[192,512]{1,0:T(8,128)(2,1)S(1)} %get-tuple-element.39), channel_id=1, source_target_pairs={{0,2},{1,3},{2,0},{3,1},{4,6},{5,7},{6,4},{7,5},{8,10},{9,11},{10,... | collective-permute-start | bytes 589832 | tf_op jit(solution)/shard_map/ppermute | solution.py:163
  58.6 0.3 collective-permute-start.9
  58.9 2.3 %second_matmul.5 = (bf16[192,512]{1,0:T(8,128)(2,1)S(1)}, bf16[192,512]{1,0:T(8,128)(2,1)S(1)}, bf16[192,512]{1,0:T(8,128)(2,1)S(1)}, bf16[192,512]{1,0:T(8,128)(2,1)S(1)}) custom-call(bf16[768,1024]{1,0:T(8,128)(2,1)S(1)} %first_matmul.3.refs_0_, bf16[1024,2048]{1,0:T(8,128)(2,1)S(1)} %bitcast.18, bf16[1024,2048]{1,0:T(8,128)(2,1)} %collective-permute-done.7.refs_2_), custom_call_target="tpu_custom_call" | custom-call | tf_op jit(solution)/shard_map/second_matmul/pallas_call | solution.py:230
  61.2 0.4 collective-permute-start.13
  61.6 1.5 %collective-permute-start.14 = (bf16[192,512]{1,0:T(8,128)(2,1)S(1)}, bf16[192,512]{1,0:T(8,128)(2,1)S(1)}, u32[]{:S(2)}, u32[]{:S(2)}) collective-permute-start(bf16[192,512]{1,0:T(8,128)(2,1)S(1)} %get-tuple-element.44), channel_id=1, source_target_pairs={{0,4},{1,5},{2,6},{3,7},{4,0},{5,1},{6,2},{7,3},{8,12},{9,13},{10,... | collective-permute-start | bytes 589832 | tf_op jit(solution)/shard_map/ppermute | solution.py:163
  63.1 1.1 collective-permute-done.10.refs_5_
  64.2 0.7 collective-permute-start.15
  64.9 2.3 %second_matmul.6 = (bf16[192,512]{1,0:T(8,128)(2,1)S(1)}, bf16[192,512]{1,0:T(8,128)(2,1)S(1)}, bf16[192,512]{1,0:T(8,128)(2,1)S(1)}, bf16[192,512]{1,0:T(8,128)(2,1)S(1)}) custom-call(bf16[768,1024]{1,0:T(8,128)(2,1)S(1)} %first_matmul.3.refs_0_, bf16[1024,2048]{1,0:T(8,128)(2,1)S(1)} %bitcast.19, bf16[1024,2048]{1,0:T(8,128)(2,1)} %collective-permute-done.7.refs_2_), custom_call_target="tpu_custom_call" | custom-call | tf_op jit(solution)/shard_map/second_matmul/pallas_call | solution.py:230
  67.1 1.5 %collective-permute-done.8.refs_3_ = bf16[192,512]{1,0:T(8,128)(2,1)S(1)} collective-permute-done((bf16[192,512]{1,0:T(8,128)(2,1)S(1)}, bf16[192,512]{1,0:T(8,128)(2,1)S(1)}, u32[]{:S(2)}, u32[]{:S(2)}) %collective-permute-start.8) | collective-permute-done | bytes 196640 | tf_op jit(solution)/shard_map/ppermute | solution.py:163
  68.7 1.2 collective-permute-start.18
  69.8 0.3 collective-permute-start.19
  70.1 2.8 %collective-permute-done.13.refs_3_ = bf16[192,512]{1,0:T(8,128)(2,1)S(1)} collective-permute-done((bf16[192,512]{1,0:T(8,128)(2,1)S(1)}, bf16[192,512]{1,0:T(8,128)(2,1)S(1)}, u32[]{:S(2)}, u32[]{:S(2)}) %collective-permute-start.13) | collective-permute-done | bytes 196640 | tf_op jit(solution)/shard_map/ppermute | solution.py:163
  73.0 1.9 %gates.1 = (bf16[256,768]{1,0:T(8,128)(2,1)S(1)}, f32[256,2048]{1,0:T(8,128)S(1)}) custom-call(s32[1]{0:T(128)} %bitcast.refs_0_, s32[1]{0:T(128)} %bitcast.1.refs_1_, s32[2,256]{1,0:T(2,128)S(1)} %bitcast.30, f32[1,2048]{1,0:T(1,128)S(1)} %copy-done.19, bf16[256,2048]{1,0:T(8,128)(2,1)S(1)} %bitcast.25, bf16[256,2048]{1,0:T(8,128)(2,1)S(1)} %bitcast.27, ...), custom_call_target="tpu_custom_call" | custom-call | tf_op jit(solution)/shard_map/gates/pallas_call | solution.py:186
  74.9 0.4 combine.4
  75.3 3.6 %collective-permute-start.11 = (bf16[256,512]{1,0:T(8,128)(2,1)S(1)}, bf16[256,512]{1,0:T(8,128)(2,1)}, u32[]{:S(2)}, u32[]{:S(2)}) collective-permute-start(bf16[256,512]{1,0:T(8,128)(2,1)S(1)} %combine.4), channel_id=1, source_target_pairs={{0,24},{8,16},{16,8},{24,0},{1,25},{9,17},{17,9},{25,1},{2,26},{10... | collective-permute-start | bytes 786440 | tf_op jit(solution)/shard_map/ppermute | solution.py:254
  78.9 2.2 %collective-permute-start.12 = (bf16[256,512]{1,0:T(8,128)(2,1)S(1)}, bf16[256,512]{1,0:T(8,128)(2,1)}, u32[]{:S(2)}, u32[]{:S(2)}) collective-permute-start(bf16[256,512]{1,0:T(8,128)(2,1)S(1)} %combine.4), channel_id=1, source_target_pairs={{0,8},{16,24},{1,9},{17,25},{2,10},{18,26},{3,11},{19,27},{4,12},{... | collective-permute-start | bytes 786440 | tf_op jit(solution)/shard_map/ppermute | solution.py:256
  81.0 3.0 %second_matmul.7 = (bf16[192,512]{1,0:T(8,128)(2,1)S(1)}, bf16[192,512]{1,0:T(8,128)(2,1)S(1)}, bf16[192,512]{1,0:T(8,128)(2,1)S(1)}, bf16[192,512]{1,0:T(8,128)(2,1)}) custom-call(bf16[768,1024]{1,0:T(8,128)(2,1)S(1)} %first_matmul.3.refs_0_, bf16[1024,2048]{1,0:T(8,128)(2,1)S(1)} %bitcast.20, bf16[1024,2048]{1,0:T(8,128)(2,1)} %collective-permute-done.7.refs_2_), custom_call_target="tpu_custom_call" | custom-call | tf_op jit(solution)/shard_map/second_matmul/pallas_call | solution.py:230
  84.0 0.7 copy-done.11
  84.7 0.8 collective-permute-start.23
  85.4 0.7 copy-done.7
  86.1 1.8 %collective-permute-start.24 = (bf16[192,512]{1,0:T(8,128)(2,1)S(1)}, bf16[192,512]{1,0:T(8,128)(2,1)S(1)}, u32[]{:S(2)}, u32[]{:S(2)}) collective-permute-start(bf16[192,512]{1,0:T(8,128)(2,1)S(1)} %get-tuple-element.52), channel_id=1, source_target_pairs={{0,4},{1,5},{2,6},{3,7},{4,0},{5,1},{6,2},{7,3},{8,12},{9,13},{10,... | collective-permute-start | bytes 589832 | tf_op jit(solution)/shard_map/ppermute | solution.py:163
  87.9 0.9 collective-permute-start.25
  88.9 0.4 combine.5
  89.2 1.1 collective-permute-done.23.refs_3_
  90.4 0.7 copy-done.13
  91.0 0.9 collective-permute-start.16
  92.0 1.3 collective-permute-done.24.refs_4_
  93.2 0.7 copy-done.15
  93.9 3.0 %collective-permute-start.17 = (bf16[256,512]{1,0:T(8,128)(2,1)S(1)}, bf16[256,512]{1,0:T(8,128)(2,1)}, u32[]{:S(2)}, u32[]{:S(2)}) collective-permute-start(bf16[256,512]{1,0:T(8,128)(2,1)S(1)} %combine.5), channel_id=1, source_target_pairs={{0,8},{16,24},{1,9},{17,25},{2,10},{18,26},{3,11},{19,27},{4,12},{... | collective-permute-start | bytes 786440 | tf_op jit(solution)/shard_map/ppermute | solution.py:256
  96.9 0.9 copy-done.8
  97.8 0.9 copy-done.10
  98.8 0.4 combine.6
  99.2 0.5 copy-done.12
  99.7 0.1 copy-done.14
  99.9 1.3 %combine.7 = bf16[256,512]{1,0:T(8,128)(2,1)S(1)} custom-call(f32[256,2048]{1,0:T(8,128)S(1)} %get-tuple-element.28.refs_0_, bf16[256,768]{1,0:T(8,128)(2,1)S(1)} %get-tuple-element.29.refs_1_, bf16[192,512]{1,0:T(8,128)(2,1)S(1)} %copy-done.12, bf16[192,512]{1,0:T(8,128)(2,1)S(1)} %copy-done.14, bf16[192,512]{1,0:T(8,128)(2,1)S(1)} %copy-done.16, ...), custom_call_target="tpu_custom_call" | custom-call | tf_op jit(solution)/shard_map/combine/pallas_call | solution.py:240
  101.2 3.6 %collective-permute-start.22 = (bf16[256,512]{1,0:T(8,128)(2,1)S(1)}, bf16[256,512]{1,0:T(8,128)(2,1)S(1)}, u32[]{:S(2)}, u32[]{:S(2)}) collective-permute-start(bf16[256,512]{1,0:T(8,128)(2,1)S(1)} %combine.6), channel_id=1, source_target_pairs={{0,8},{16,24},{1,9},{17,25},{2,10},{18,26},{3,11},{19,27},{4,12},{... | collective-permute-start | bytes 786440 | tf_op jit(solution)/shard_map/ppermute | solution.py:256
  104.9 0.9 collective-permute-start.26
  105.8 1.0 broadcast_select_fusion.3
  106.8 3.7 %collective-permute-start.27 = (bf16[256,512]{1,0:T(8,128)(2,1)S(1)}, bf16[256,512]{1,0:T(8,128)(2,1)S(1)}, u32[]{:S(2)}, u32[]{:S(2)}) collective-permute-start(bf16[256,512]{1,0:T(8,128)(2,1)S(1)} %combine.7), channel_id=1, source_target_pairs={{0,8},{16,24},{1,9},{17,25},{2,10},{18,26},{3,11},{19,27},{4,12},{... | collective-permute-start | bytes 786440 | tf_op jit(solution)/shard_map/ppermute | solution.py:256
  110.4 1.0 broadcast_select_fusion.2
  111.4 4.2 %collective-permute-done.22 = bf16[256,512]{1,0:T(8,128)(2,1)S(1)} collective-permute-done((bf16[256,512]{1,0:T(8,128)(2,1)S(1)}, bf16[256,512]{1,0:T(8,128)(2,1)S(1)}, u32[]{:S(2)}, u32[]{:S(2)}) %collective-permute-start.22) | collective-permute-done | bytes 262176 | tf_op jit(solution)/shard_map/ppermute | solution.py:256
  115.7 4.1 %collective-permute-done.26 = bf16[256,512]{1,0:T(8,128)(2,1)S(1)} collective-permute-done((bf16[256,512]{1,0:T(8,128)(2,1)S(1)}, bf16[256,512]{1,0:T(8,128)(2,1)S(1)}, u32[]{:S(2)}, u32[]{:S(2)}) %collective-permute-start.26) | collective-permute-done | bytes 262176 | tf_op jit(solution)/shard_map/ppermute | solution.py:254
  119.8 2.8 %collective-permute-done.27 = bf16[256,512]{1,0:T(8,128)(2,1)S(1)} collective-permute-done((bf16[256,512]{1,0:T(8,128)(2,1)S(1)}, bf16[256,512]{1,0:T(8,128)(2,1)S(1)}, u32[]{:S(2)}, u32[]{:S(2)}) %collective-permute-start.27) | collective-permute-done | bytes 262176 | tf_op jit(solution)/shard_map/ppermute | solution.py:256
  122.6 1.1 maximum_bitcast_fusion
  123.7 2.1 %maximum_bitcast_fusion.1 = bf16[1,256,2048]{2,1,0:T(8,128)(2,1)} fusion(bf16[256,512]{1,0:T(8,128)(2,1)S(1)} %collective-permute-done.26, bf16[256,512]{1,0:T(8,128)(2,1)S(1)} %collective-permute-done.21, bf16[256,512]{1,0:T(8,128)(2,1)} %collective-permute-done.16, bf16[256,512]{1,0:T(8,128)(2,1)} %collective-permute-done.11), kind=kLoop, calls=%fused_computation.1 | loop fusion | flops 4194304 | bytes 2097152 | tf_op jit(solution)/shard_map/broadcast_in_dim | solution.py:257
  (54 shorter events, 0.5 us)
Async XLA Ops:
  0.6 31.6 %collective-permute-start.3 = (bf16[2048,1024]{1,0:T(8,128)(2,1)}, bf16[2048,1024]{1,0:T(8,128)(2,1)}, u32[]{:S(2)}, u32[]{:S(2)}) collective-permute-start(bf16[2048,1024]{1,0:T(8,128)(2,1)} %bitcast.21), channel_id=1, source_target_pairs={{0,1},{1,0},{2,3},{3,2},{4,5},{5,4},{6,7},{7,6},{8,9},{9,8},{10,11... | collective-permute-start | bytes 12582920 | tf_op jit(solution)/shard_map/ppermute | solution.py:159
  1.1 51.9 %collective-permute-start.7 = (bf16[1024,2048]{1,0:T(8,128)(2,1)}, bf16[1024,2048]{1,0:T(8,128)(2,1)}, u32[]{:S(2)}, u32[]{:S(2)}) collective-permute-start(bf16[1024,2048]{1,0:T(8,128)(2,1)} %bitcast.16), channel_id=1, source_target_pairs={{0,1},{1,0},{2,3},{3,2},{4,5},{5,4},{6,7},{7,6},{8,9},{9,8},{10,11... | collective-permute-start | bytes 12582920 | tf_op jit(solution)/shard_map/ppermute | solution.py:159
  1.2 1.2 copy-start.3
  2.5 1.2 copy-start.5
  3.7 0.7 copy-start.18
  4.4 0.7 copy-start.20
  7.9 12.9 %collective-permute-start.4 = (bf16[192,1024]{1,0:T(8,128)(2,1)S(1)}, bf16[192,1024]{1,0:T(8,128)(2,1)S(1)}, u32[]{:S(2)}, u32[]{:S(2)}) collective-permute-start(bf16[192,1024]{1,0:T(8,128)(2,1)S(1)} %get-tuple-element.35), channel_id=1, source_target_pairs={{0,2},{1,3},{2,0},{3,1},{4,6},{5,7},{6,4},{7,5},{8,10},{9,11},{10,... | collective-permute-start | bytes 1179656 | tf_op jit(solution)/shard_map/ppermute | solution.py:163
  10.9 18.6 %collective-permute-start.5 = (bf16[192,1024]{1,0:T(8,128)(2,1)S(1)}, bf16[192,1024]{1,0:T(8,128)(2,1)S(1)}, u32[]{:S(2)}, u32[]{:S(2)}) collective-permute-start(bf16[192,1024]{1,0:T(8,128)(2,1)S(1)} %get-tuple-element.36), channel_id=1, source_target_pairs={{0,4},{1,5},{2,6},{3,7},{4,0},{5,1},{6,2},{7,3},{8,12},{9,13},{10,... | collective-permute-start | bytes 1179656 | tf_op jit(solution)/shard_map/ppermute | solution.py:163
  12.4 19.3 %collective-permute-start.6 = (bf16[192,1024]{1,0:T(8,128)(2,1)S(1)}, bf16[192,1024]{1,0:T(8,128)(2,1)S(1)}, u32[]{:S(2)}, u32[]{:S(2)}) collective-permute-start(bf16[192,1024]{1,0:T(8,128)(2,1)S(1)} %get-tuple-element.37), channel_id=1, source_target_pairs={{0,6},{1,7},{2,4},{3,5},{4,2},{5,3},{6,0},{7,1},{8,14},{9,15},{10,... | collective-permute-start | bytes 1179656 | tf_op jit(solution)/shard_map/ppermute | solution.py:163
  20.8 18.1 %collective-permute-start = (bf16[192,1024]{1,0:T(8,128)(2,1)S(1)}, bf16[192,1024]{1,0:T(8,128)(2,1)S(1)}, u32[]{:S(2)}, u32[]{:S(2)}) collective-permute-start(bf16[192,1024]{1,0:T(8,128)(2,1)S(1)} %get-tuple-element.31), channel_id=1, source_target_pairs={{0,2},{1,3},{2,0},{3,1},{4,6},{5,7},{6,4},{7,5},{8,10},{9,11},{10,... | collective-permute-start | bytes 1179656 | tf_op jit(solution)/shard_map/ppermute | solution.py:163
  29.5 18.5 %collective-permute-start.1 = (bf16[192,1024]{1,0:T(8,128)(2,1)S(1)}, bf16[192,1024]{1,0:T(8,128)(2,1)S(1)}, u32[]{:S(2)}, u32[]{:S(2)}) collective-permute-start(bf16[192,1024]{1,0:T(8,128)(2,1)S(1)} %get-tuple-element.32), channel_id=1, source_target_pairs={{0,4},{1,5},{2,6},{3,7},{4,0},{5,1},{6,2},{7,3},{8,12},{9,13},{10,... | collective-permute-start | bytes 1179656 | tf_op jit(solution)/shard_map/ppermute | solution.py:163
  31.7 16.3 %collective-permute-start.2 = (bf16[192,1024]{1,0:T(8,128)(2,1)S(1)}, bf16[192,1024]{1,0:T(8,128)(2,1)S(1)}, u32[]{:S(2)}, u32[]{:S(2)}) collective-permute-start(bf16[192,1024]{1,0:T(8,128)(2,1)S(1)} %get-tuple-element.33), channel_id=1, source_target_pairs={{0,6},{1,7},{2,4},{3,5},{4,2},{5,3},{6,0},{7,1},{8,14},{9,15},{10,... | collective-permute-start | bytes 1179656 | tf_op jit(solution)/shard_map/ppermute | solution.py:163
  32.2 2.2 %copy-start.1 = (bf16[1,1,2048,1024]{3,2,1,0:T(8,128)(2,1)S(1)}, bf16[1,1,2048,1024]{3,2,1,0:T(8,128)(2,1)}, u32[]{:S(2)}) copy-start(bf16[1,1,2048,1024]{3,2,1,0:T(8,128)(2,1)} %param.12) | copy-start | bytes 12582916
  34.4 13.6 %copy-start.2 = (bf16[1,1,2048,1024]{3,2,1,0:T(8,128)(2,1)S(1)}, bf16[1,1,2048,1024]{3,2,1,0:T(8,128)(2,1)}, u32[]{:S(2)}) copy-start(bf16[1,1,2048,1024]{3,2,1,0:T(8,128)(2,1)} %param.12) | copy-start | bytes 12582916
  48.0 5.1 %copy-start = (bf16[1,1,1024,2048]{3,2,1,0:T(8,128)(2,1)S(1)}, bf16[1,1,1024,2048]{3,2,1,0:T(8,128)(2,1)}, u32[]{:S(2)}) copy-start(bf16[1,1,1024,2048]{3,2,1,0:T(8,128)(2,1)} %param.13) | copy-start | bytes 12582916
  55.4 8.8 %collective-permute-start.10 = (bf16[192,512]{1,0:T(8,128)(2,1)S(1)}, bf16[192,512]{1,0:T(8,128)(2,1)S(1)}, u32[]{:S(2)}, u32[]{:S(2)}) collective-permute-start(bf16[192,512]{1,0:T(8,128)(2,1)S(1)} %get-tuple-element.41), channel_id=1, source_target_pairs={{0,6},{1,7},{2,4},{3,5},{4,2},{5,3},{6,0},{7,1},{8,14},{9,15},{10,... | collective-permute-start | bytes 589832 | tf_op jit(solution)/shard_map/ppermute | solution.py:163
  55.9 12.7 %collective-permute-start.8 = (bf16[192,512]{1,0:T(8,128)(2,1)S(1)}, bf16[192,512]{1,0:T(8,128)(2,1)S(1)}, u32[]{:S(2)}, u32[]{:S(2)}) collective-permute-start(bf16[192,512]{1,0:T(8,128)(2,1)S(1)} %get-tuple-element.39), channel_id=1, source_target_pairs={{0,2},{1,3},{2,0},{3,1},{4,6},{5,7},{6,4},{7,5},{8,10},{9,11},{10,... | collective-permute-start | bytes 589832 | tf_op jit(solution)/shard_map/ppermute | solution.py:163
  58.6 11.2 %collective-permute-start.9 = (bf16[192,512]{1,0:T(8,128)(2,1)S(1)}, bf16[192,512]{1,0:T(8,128)(2,1)S(1)}, u32[]{:S(2)}, u32[]{:S(2)}) collective-permute-start(bf16[192,512]{1,0:T(8,128)(2,1)S(1)} %get-tuple-element.40), channel_id=1, source_target_pairs={{0,4},{1,5},{2,6},{3,7},{4,0},{5,1},{6,2},{7,3},{8,12},{9,13},{10,... | collective-permute-start | bytes 589832 | tf_op jit(solution)/shard_map/ppermute | solution.py:163
  61.2 11.7 %collective-permute-start.13 = (bf16[192,512]{1,0:T(8,128)(2,1)S(1)}, bf16[192,512]{1,0:T(8,128)(2,1)S(1)}, u32[]{:S(2)}, u32[]{:S(2)}) collective-permute-start(bf16[192,512]{1,0:T(8,128)(2,1)S(1)} %get-tuple-element.43), channel_id=1, source_target_pairs={{0,2},{1,3},{2,0},{3,1},{4,6},{5,7},{6,4},{7,5},{8,10},{9,11},{10,... | collective-permute-start | bytes 589832 | tf_op jit(solution)/shard_map/ppermute | solution.py:163
  61.6 13.6 %collective-permute-start.14 = (bf16[192,512]{1,0:T(8,128)(2,1)S(1)}, bf16[192,512]{1,0:T(8,128)(2,1)S(1)}, u32[]{:S(2)}, u32[]{:S(2)}) collective-permute-start(bf16[192,512]{1,0:T(8,128)(2,1)S(1)} %get-tuple-element.44), channel_id=1, source_target_pairs={{0,4},{1,5},{2,6},{3,7},{4,0},{5,1},{6,2},{7,3},{8,12},{9,13},{10,... | collective-permute-start | bytes 589832 | tf_op jit(solution)/shard_map/ppermute | solution.py:163
  64.2 8.8 %copy-start.4 = (bf16[1,256,2048]{2,1,0:T(8,128)(2,1)S(1)}, bf16[1,256,2048]{2,1,0:T(8,128)(2,1)}, u32[]{:S(2)}) copy-start(bf16[1,256,2048]{2,1,0:T(8,128)(2,1)} %param.7) | copy-start | bytes 3145732
  64.2 8.8 %copy-start.6 = (bf16[1,256,2048]{2,1,0:T(8,128)(2,1)S(1)}, bf16[1,256,2048]{2,1,0:T(8,128)(2,1)}, u32[]{:S(2)}) copy-start(bf16[1,256,2048]{2,1,0:T(8,128)(2,1)} %param.11) | copy-start | bytes 3145732
  64.2 8.8 %copy-start.17 = (bf16[1,2048,8]{1,2,0:T(8,128)(2,1)S(1)}, bf16[1,2048,8]{1,2,0:T(8,128)(2,1)}, u32[]{:S(2)}) copy-start(bf16[1,2048,8]{1,2,0:T(8,128)(2,1)} %param.9) | copy-start | bytes 98308
  64.2 8.8 %copy-start.19 = (f32[1,2048]{1,0:T(1,128)S(1)}, f32[1,2048]{1,0:T(1,128)}, u32[]{:S(2)}) copy-start(f32[1,2048]{1,0:T(1,128)} %refs_3_.3) | copy-start | bytes 24580
  64.2 8.8 %copy-start.21 = (s32[1,256,2]{1,2,0:T(2,128)S(1)}, s32[1,256,2]{1,2,0:T(2,128)}, u32[]{:S(2)}) copy-start(s32[1,256,2]{1,2,0:T(2,128)} %param.8) | copy-start | bytes 6148
  64.2 14.7 %collective-permute-start.15 = (bf16[192,512]{1,0:T(8,128)(2,1)S(1)}, bf16[192,512]{1,0:T(8,128)(2,1)S(1)}, u32[]{:S(2)}, u32[]{:S(2)}) collective-permute-start(bf16[192,512]{1,0:T(8,128)(2,1)S(1)} %get-tuple-element.45), channel_id=1, source_target_pairs={{0,6},{1,7},{2,4},{3,5},{4,2},{5,3},{6,0},{7,1},{8,14},{9,15},{10,... | collective-permute-start | bytes 589832 | tf_op jit(solution)/shard_map/ppermute | solution.py:163
  68.7 16.0 %collective-permute-start.18 = (bf16[192,512]{1,0:T(8,128)(2,1)S(1)}, bf16[192,512]{1,0:T(8,128)(2,1)S(1)}, u32[]{:S(2)}, u32[]{:S(2)}) collective-permute-start(bf16[192,512]{1,0:T(8,128)(2,1)S(1)} %get-tuple-element.47), channel_id=1, source_target_pairs={{0,2},{1,3},{2,0},{3,1},{4,6},{5,7},{6,4},{7,5},{8,10},{9,11},{10,... | collective-permute-start | bytes 589832 | tf_op jit(solution)/shard_map/ppermute | solution.py:163
  69.8 15.6 %collective-permute-start.19 = (bf16[192,512]{1,0:T(8,128)(2,1)S(1)}, bf16[192,512]{1,0:T(8,128)(2,1)S(1)}, u32[]{:S(2)}, u32[]{:S(2)}) collective-permute-start(bf16[192,512]{1,0:T(8,128)(2,1)S(1)} %get-tuple-element.48), channel_id=1, source_target_pairs={{0,4},{1,5},{2,6},{3,7},{4,0},{5,1},{6,2},{7,3},{8,12},{9,13},{10,... | collective-permute-start | bytes 589832 | tf_op jit(solution)/shard_map/ppermute | solution.py:163
  72.9 15.1 %collective-permute-start.20 = (bf16[192,512]{1,0:T(8,128)(2,1)S(1)}, bf16[192,512]{1,0:T(8,128)(2,1)S(1)}, u32[]{:S(2)}, u32[]{:S(2)}) collective-permute-start(bf16[192,512]{1,0:T(8,128)(2,1)S(1)} %get-tuple-element.49), channel_id=1, source_target_pairs={{0,6},{1,7},{2,4},{3,5},{4,2},{5,3},{6,0},{7,1},{8,14},{9,15},{10,... | collective-permute-start | bytes 589832 | tf_op jit(solution)/shard_map/ppermute | solution.py:163
  75.3 25.9 %collective-permute-start.11 = (bf16[256,512]{1,0:T(8,128)(2,1)S(1)}, bf16[256,512]{1,0:T(8,128)(2,1)}, u32[]{:S(2)}, u32[]{:S(2)}) collective-permute-start(bf16[256,512]{1,0:T(8,128)(2,1)S(1)} %combine.4), channel_id=1, source_target_pairs={{0,24},{8,16},{16,8},{24,0},{1,25},{9,17},{17,9},{25,1},{2,26},{10... | collective-permute-start | bytes 786440 | tf_op jit(solution)/shard_map/ppermute | solution.py:254
  78.9 26.0 %collective-permute-start.12 = (bf16[256,512]{1,0:T(8,128)(2,1)S(1)}, bf16[256,512]{1,0:T(8,128)(2,1)}, u32[]{:S(2)}, u32[]{:S(2)}) collective-permute-start(bf16[256,512]{1,0:T(8,128)(2,1)S(1)} %combine.4), channel_id=1, source_target_pairs={{0,8},{16,24},{1,9},{17,25},{2,10},{18,26},{3,11},{19,27},{4,12},{... | collective-permute-start | bytes 786440 | tf_op jit(solution)/shard_map/ppermute | solution.py:256
  84.0 0.7 copy-start.11
  84.7 5.7 %collective-permute-start.23 = (bf16[192,512]{1,0:T(8,128)(2,1)S(1)}, bf16[192,512]{1,0:T(8,128)(2,1)S(1)}, u32[]{:S(2)}, u32[]{:S(2)}) collective-permute-start(bf16[192,512]{1,0:T(8,128)(2,1)S(1)} %get-tuple-element.51), channel_id=1, source_target_pairs={{0,2},{1,3},{2,0},{3,1},{4,6},{5,7},{6,4},{7,5},{8,10},{9,11},{10,... | collective-permute-start | bytes 589832 | tf_op jit(solution)/shard_map/ppermute | solution.py:163
  85.4 0.7 copy-start.7
  86.1 7.1 %collective-permute-start.24 = (bf16[192,512]{1,0:T(8,128)(2,1)S(1)}, bf16[192,512]{1,0:T(8,128)(2,1)S(1)}, u32[]{:S(2)}, u32[]{:S(2)}) collective-permute-start(bf16[192,512]{1,0:T(8,128)(2,1)S(1)} %get-tuple-element.52), channel_id=1, source_target_pairs={{0,4},{1,5},{2,6},{3,7},{4,0},{5,1},{6,2},{7,3},{8,12},{9,13},{10,... | collective-permute-start | bytes 589832 | tf_op jit(solution)/shard_map/ppermute | solution.py:163
  87.9 4.0 %copy-start.9 = (bf16[192,512]{1,0:T(8,128)(2,1)}, bf16[192,512]{1,0:T(8,128)(2,1)S(1)}, u32[]{:S(2)}) copy-start(bf16[192,512]{1,0:T(8,128)(2,1)S(1)} %collective-permute-done.20.refs_5_) | copy-start | bytes 589828
  87.9 11.2 %collective-permute-start.25 = (bf16[192,512]{1,0:T(8,128)(2,1)}, bf16[192,512]{1,0:T(8,128)(2,1)}, u32[]{:S(2)}, u32[]{:S(2)}) collective-permute-start(bf16[192,512]{1,0:T(8,128)(2,1)} %get-tuple-element.53), channel_id=1, source_target_pairs={{0,6},{1,7},{2,4},{3,5},{4,2},{5,3},{6,0},{7,1},{8,14},{9,15},{10,... | collective-permute-start | bytes 589832 | tf_op jit(solution)/shard_map/ppermute | solution.py:163
  90.4 0.7 copy-start.13
  91.0 15.7 %collective-permute-start.16 = (bf16[256,512]{1,0:T(8,128)(2,1)S(1)}, bf16[256,512]{1,0:T(8,128)(2,1)}, u32[]{:S(2)}, u32[]{:S(2)}) collective-permute-start(bf16[256,512]{1,0:T(8,128)(2,1)S(1)} %combine.5), channel_id=1, source_target_pairs={{0,24},{8,16},{16,8},{24,0},{1,25},{9,17},{17,9},{25,1},{2,26},{10... | collective-permute-start | bytes 786440 | tf_op jit(solution)/shard_map/ppermute | solution.py:254
  93.2 0.7 copy-start.15
  93.9 16.5 %collective-permute-start.17 = (bf16[256,512]{1,0:T(8,128)(2,1)S(1)}, bf16[256,512]{1,0:T(8,128)(2,1)}, u32[]{:S(2)}, u32[]{:S(2)}) collective-permute-start(bf16[256,512]{1,0:T(8,128)(2,1)S(1)} %combine.5), channel_id=1, source_target_pairs={{0,8},{16,24},{1,9},{17,25},{2,10},{18,26},{3,11},{19,27},{4,12},{... | collective-permute-start | bytes 786440 | tf_op jit(solution)/shard_map/ppermute | solution.py:256
  96.9 0.9 copy-start.8
  97.8 0.9 copy-start.10
  98.8 0.9 copy-start.12
  98.8 1.0 copy-start.14
  98.8 1.1 copy-start.16
  99.1 12.3 %collective-permute-start.21 = (bf16[256,512]{1,0:T(8,128)(2,1)S(1)}, bf16[256,512]{1,0:T(8,128)(2,1)S(1)}, u32[]{:S(2)}, u32[]{:S(2)}) collective-permute-start(bf16[256,512]{1,0:T(8,128)(2,1)S(1)} %combine.6), channel_id=1, source_target_pairs={{0,24},{8,16},{16,8},{24,0},{1,25},{9,17},{17,9},{25,1},{2,26},{10... | collective-permute-start | bytes 786440 | tf_op jit(solution)/shard_map/ppermute | solution.py:254
  101.2 14.5 %collective-permute-start.22 = (bf16[256,512]{1,0:T(8,128)(2,1)S(1)}, bf16[256,512]{1,0:T(8,128)(2,1)S(1)}, u32[]{:S(2)}, u32[]{:S(2)}) collective-permute-start(bf16[256,512]{1,0:T(8,128)(2,1)S(1)} %combine.6), channel_id=1, source_target_pairs={{0,8},{16,24},{1,9},{17,25},{2,10},{18,26},{3,11},{19,27},{4,12},{... | collective-permute-start | bytes 786440 | tf_op jit(solution)/shard_map/ppermute | solution.py:256
  104.9 14.9 %collective-permute-start.26 = (bf16[256,512]{1,0:T(8,128)(2,1)S(1)}, bf16[256,512]{1,0:T(8,128)(2,1)S(1)}, u32[]{:S(2)}, u32[]{:S(2)}) collective-permute-start(bf16[256,512]{1,0:T(8,128)(2,1)S(1)} %combine.7), channel_id=1, source_target_pairs={{0,24},{8,16},{16,8},{24,0},{1,25},{9,17},{17,9},{25,1},{2,26},{10... | collective-permute-start | bytes 786440 | tf_op jit(solution)/shard_map/ppermute | solution.py:254
  106.8 15.8 %collective-permute-start.27 = (bf16[256,512]{1,0:T(8,128)(2,1)S(1)}, bf16[256,512]{1,0:T(8,128)(2,1)S(1)}, u32[]{:S(2)}, u32[]{:S(2)}) collective-permute-start(bf16[256,512]{1,0:T(8,128)(2,1)S(1)} %combine.7), channel_id=1, source_target_pairs={{0,8},{16,24},{1,9},{17,25},{2,10},{18,26},{3,11},{19,27},{4,12},{... | collective-permute-start | bytes 786440 | tf_op jit(solution)/shard_map/ppermute | solution.py:256

commit v3 on v2

v3 whole, which is shorter than its diff:
```python
import jax
import jax.numpy as jnp
from jax import lax
from jax.experimental import pallas as pl
from jax.experimental.pallas import tpu as pltpu
from jax.sharding import PartitionSpec as P

VMEM = pl.BlockSpec(memory_space=pltpu.VMEM)
SMEM = pl.BlockSpec(memory_space=pltpu.SMEM)
HBM = pl.BlockSpec(memory_space=pltpu.HBM)
ANY = pl.BlockSpec(memory_space=pl.ANY)
BF16 = jnp.bfloat16
F32 = jnp.float32
IN_PARTS = (10, 6)
OUT_PARTS = (4, 5, 4, 3)


def cut(width, parts):
    unit, start, ranges = width // sum(parts), 0, []
    for part in parts:
        ranges.append((start, start + part * unit))
        start += part * unit
    return ranges


def inverse_rms(values):
    return lax.rsqrt(jnp.mean(values * values, axis=-1, keepdims=True) + 1e-06)


def matmul(a, b):
    return jnp.dot(a, b, preferred_element_type=F32)


def slot_table(me, ids, experts, slots):
    tokens = ids.shape[1]
    rows = experts * slots
    expert = lax.broadcasted_iota(jnp.int32, (experts, tokens), 0) ^ me
    named = jnp.zeros((experts, tokens), F32)
    for k in range(ids.shape[0]):
        named = named + jnp.where(ids[k : k + 1, :] == expert, 1.0, 0.0)
    before = lax.broadcasted_iota(jnp.int32, (tokens, tokens), 0)
    after = lax.broadcasted_iota(jnp.int32, (tokens, tokens), 1)
    earlier = jnp.where(before < after, 1.0, 0.0)
    tally = matmul(named.astype(BF16), earlier.astype(BF16))
    slot = jnp.where(named > 0.0, tally, -1.0)
    row = lax.broadcasted_iota(jnp.int32, (rows, experts), 0)
    low = lax.broadcasted_iota(jnp.int32, (rows, experts), 1) * slots
    spread = jnp.where((row >= low) & (row < low + slots), 1.0, 0.0)
    wanted = matmul(spread.astype(BF16), slot.astype(BF16))
    first = jnp.sum(spread * low.astype(F32), axis=1, keepdims=True)
    place = lax.broadcasted_iota(jnp.int32, (rows, 1), 0).astype(F32) - first
    return wanted == place, spread.astype(BF16), named, expert


def sum_rows(late, acts, skip, gain):
    skip = skip.astype(F32)
    term = gain * (skip * inverse_rms(skip))
    return acts.astype(F32) + jnp.where(late > 0, term, jnp.zeros_like(term))


def dispatch_kernel(experts, slots, pieces, columns, late_ref, me_ref, ids_hbm, gain_hbm, acts_hbm, skip_hbm, *rest):
    chips = experts // 2
    out_refs = rest[: chips * len(columns)]
    ids_ref, gain_ref, acts_ref, skip_ref, normed_ref, *held, sems, small, done = rest[chips * len(columns) :]
    tokens = acts_ref.shape[0]
    size = tokens // pieces
    ids_copy = pltpu.make_async_copy(ids_hbm, ids_ref, small.at[0])
    gain_copy = pltpu.make_async_copy(gain_hbm, gain_ref, small.at[1])
    ids_copy.start()
    gain_copy.start()
    copies = []
    for r in range(pieces):
        part = pl.ds(r * size, size)
        pair = (
            pltpu.make_async_copy(skip_hbm.at[part], skip_ref.at[part], sems.at[0, r]),
            pltpu.make_async_copy(acts_hbm.at[part], acts_ref.at[part], sems.at[1, r]),
        )
        for copy in pair:
            copy.start()
        copies.append(pair)
    ids_copy.wait()
    taken, _, _, _ = slot_table(me_ref[0], ids_ref[...], experts, slots)
    pick = jnp.where(taken, 1.0, 0.0).astype(BF16)
    gain_copy.wait()
    for r in range(pieces):
        part = pl.ds(r * size, size)
        for copy in copies[r]:
            copy.wait()
        h = sum_rows(late_ref[0], acts_ref[part], skip_ref[part], gain_ref[...])
        normed_ref[part] = (h * inverse_rms(h)).astype(BF16)
    sends = []
    for c, ends in enumerate(columns):
        held[c][...] = matmul(pick, normed_ref[:, ends[0] : ends[1]]).astype(BF16)
        for k in range(chips):
            block = held[c].at[pl.ds(k * 2 * slots, 2 * slots)]
            send = pltpu.make_async_copy(block, out_refs[c * chips + k], done.at[c * chips + k])
            send.start()
            sends.append(send)
    for send in sends:
        send.wait()


def gate_kernel(experts, slots, late_ref, me_ref, ids_ref, gain_ref, acts_ref, skip_ref, router_ref, mix_ref, h_ref):
    h = sum_rows(late_ref[0], acts_ref[...], skip_ref[...], gain_ref[...])
    h_ref[...] = h
    normed = (h * inverse_rms(h)).astype(BF16)
    logits = lax.dot_general(
        router_ref[...], normed, (((1,), (1,)), ((), ())), preferred_element_type=F32
    )
    taken, spread, named, expert = slot_table(me_ref[0], ids_ref[...], experts, slots)
    natural = lax.broadcasted_iota(jnp.int32, (experts, ids_ref.shape[1]), 0)
    chosen = jnp.zeros(natural.shape, F32)
    for k in range(ids_ref.shape[0]):
        chosen = chosen + jnp.where(ids_ref[k : k + 1, :] == natural, 1.0, 0.0)
    peak = jnp.max(jnp.where(chosen > 0.0, logits, -jnp.inf), axis=0, keepdims=True)
    mass = jnp.where(chosen > 0.0, jnp.exp(logits - peak), 0.0)
    gates = (mass / jnp.sum(mass, axis=0, keepdims=True)).astype(BF16)
    order = lax.broadcasted_iota(jnp.int32, (experts, experts), 0) ^ me_ref[0]
    swap = jnp.where(order == lax.broadcasted_iota(jnp.int32, (experts, experts), 1), 1.0, 0.0)
    turned = matmul(swap.astype(BF16), gates).astype(BF16)
    wide = matmul(spread, turned)
    mix_ref[...] = jnp.where(taken, wide, 0.0).T.astype(BF16)


def hold_kernel(source, target, sem):
    copy = pltpu.make_async_copy(source, target, sem)
    copy.start()
    copy.wait()


def first_kernel(chips, slots, columns, tile, first, last, *refs):
    blocks, (own_ref, other_ref, before_ref), (out_ref, held) = refs[:chips], refs[chips : chips + 3], refs[-2:]
    for k in range(chips):
        for half in range(2):
            held[half, k * slots : (k + 1) * slots] = blocks[k][half * slots : (half + 1) * slots]
    size = chips * slots
    for half, weight in enumerate((own_ref, other_ref)):
        part = slice(half * size, (half + 1) * size)
        for j in range(0, out_ref.shape[1], tile):
            total = matmul(held[half], weight[columns[0] : columns[1], j : j + tile])
            if not first:
                total = total + before_ref[part, j : j + tile]
            out_ref[part, j : j + tile] = jax.nn.gelu(total, approximate=True).astype(BF16) if last else total


def second_kernel(chips, slots, columns, hidden_ref, own_ref, other_ref, *refs):
    size = chips * slots
    out_refs = refs[-chips:]
    for half, weight in enumerate((own_ref, other_ref)):
        worked = matmul(hidden_ref[half * size : (half + 1) * size], weight[:, columns[0] : columns[1]]).astype(BF16)
        for k in range(chips):
            out_refs[k][half * slots : (half + 1) * slots] = worked[k * slots : (k + 1) * slots]


def combine_kernel(chips, columns, h_ref, mix_ref, *refs):
    blocks, out_ref, held = refs[:chips], refs[-2], refs[-1]
    size = blocks[0].shape[0]
    for k in range(chips):
        held[k * size : (k + 1) * size] = blocks[k][...]
    out_ref[...] = (h_ref[:, columns[0] : columns[1]] + matmul(mix_ref[...], held[...])).astype(BF16)


def place_kernel(columns, shared_ref, across_ref, onward_ref, *refs):
    handed_ref, mirrored_ref, sems = refs[-3:]
    part = pl.ds(columns[0], columns[1] - columns[0])
    copy = pltpu.make_async_copy(across_ref, mirrored_ref.at[:, part], sems.at[0])
    copy.start()

    @pl.when(shared_ref[0] > 0)
    def _():
        again = pltpu.make_async_copy(across_ref, handed_ref.at[:, part], sems.at[1])
        again.start()
        again.wait()

    @pl.when(shared_ref[0] == 0)
    def _():
        again = pltpu.make_async_copy(onward_ref, handed_ref.at[:, part], sems.at[1])
        again.start()
        again.wait()

    copy.wait()


def local(acts, expert_ids, router, skip_gain, skip_rows, w_in, w_out):
    section_pos = lax.axis_index("section")
    sections = lax.axis_size("section")
    devices = lax.axis_size("expert")
    tokens, width = acts.shape[1:]
    topk = expert_ids.shape[2]
    experts = router.shape[2]
    hidden_width = w_in.shape[3]
    capacity = 3 * tokens * topk // (2 * experts)
    slots = -(-capacity // 16) * 16
    rows = experts * slots
    chips = devices // 2

    def params(mib):
        return pltpu.CompilerParams(vmem_limit_bytes=mib * 2**20)

    late = (section_pos >= sections // 2).astype(jnp.int32).reshape(1)
    me = lax.axis_index("expert").astype(jnp.int32).reshape(1)
    ids = expert_ids[0].T
    first, second = w_in[0, 0], w_out[0, 0]

    def across_core(block):
        return lax.ppermute(block, "expert", [(i, i ^ 1) for i in range(devices)])

    def exchange(blocks):
        return [blocks[0]] + [
            lax.ppermute(blocks[k], "expert", [(i, i ^ (2 * k)) for i in range(devices)])
            for k in range(1, chips)
        ]

    incoming = cut(width, IN_PARTS)
    outgoing = cut(width, OUT_PARTS)

    def sendable(ends):
        return [jax.ShapeDtypeStruct((2 * slots, ends[1] - ends[0]), BF16)] * chips

    pieces = 4
    sent = pl.pallas_call(
        lambda *refs: dispatch_kernel(experts, slots, pieces, incoming, *refs),
        out_shape=[shape for ends in incoming for shape in sendable(ends)],
        in_specs=[SMEM, SMEM, HBM, HBM, HBM, HBM],
        out_specs=[HBM] * (chips * len(incoming)),
        scratch_shapes=[
            pltpu.VMEM((topk, tokens), jnp.int32),
            pltpu.VMEM((1, width), F32),
            pltpu.VMEM((tokens, width), BF16),
            pltpu.VMEM((tokens, width), BF16),
            pltpu.VMEM((tokens, width), BF16),
        ]
        + [pltpu.VMEM((rows, ends[1] - ends[0]), BF16) for ends in incoming]
        + [
            pltpu.SemaphoreType.DMA((2, pieces)),
            pltpu.SemaphoreType.DMA((2,)),
            pltpu.SemaphoreType.DMA((chips * len(incoming),)),
        ],
        compiler_params=params(62),
        name="dispatch",
    )(late, me, ids, skip_gain, acts[0], skip_rows[0])

    def hold(block):
        return pl.pallas_call(
            hold_kernel,
            out_shape=jax.ShapeDtypeStruct(block.shape, block.dtype),
            in_specs=[ANY],
            out_specs=VMEM,
            scratch_shapes=[pltpu.SemaphoreType.DMA],
            compiler_params=params(16),
            name="hold",
        )(block)

    other_first = hold(across_core(first))
    other_second = hold(across_core(second))

    mix, h_rows = pl.pallas_call(
        lambda *refs: gate_kernel(experts, slots, *refs),
        out_shape=(
            jax.ShapeDtypeStruct((tokens, rows), BF16),
            jax.ShapeDtypeStruct((tokens, width), F32),
        ),
        in_specs=[SMEM, SMEM] + [VMEM] * 5,
        out_specs=(VMEM, VMEM),
        compiler_params=params(16),
        name="gates",
    )(late, me, ids, skip_gain, acts[0], skip_rows[0], router[0].T)

    total = mix
    for c, ends in enumerate(incoming):
        arrived = exchange(sent[c * chips : (c + 1) * chips])
        last = c == len(incoming) - 1
        total = pl.pallas_call(
            lambda *refs, c=c, ends=ends, last=last: first_kernel(
                chips, slots, ends, min(512, hidden_width), c == 0, last, *refs
            ),
            out_shape=jax.ShapeDtypeStruct((rows, hidden_width), BF16 if last else F32),
            in_specs=[VMEM] * (chips + 2) + [ANY if c == 0 else VMEM, ANY],
            out_specs=VMEM,
            scratch_shapes=[pltpu.VMEM((2, chips * slots, ends[1] - ends[0]), BF16)],
            compiler_params=params(16),
            name="first_matmul",
        )(*arrived, first, other_first, total, mix if c == 0 else other_second)
    hidden = total

    mirror = [(s, sections - 1 - s) for s in range(sections)]
    same = [s for s in range(sections) if (s - 1) % sections == sections - 1 - s]
    onward = [((s - 1) % sections, s) for s in range(sections) if s not in same]
    shared = jnp.zeros((), jnp.bool_)
    for s in same:
        shared = shared | (section_pos == s)
    shared = shared.astype(jnp.int32).reshape(1)
    made, gone, placed = [], [], []
    for c, ends in enumerate(outgoing):
        after = gone[c - 2] + [made[c - 1]] if c >= 2 else []
        worked = pl.pallas_call(
            lambda *refs, ends=ends: second_kernel(chips, slots, ends, *refs),
            out_shape=sendable(ends),
            in_specs=[VMEM] * 3 + [ANY] * len(after),
            out_specs=[VMEM] * chips,
            compiler_params=params(16),
            name="second_matmul",
        )(hidden, second, other_second, *after)
        back = exchange(worked)
        later = gone[c - 1] if c == len(outgoing) - 1 else []
        y = pl.pallas_call(
            lambda *refs, ends=ends: combine_kernel(chips, ends, *refs),
            out_shape=jax.ShapeDtypeStruct((tokens, ends[1] - ends[0]), BF16),
            in_specs=[VMEM] * (chips + 2) + [ANY] * len(later),
            out_specs=VMEM,
            scratch_shapes=[pltpu.VMEM((rows, ends[1] - ends[0]), BF16)],
            compiler_params=params(16),
            name="combine",
        )(h_rows, mix, *back, *later)
        made.append(y)
        across = lax.ppermute(y, "section", mirror)
        ahead = lax.ppermute(y, "section", onward) if onward else across
        gone.append([across, ahead])
        placed = pl.pallas_call(
            lambda *refs, ends=ends: place_kernel(ends, *refs),
            out_shape=[jax.ShapeDtypeStruct((tokens, width), BF16)] * 2,
            in_specs=[SMEM, ANY, ANY] + [HBM] * len(placed),
            out_specs=[HBM, HBM],
            scratch_shapes=[pltpu.SemaphoreType.DMA((2,))],
            input_output_aliases={3: 0, 4: 1} if placed else {},
            compiler_params=params(16),
            name="place",
        )(shared, across, ahead, *placed)
    return (placed[0][None], placed[1][None])


def solution(mesh):
    placed = (
        P("section", "expert", None),
        P("section", "expert", None),
        P("section", None, None),
        P("section", None),
        P("section", "expert", None),
        P("section", "expert", None, None),
        P("section", "expert", None, None),
    )
    return jax.shard_map(
        local,
        mesh=mesh,
        in_specs=placed,
        out_specs=(P("section", "expert", None), P("section", "expert", None)),
        check_vma=False,
    )
```

time: 127 us -> 114 us (0.90)
  local copies, waits for them, and re-layouts: 11.3 us -> 5.87 us
  other arithmetic: 5.27 us -> 0 us
  starting transfers between devices: 39 us -> 42.3 us
  waiting for transfers between devices: 42.9 us -> 39.7 us
  Pallas kernels: 26.5 us -> 25.2 us
    ppermute x4, waiting for transfers between devices: 7.04 us -> 0.01 us  [local(): ahead = lax.ppermute(y, 'section', onward) if onward else across]
    unnamed x44 -> x18, local copies, waits for them, and re-layouts: 11.3 us -> 5.87 us
    ppermute x18, waiting for transfers between devices: 31.8 us -> 36.7 us  [exchange(): lax.ppermute(blocks[k], 'expert', [(i, i ^ 2 * k) for i in range(devices)])]
    broadcast_in_dim x2 -> x0, other arithmetic: 3.22 us -> none  [the longest x1 2.13 us: local(): jnp.concatenate(mirrored, axis=1)[None]]
    select_n x4 -> x0, other arithmetic: 2.05 us -> none  [local(): jnp.where(shared, across, lax.ppermute(y, 'section', onward))]
    ppermute x18, starting transfers between devices: 20.4 us -> 22.4 us  [exchange(): lax.ppermute(blocks[k], 'expert', [(i, i ^ 2 * k) for i in range(devices)])]
    ppermute x4, starting transfers between devices: 12.5 us -> 14.1 us  [local(): ahead = lax.ppermute(y, 'section', onward) if onward else across]
    pallas_call x11 -> x17, Pallas kernels: 24.6 us -> 23.3 us  [the longest x1 5.39 us: local(): pl.pallas_call(lambda *refs: dispatch_kernel(experts, slots, pieces, inco...]
  transfers between devices with their start and end apart: 28 -> 28, of which waited for: 11 -> 12; matrix products, arithmetic and copies ran while one was open for 2% -> 0% of each run, Pallas kernels for 19% -> 18%
where the time goes in v3:
time: 114 us
  starting transfers between devices  42.3 us (37%)
  waiting for transfers between devices  39.7 us (35%)
  Pallas kernels  25.2 us (22%)
  local copies, waits for them, and re-layouts  5.87 us (5%)
    ppermute x18, waiting for transfers between devices, exchange(): lax.ppermute(blocks[k], 'expert', [(i, i ^ 2 * k) for i in range(devices)])  36.7 us
    ppermute x18, starting transfers between devices, exchange(): lax.ppermute(blocks[k], 'expert', [(i, i ^ 2 * k) for i in range(devices)])  22.4 us
    ppermute x4, starting transfers between devices, local(): ahead = lax.ppermute(y, 'section', onward) if onward else across  14.1 us
    unnamed x18, local copies, waits for them, and re-layouts  5.87 us
    pallas_call x1, Pallas kernels, local(): pl.pallas_call(lambda *refs: dispatch_kernel(experts, slots, pieces, inco...  5.39 us
    ppermute x4, starting transfers between devices, local(): across = lax.ppermute(y, 'section', mirror)  5.13 us
    pallas_call x2, Pallas kernels, hold(): pl.pallas_call(hold_kernel, out_shape=jax.ShapeDtypeStruct(block.shape, b...  4.54 us
    pallas_call x4, Pallas kernels, local(): pl.pallas_call(lambda *refs, ends=ends: second_kernel(chips, slots, ends,...  4.31 us
  transfers between devices with their start and end apart: 28, of which 12 were waited for; matrix products, arithmetic and copies ran while one was open for 0% of the time, Pallas kernels for 18%

profile of v3, /device:TPU:0, one launch (start us, length us, event | category | flops | bytes accessed | tf_op | source)
XLA Modules:
  0.0 113.9 jit_solution(17911092197129975035)
XLA Ops:
  0.6 0.5 collective-permute-start.3
  1.1 0.1 collective-permute-start.7
  1.2 5.4 %dispatch.1 = (bf16[192,1280]{1,0:T(8,128)(2,1)}, bf16[192,1280]{1,0:T(8,128)(2,1)}, bf16[192,1280]{1,0:T(8,128)(2,1)}, bf16[192,1280]{1,0:T(8,128)(2,1)}, bf16[...) custom-call(s32[1]{0:T(128)} %bitcast.1.refs_0_, ...), custom_call_target="tpu_custom_call" | custom-call | tf_op jit(solution)/shard_map/dispatch/pallas_call | solution.py:221
  6.6 3.0 %collective-permute-start.4 = (bf16[192,1280]{1,0:T(8,128)(2,1)}, bf16[192,1280]{1,0:T(8,128)(2,1)S(1)}, u32[]{:S(2)}, u32[]{:S(2)}) collective-permute-start(bf16[192,1280]{1,0:T(8,128)(2,1)} %get-tuple-element.43), channel_id=1, source_target_pairs={{0,2},{1,3},{2,0},{3,1},{4,6},{5,7},{6,4},{7,5},{8,10},{9,11},{10,... | collective-permute-start | bytes 1474568 | tf_op jit(solution)/shard_map/ppermute | solution.py:210
  9.6 1.5 %collective-permute-start.5 = (bf16[192,1280]{1,0:T(8,128)(2,1)}, bf16[192,1280]{1,0:T(8,128)(2,1)S(1)}, u32[]{:S(2)}, u32[]{:S(2)}) collective-permute-start(bf16[192,1280]{1,0:T(8,128)(2,1)} %get-tuple-element.44), channel_id=1, source_target_pairs={{0,4},{1,5},{2,6},{3,7},{4,0},{5,1},{6,2},{7,3},{8,12},{9,13},{10,... | collective-permute-start | bytes 1474568 | tf_op jit(solution)/shard_map/ppermute | solution.py:210
  11.2 10.7 %collective-permute-done.4.refs_1_ = bf16[192,1280]{1,0:T(8,128)(2,1)S(1)} collective-permute-done((bf16[192,1280]{1,0:T(8,128)(2,1)}, bf16[192,1280]{1,0:T(8,128)(2,1)S(1)}, u32[]{:S(2)}, u32[]{:S(2)}) %collective-permute-start.4) | collective-permute-done | bytes 491552 | tf_op jit(solution)/shard_map/ppermute | solution.py:210
  21.8 2.1 %collective-permute-start = (bf16[192,768]{1,0:T(8,128)(2,1)}, bf16[192,768]{1,0:T(8,128)(2,1)S(1)}, u32[]{:S(2)}, u32[]{:S(2)}) collective-permute-start(bf16[192,768]{1,0:T(8,128)(2,1)} %get-tuple-element.39), channel_id=1, source_target_pairs={{0,2},{1,3},{2,0},{3,1},{4,6},{5,7},{6,4},{7,5},{8,10},{9,11},{10,... | collective-permute-start | bytes 884744 | tf_op jit(solution)/shard_map/ppermute | solution.py:210
  23.9 1.5 %collective-permute-start.1 = (bf16[192,768]{1,0:T(8,128)(2,1)}, bf16[192,768]{1,0:T(8,128)(2,1)S(1)}, u32[]{:S(2)}, u32[]{:S(2)}) collective-permute-start(bf16[192,768]{1,0:T(8,128)(2,1)} %get-tuple-element.40), channel_id=1, source_target_pairs={{0,4},{1,5},{2,6},{3,7},{4,0},{5,1},{6,2},{7,3},{8,12},{9,13},{10,... | collective-permute-start | bytes 884744 | tf_op jit(solution)/shard_map/ppermute | solution.py:210
  25.5 1.2 %copy-done.2 = bf16[1,256,2048]{2,1,0:T(8,128)(2,1)S(1)} copy-done((bf16[1,256,2048]{2,1,0:T(8,128)(2,1)S(1)}, bf16[1,256,2048]{2,1,0:T(8,128)(2,1)}, u32[]{:S(2)}) %copy-start.2) | copy-done | bytes 1048600
  26.7 1.2 %copy-done.3 = bf16[1,256,2048]{2,1,0:T(8,128)(2,1)S(1)} copy-done((bf16[1,256,2048]{2,1,0:T(8,128)(2,1)S(1)}, bf16[1,256,2048]{2,1,0:T(8,128)(2,1)}, u32[]{:S(2)}) %copy-start.3) | copy-done | bytes 1048600
  27.9 0.8 copy-done.6
  28.7 0.7 copy-done.7
  29.4 0.7 copy-done.8
  30.1 1.9 %gates.1 = (bf16[256,768]{1,0:T(8,128)(2,1)S(1)}, f32[256,2048]{1,0:T(8,128)S(1)}) custom-call(s32[1]{0:T(128)} %bitcast.1.refs_0_, s32[1]{0:T(128)} %bitcast.2.refs_1_, s32[2,256]{1,0:T(2,128)S(1)} %bitcast.29, f32[1,2048]{1,0:T(1,128)S(1)} %copy-done.7, bf16[256,2048]{1,0:T(8,128)(2,1)S(1)} %bitcast.24, bf16[256,2048]{1,0:T(8,128)(2,1)S(1)} %bitcast.26, ...), custom_call_target="tpu_custom_call" | custom-call | tf_op jit(solution)/shard_map/gates/pallas_call | solution.py:257
  32.0 2.2 %hold.2.refs_5_ = bf16[2048,1024]{1,0:T(8,128)(2,1)S(1)} custom-call(bf16[2048,1024]{1,0:T(8,128)(2,1)} %collective-permute-done.3.source), custom_call_target="tpu_custom_call" | custom-call | tf_op jit(solution)/shard_map/hold/pallas_call | solution.py:244
  34.2 2.3 %hold.3.refs_7_.refs_2_ = bf16[1024,2048]{1,0:T(8,128)(2,1)S(1)} custom-call(bf16[1024,2048]{1,0:T(8,128)(2,1)} %collective-permute-done.7.source), custom_call_target="tpu_custom_call" | custom-call | tf_op jit(solution)/shard_map/hold/pallas_call | solution.py:244
  36.6 1.1 copy-done.1
  37.6 0.1 copy-done.4
  37.7 2.2 %first_matmul.2.refs_6_ = f32[768,1024]{1,0:T(8,128)S(1)} custom-call(bf16[192,1280]{1,0:T(8,128)(2,1)S(1)} %copy-done.4, bf16[192,1280]{1,0:T(8,128)(2,1)S(1)} %collective-permute-done.4.refs_1_, bf16[192,1280]{1,0:T(8,128)(2,1)S(1)} %collective-permute-done.5.refs_2_, bf16[192,1280]{1,0:T(8,128)(2,1)S(1)} %collective-permute-done.6.refs_3_, ...), custom_call_target="tpu_custom_call" | custom-call | tf_op jit(solution)/shard_map/first_matmul/pallas_call | solution.py:273
  39.9 6.0 %collective-permute-done.1.refs_2_ = bf16[192,768]{1,0:T(8,128)(2,1)S(1)} collective-permute-done((bf16[192,768]{1,0:T(8,128)(2,1)}, bf16[192,768]{1,0:T(8,128)(2,1)S(1)}, u32[]{:S(2)}, u32[]{:S(2)}) %collective-permute-start.1) | collective-permute-done | bytes 294944 | tf_op jit(solution)/shard_map/ppermute | solution.py:210
  45.9 2.1 %first_matmul.3.refs_0_ = bf16[768,1024]{1,0:T(8,128)(2,1)S(1)} custom-call(bf16[192,768]{1,0:T(8,128)(2,1)S(1)} %copy-done.5, bf16[192,768]{1,0:T(8,128)(2,1)S(1)} %collective-permute-done.refs_1_, bf16[192,768]{1,0:T(8,128)(2,1)S(1)} %collective-permute-done.1.refs_2_, bf16[192,768]{1,0:T(8,128)(2,1)S(1)} %collective-permute-done.2.refs_3_, ...), custom_call_target="tpu_custom_call" | custom-call | tf_op jit(solution)/shard_map/first_matmul/pallas_call | solution.py:273
  48.0 0.1 copy-done
  48.1 1.0 second_matmul.5
  49.1 1.3 %collective-permute-start.13 = (bf16[192,512]{1,0:T(8,128)(2,1)S(1)}, bf16[192,512]{1,0:T(8,128)(2,1)S(1)}, u32[]{:S(2)}, u32[]{:S(2)}) collective-permute-start(bf16[192,512]{1,0:T(8,128)(2,1)S(1)} %get-tuple-element.51), channel_id=1, source_target_pairs={{0,2},{1,3},{2,0},{3,1},{4,6},{5,7},{6,4},{7,5},{8,10},{9,11},{10,... | collective-permute-start | bytes 589832 | tf_op jit(solution)/shard_map/ppermute | solution.py:210
  50.4 0.8 collective-permute-start.14
  51.2 1.4 %collective-permute-start.15 = (bf16[192,512]{1,0:T(8,128)(2,1)S(1)}, bf16[192,512]{1,0:T(8,128)(2,1)S(1)}, u32[]{:S(2)}, u32[]{:S(2)}) collective-permute-start(bf16[192,512]{1,0:T(8,128)(2,1)S(1)} %get-tuple-element.53), channel_id=1, source_target_pairs={{0,6},{1,7},{2,4},{3,5},{4,2},{5,3},{6,0},{7,1},{8,14},{9,15},{10,... | collective-permute-start | bytes 589832 | tf_op jit(solution)/shard_map/ppermute | solution.py:210
  52.7 1.4 %second_matmul.4 = (bf16[192,640]{1,0:T(8,128)(2,1)S(1)}, bf16[192,640]{1,0:T(8,128)(2,1)S(1)}, bf16[192,640]{1,0:T(8,128)(2,1)S(1)}, bf16[192,640]{1,0:T(8,128)(2,1)S(1)}) custom-call(bf16[768,1024]{1,0:T(8,128)(2,1)S(1)} %first_matmul.3.refs_0_, bf16[1024,2048]{1,0:T(8,128)(2,1)S(1)} %bitcast.17, bf16[1024,2048]{1,0:T(8,128)(2,1)S(1)} %hold.3.refs_7_.refs_2_), custom_call_target="tpu_custom_call" | custom-call | tf_op jit(solution)/shard_map/second_matmul/pallas_call | solution.py:296
  54.0 1.3 %collective-permute-start.8 = (bf16[192,640]{1,0:T(8,128)(2,1)S(1)}, bf16[192,640]{1,0:T(8,128)(2,1)S(1)}, u32[]{:S(2)}, u32[]{:S(2)}) collective-permute-start(bf16[192,640]{1,0:T(8,128)(2,1)S(1)} %get-tuple-element.47), channel_id=1, source_target_pairs={{0,2},{1,3},{2,0},{3,1},{4,6},{5,7},{6,4},{7,5},{8,10},{9,11},{10,... | collective-permute-start | bytes 737288 | tf_op jit(solution)/shard_map/ppermute | solution.py:210
  55.4 0.8 collective-permute-start.9
  56.2 0.8 collective-permute-done.13.refs_3_
  56.9 1.5 %collective-permute-start.10 = (bf16[192,640]{1,0:T(8,128)(2,1)S(1)}, bf16[192,640]{1,0:T(8,128)(2,1)S(1)}, u32[]{:S(2)}, u32[]{:S(2)}) collective-permute-start(bf16[192,640]{1,0:T(8,128)(2,1)S(1)} %get-tuple-element.49), channel_id=1, source_target_pairs={{0,6},{1,7},{2,4},{3,5},{4,2},{5,3},{6,0},{7,1},{8,14},{9,15},{10,... | collective-permute-start | bytes 737288 | tf_op jit(solution)/shard_map/ppermute | solution.py:210
  58.4 2.7 %collective-permute-done.14.refs_4_ = bf16[192,512]{1,0:T(8,128)(2,1)S(1)} collective-permute-done((bf16[192,512]{1,0:T(8,128)(2,1)S(1)}, bf16[192,512]{1,0:T(8,128)(2,1)S(1)}, u32[]{:S(2)}, u32[]{:S(2)}) %collective-permute-start.14) | collective-permute-done | bytes 196640 | tf_op jit(solution)/shard_map/ppermute | solution.py:210
  61.1 0.8 collective-permute-done.15.refs_5_
  61.9 0.4 combine.5
  62.2 3.6 %collective-permute-start.17 = (bf16[256,512]{1,0:T(8,128)(2,1)S(1)}, bf16[256,512]{1,0:T(8,128)(2,1)S(1)}, u32[]{:S(2)}, u32[]{:S(2)}) collective-permute-start(bf16[256,512]{1,0:T(8,128)(2,1)S(1)} %combine.5), channel_id=1, source_target_pairs={{0,8},{16,24},{1,9},{17,25},{2,10},{18,26},{3,11},{19,27},{4,12},{... | collective-permute-start | bytes 786440 | tf_op jit(solution)/shard_map/ppermute | solution.py:317
  65.8 1.5 %collective-permute-start.16 = (bf16[256,512]{1,0:T(8,128)(2,1)S(1)}, bf16[256,512]{1,0:T(8,128)(2,1)S(1)}, u32[]{:S(2)}, u32[]{:S(2)}) collective-permute-start(bf16[256,512]{1,0:T(8,128)(2,1)S(1)} %combine.5), channel_id=1, source_target_pairs={{0,24},{8,16},{16,8},{24,0},{1,25},{9,17},{17,9},{25,1},{2,26},{10... | collective-permute-start | bytes 786440 | tf_op jit(solution)/shard_map/ppermute | solution.py:316
  67.3 3.6 %collective-permute-done.9.refs_4_ = bf16[192,640]{1,0:T(8,128)(2,1)S(1)} collective-permute-done((bf16[192,640]{1,0:T(8,128)(2,1)S(1)}, bf16[192,640]{1,0:T(8,128)(2,1)S(1)}, u32[]{:S(2)}, u32[]{:S(2)}) %collective-permute-start.9) | collective-permute-done | bytes 245792 | tf_op jit(solution)/shard_map/ppermute | solution.py:210
  71.0 0.5 combine.4.refs_5_
  71.4 3.5 %collective-permute-start.12 = (bf16[256,640]{1,0:T(8,128)(2,1)S(1)}, bf16[256,640]{1,0:T(8,128)(2,1)S(1)}, u32[]{:S(2)}, u32[]{:S(2)}) collective-permute-start(bf16[256,640]{1,0:T(8,128)(2,1)S(1)} %combine.4.refs_5_), channel_id=1, source_target_pairs={{0,8},{16,24},{1,9},{17,25},{2,10},{18,26},{3,11},{19,27},{4,12},{... | collective-permute-start | bytes 983048 | tf_op jit(solution)/shard_map/ppermute | solution.py:317
  74.9 1.5 %collective-permute-start.11 = (bf16[256,640]{1,0:T(8,128)(2,1)S(1)}, bf16[256,640]{1,0:T(8,128)(2,1)S(1)}, u32[]{:S(2)}, u32[]{:S(2)}) collective-permute-start(bf16[256,640]{1,0:T(8,128)(2,1)S(1)} %combine.4.refs_5_), channel_id=1, source_target_pairs={{0,24},{8,16},{16,8},{24,0},{1,25},{9,17},{17,9},{25,1},{2,26},{10... | collective-permute-start | bytes 983048 | tf_op jit(solution)/shard_map/ppermute | solution.py:316
  76.4 1.0 second_matmul.6
  77.4 1.6 %collective-permute-start.18 = (bf16[192,512]{1,0:T(8,128)(2,1)S(1)}, bf16[192,512]{1,0:T(8,128)(2,1)S(1)}, u32[]{:S(2)}, u32[]{:S(2)}) collective-permute-start(bf16[192,512]{1,0:T(8,128)(2,1)S(1)} %get-tuple-element.55), channel_id=1, source_target_pairs={{0,2},{1,3},{2,0},{3,1},{4,6},{5,7},{6,4},{7,5},{8,10},{9,11},{10,... | collective-permute-start | bytes 589832 | tf_op jit(solution)/shard_map/ppermute | solution.py:210
  79.0 0.6 collective-permute-start.19
  79.6 1.4 %collective-permute-start.20 = (bf16[192,512]{1,0:T(8,128)(2,1)S(1)}, bf16[192,512]{1,0:T(8,128)(2,1)S(1)}, u32[]{:S(2)}, u32[]{:S(2)}) collective-permute-start(bf16[192,512]{1,0:T(8,128)(2,1)S(1)} %get-tuple-element.57), channel_id=1, source_target_pairs={{0,6},{1,7},{2,4},{3,5},{4,2},{5,3},{6,0},{7,1},{8,14},{9,15},{10,... | collective-permute-start | bytes 589832 | tf_op jit(solution)/shard_map/ppermute | solution.py:210
  81.0 4.2 %collective-permute-done.18.refs_3_ = bf16[192,512]{1,0:T(8,128)(2,1)S(1)} collective-permute-done((bf16[192,512]{1,0:T(8,128)(2,1)S(1)}, bf16[192,512]{1,0:T(8,128)(2,1)S(1)}, u32[]{:S(2)}, u32[]{:S(2)}) %collective-permute-start.18) | collective-permute-done | bytes 196640 | tf_op jit(solution)/shard_map/ppermute | solution.py:210
  85.2 3.2 %collective-permute-done.19.refs_4_ = bf16[192,512]{1,0:T(8,128)(2,1)S(1)} collective-permute-done((bf16[192,512]{1,0:T(8,128)(2,1)S(1)}, bf16[192,512]{1,0:T(8,128)(2,1)S(1)}, u32[]{:S(2)}, u32[]{:S(2)}) %collective-permute-start.19) | collective-permute-done | bytes 196640 | tf_op jit(solution)/shard_map/ppermute | solution.py:210
  88.4 0.4 combine.6.refs_5_
  88.8 4.0 %collective-permute-start.25 = (bf16[256,512]{1,0:T(8,128)(2,1)S(1)}, bf16[256,512]{1,0:T(8,128)(2,1)S(1)}, u32[]{:S(2)}, u32[]{:S(2)}) collective-permute-start(bf16[256,512]{1,0:T(8,128)(2,1)S(1)} %combine.6.refs_5_), channel_id=1, source_target_pairs={{0,8},{16,24},{1,9},{17,25},{2,10},{18,26},{3,11},{19,27},{4,12},{... | collective-permute-start | bytes 786440 | tf_op jit(solution)/shard_map/ppermute | solution.py:317
  92.8 0.1 collective-permute-start.24
  92.9 1.0 second_matmul.7
  93.9 0.7 collective-permute-start.21
  94.6 1.5 %collective-permute-start.22 = (bf16[192,384]{1,0:T(8,128)(2,1)S(1)}, bf16[192,384]{1,0:T(8,128)(2,1)S(1)}, u32[]{:S(2)}, u32[]{:S(2)}) collective-permute-start(bf16[192,384]{1,0:T(8,128)(2,1)S(1)} %get-tuple-element.60), channel_id=1, source_target_pairs={{0,4},{1,5},{2,6},{3,7},{4,0},{5,1},{6,2},{7,3},{8,12},{9,13},{10,... | collective-permute-start | bytes 442376 | tf_op jit(solution)/shard_map/ppermute | solution.py:210
  96.1 1.4 %collective-permute-start.23 = (bf16[192,384]{1,0:T(8,128)(2,1)S(1)}, bf16[192,384]{1,0:T(8,128)(2,1)S(1)}, u32[]{:S(2)}, u32[]{:S(2)}) collective-permute-start(bf16[192,384]{1,0:T(8,128)(2,1)S(1)} %get-tuple-element.61), channel_id=1, source_target_pairs={{0,6},{1,7},{2,4},{3,5},{4,2},{5,3},{6,0},{7,1},{8,14},{9,15},{10,... | collective-permute-start | bytes 442376 | tf_op jit(solution)/shard_map/ppermute | solution.py:210
  97.4 1.7 %collective-permute-done.21.refs_3_ = bf16[192,384]{1,0:T(8,128)(2,1)S(1)} collective-permute-done((bf16[192,384]{1,0:T(8,128)(2,1)S(1)}, bf16[192,384]{1,0:T(8,128)(2,1)S(1)}, u32[]{:S(2)}, u32[]{:S(2)}) %collective-permute-start.21) | collective-permute-done | bytes 147488 | tf_op jit(solution)/shard_map/ppermute | solution.py:210
  99.1 0.6 collective-permute-done.22.refs_4_
  99.7 2.4 %collective-permute-done.23.refs_5_ = bf16[192,384]{1,0:T(8,128)(2,1)S(1)} collective-permute-done((bf16[192,384]{1,0:T(8,128)(2,1)S(1)}, bf16[192,384]{1,0:T(8,128)(2,1)S(1)}, u32[]{:S(2)}, u32[]{:S(2)}) %collective-permute-start.23) | collective-permute-done | bytes 147488 | tf_op jit(solution)/shard_map/ppermute | solution.py:210
  102.1 0.4 combine.7
  102.5 3.0 %collective-permute-start.27 = (bf16[256,384]{1,0:T(8,128)(2,1)S(1)}, bf16[256,384]{1,0:T(8,128)(2,1)S(1)}, u32[]{:S(2)}, u32[]{:S(2)}) collective-permute-start(bf16[256,384]{1,0:T(8,128)(2,1)S(1)} %combine.7), channel_id=1, source_target_pairs={{0,8},{16,24},{1,9},{17,25},{2,10},{18,26},{3,11},{19,27},{4,12},{... | collective-permute-start | bytes 589832 | tf_op jit(solution)/shard_map/ppermute | solution.py:317
  105.5 2.1 %collective-permute-start.26 = (bf16[256,384]{1,0:T(8,128)(2,1)S(1)}, bf16[256,384]{1,0:T(8,128)(2,1)S(1)}, u32[]{:S(2)}, u32[]{:S(2)}) collective-permute-start(bf16[256,384]{1,0:T(8,128)(2,1)S(1)} %combine.7), channel_id=1, source_target_pairs={{0,24},{8,16},{16,8},{24,0},{1,25},{9,17},{17,9},{25,1},{2,26},{10... | collective-permute-start | bytes 589832 | tf_op jit(solution)/shard_map/ppermute | solution.py:316
  107.7 0.8 place.4
  108.5 0.9 place.5
  109.3 0.8 place.6
  110.2 3.0 %collective-permute-done.26.refs_1_ = bf16[256,384]{1,0:T(8,128)(2,1)S(1)} collective-permute-done((bf16[256,384]{1,0:T(8,128)(2,1)S(1)}, bf16[256,384]{1,0:T(8,128)(2,1)S(1)}, u32[]{:S(2)}, u32[]{:S(2)}) %collective-permute-start.26) | collective-permute-done | bytes 196640 | tf_op jit(solution)/shard_map/ppermute | solution.py:316
  113.2 0.8 place.7
  (28 shorter events, 0.1 us)
Async XLA Ops:
  0.6 23.3 %collective-permute-start.3 = (bf16[2048,1024]{1,0:T(8,128)(2,1)}, bf16[2048,1024]{1,0:T(8,128)(2,1)}, u32[]{:S(2)}, u32[]{:S(2)}) collective-permute-start(bf16[2048,1024]{1,0:T(8,128)(2,1)} %bitcast.20), channel_id=1, source_target_pairs={{0,1},{1,0},{2,3},{3,2},{4,5},{5,4},{6,7},{7,6},{8,9},{9,8},{10,11... | collective-permute-start | bytes 12582920 | tf_op jit(solution)/shard_map/ppermute | solution.py:206
  1.1 24.3 %collective-permute-start.7 = (bf16[1024,2048]{1,0:T(8,128)(2,1)}, bf16[1024,2048]{1,0:T(8,128)(2,1)}, u32[]{:S(2)}, u32[]{:S(2)}) collective-permute-start(bf16[1024,2048]{1,0:T(8,128)(2,1)} %bitcast.15), channel_id=1, source_target_pairs={{0,1},{1,0},{2,3},{3,2},{4,5},{5,4},{6,7},{7,6},{8,9},{9,8},{10,11... | collective-permute-start | bytes 12582920 | tf_op jit(solution)/shard_map/ppermute | solution.py:206
  6.6 15.2 %collective-permute-start.4 = (bf16[192,1280]{1,0:T(8,128)(2,1)}, bf16[192,1280]{1,0:T(8,128)(2,1)S(1)}, u32[]{:S(2)}, u32[]{:S(2)}) collective-permute-start(bf16[192,1280]{1,0:T(8,128)(2,1)} %get-tuple-element.43), channel_id=1, source_target_pairs={{0,2},{1,3},{2,0},{3,1},{4,6},{5,7},{6,4},{7,5},{8,10},{9,11},{10,... | collective-permute-start | bytes 1474568 | tf_op jit(solution)/shard_map/ppermute | solution.py:210
  9.6 26.9 %collective-permute-start.5 = (bf16[192,1280]{1,0:T(8,128)(2,1)}, bf16[192,1280]{1,0:T(8,128)(2,1)S(1)}, u32[]{:S(2)}, u32[]{:S(2)}) collective-permute-start(bf16[192,1280]{1,0:T(8,128)(2,1)} %get-tuple-element.44), channel_id=1, source_target_pairs={{0,4},{1,5},{2,6},{3,7},{4,0},{5,1},{6,2},{7,3},{8,12},{9,13},{10,... | collective-permute-start | bytes 1474568 | tf_op jit(solution)/shard_map/ppermute | solution.py:210
  11.1 25.4 %collective-permute-start.6 = (bf16[192,1280]{1,0:T(8,128)(2,1)}, bf16[192,1280]{1,0:T(8,128)(2,1)S(1)}, u32[]{:S(2)}, u32[]{:S(2)}) collective-permute-start(bf16[192,1280]{1,0:T(8,128)(2,1)} %get-tuple-element.45), channel_id=1, source_target_pairs={{0,6},{1,7},{2,4},{3,5},{4,2},{5,3},{6,0},{7,1},{8,14},{9,15},{10,... | collective-permute-start | bytes 1474568 | tf_op jit(solution)/shard_map/ppermute | solution.py:210
  21.8 18.1 %collective-permute-start = (bf16[192,768]{1,0:T(8,128)(2,1)}, bf16[192,768]{1,0:T(8,128)(2,1)S(1)}, u32[]{:S(2)}, u32[]{:S(2)}) collective-permute-start(bf16[192,768]{1,0:T(8,128)(2,1)} %get-tuple-element.39), channel_id=1, source_target_pairs={{0,2},{1,3},{2,0},{3,1},{4,6},{5,7},{6,4},{7,5},{8,10},{9,11},{10,... | collective-permute-start | bytes 884744 | tf_op jit(solution)/shard_map/ppermute | solution.py:210
  23.9 22.0 %collective-permute-start.1 = (bf16[192,768]{1,0:T(8,128)(2,1)}, bf16[192,768]{1,0:T(8,128)(2,1)S(1)}, u32[]{:S(2)}, u32[]{:S(2)}) collective-permute-start(bf16[192,768]{1,0:T(8,128)(2,1)} %get-tuple-element.40), channel_id=1, source_target_pairs={{0,4},{1,5},{2,6},{3,7},{4,0},{5,1},{6,2},{7,3},{8,12},{9,13},{10,... | collective-permute-start | bytes 884744 | tf_op jit(solution)/shard_map/ppermute | solution.py:210
  25.4 20.5 %collective-permute-start.2 = (bf16[192,768]{1,0:T(8,128)(2,1)}, bf16[192,768]{1,0:T(8,128)(2,1)S(1)}, u32[]{:S(2)}, u32[]{:S(2)}) collective-permute-start(bf16[192,768]{1,0:T(8,128)(2,1)} %get-tuple-element.41), channel_id=1, source_target_pairs={{0,6},{1,7},{2,4},{3,5},{4,2},{5,3},{6,0},{7,1},{8,14},{9,15},{10,... | collective-permute-start | bytes 884744 | tf_op jit(solution)/shard_map/ppermute | solution.py:210
  25.5 1.2 %copy-start.2 = (bf16[1,256,2048]{2,1,0:T(8,128)(2,1)S(1)}, bf16[1,256,2048]{2,1,0:T(8,128)(2,1)}, u32[]{:S(2)}) copy-start(bf16[1,256,2048]{2,1,0:T(8,128)(2,1)} %param.7) | copy-start | bytes 3145732
  26.7 1.2 %copy-start.3 = (bf16[1,256,2048]{2,1,0:T(8,128)(2,1)S(1)}, bf16[1,256,2048]{2,1,0:T(8,128)(2,1)}, u32[]{:S(2)}) copy-start(bf16[1,256,2048]{2,1,0:T(8,128)(2,1)} %param.11) | copy-start | bytes 3145732
  27.9 0.8 copy-start.6
  28.7 0.7 copy-start.7
  29.4 0.7 copy-start.8
  34.2 3.5 %copy-start.1 = (bf16[1,1,2048,1024]{3,2,1,0:T(8,128)(2,1)S(1)}, bf16[1,1,2048,1024]{3,2,1,0:T(8,128)(2,1)}, u32[]{:S(2)}) copy-start(bf16[1,1,2048,1024]{3,2,1,0:T(8,128)(2,1)} %param.12) | copy-start | bytes 12582916
  34.2 3.5 %copy-start.4 = (bf16[192,1280]{1,0:T(8,128)(2,1)S(1)}, bf16[192,1280]{1,0:T(8,128)(2,1)}, u32[]{:S(2)}) copy-start(bf16[192,1280]{1,0:T(8,128)(2,1)} %get-tuple-element.42.refs_0_) | copy-start | bytes 1474564
  37.7 8.2 %copy-start.5 = (bf16[192,768]{1,0:T(8,128)(2,1)S(1)}, bf16[192,768]{1,0:T(8,128)(2,1)}, u32[]{:S(2)}) copy-start(bf16[192,768]{1,0:T(8,128)(2,1)} %get-tuple-element.38.refs_0_) | copy-start | bytes 884740
  45.9 2.2 %copy-start = (bf16[1,1,1024,2048]{3,2,1,0:T(8,128)(2,1)S(1)}, bf16[1,1,1024,2048]{3,2,1,0:T(8,128)(2,1)}, u32[]{:S(2)}) copy-start(bf16[1,1,1024,2048]{3,2,1,0:T(8,128)(2,1)} %param.13) | copy-start | bytes 12582916
  49.1 7.8 %collective-permute-start.13 = (bf16[192,512]{1,0:T(8,128)(2,1)S(1)}, bf16[192,512]{1,0:T(8,128)(2,1)S(1)}, u32[]{:S(2)}, u32[]{:S(2)}) collective-permute-start(bf16[192,512]{1,0:T(8,128)(2,1)S(1)} %get-tuple-element.51), channel_id=1, source_target_pairs={{0,2},{1,3},{2,0},{3,1},{4,6},{5,7},{6,4},{7,5},{8,10},{9,11},{10,... | collective-permute-start | bytes 589832 | tf_op jit(solution)/shard_map/ppermute | solution.py:210
  50.4 10.7 %collective-permute-start.14 = (bf16[192,512]{1,0:T(8,128)(2,1)S(1)}, bf16[192,512]{1,0:T(8,128)(2,1)S(1)}, u32[]{:S(2)}, u32[]{:S(2)}) collective-permute-start(bf16[192,512]{1,0:T(8,128)(2,1)S(1)} %get-tuple-element.52), channel_id=1, source_target_pairs={{0,4},{1,5},{2,6},{3,7},{4,0},{5,1},{6,2},{7,3},{8,12},{9,13},{10,... | collective-permute-start | bytes 589832 | tf_op jit(solution)/shard_map/ppermute | solution.py:210
  51.2 10.6 %collective-permute-start.15 = (bf16[192,512]{1,0:T(8,128)(2,1)S(1)}, bf16[192,512]{1,0:T(8,128)(2,1)S(1)}, u32[]{:S(2)}, u32[]{:S(2)}) collective-permute-start(bf16[192,512]{1,0:T(8,128)(2,1)S(1)} %get-tuple-element.53), channel_id=1, source_target_pairs={{0,6},{1,7},{2,4},{3,5},{4,2},{5,3},{6,0},{7,1},{8,14},{9,15},{10,... | collective-permute-start | bytes 589832 | tf_op jit(solution)/shard_map/ppermute | solution.py:210
  54.0 13.3 %collective-permute-start.8 = (bf16[192,640]{1,0:T(8,128)(2,1)S(1)}, bf16[192,640]{1,0:T(8,128)(2,1)S(1)}, u32[]{:S(2)}, u32[]{:S(2)}) collective-permute-start(bf16[192,640]{1,0:T(8,128)(2,1)S(1)} %get-tuple-element.47), channel_id=1, source_target_pairs={{0,2},{1,3},{2,0},{3,1},{4,6},{5,7},{6,4},{7,5},{8,10},{9,11},{10,... | collective-permute-start | bytes 737288 | tf_op jit(solution)/shard_map/ppermute | solution.py:210
  55.4 15.6 %collective-permute-start.9 = (bf16[192,640]{1,0:T(8,128)(2,1)S(1)}, bf16[192,640]{1,0:T(8,128)(2,1)S(1)}, u32[]{:S(2)}, u32[]{:S(2)}) collective-permute-start(bf16[192,640]{1,0:T(8,128)(2,1)S(1)} %get-tuple-element.48), channel_id=1, source_target_pairs={{0,4},{1,5},{2,6},{3,7},{4,0},{5,1},{6,2},{7,3},{8,12},{9,13},{10,... | collective-permute-start | bytes 737288 | tf_op jit(solution)/shard_map/ppermute | solution.py:210
  56.9 14.0 %collective-permute-start.10 = (bf16[192,640]{1,0:T(8,128)(2,1)S(1)}, bf16[192,640]{1,0:T(8,128)(2,1)S(1)}, u32[]{:S(2)}, u32[]{:S(2)}) collective-permute-start(bf16[192,640]{1,0:T(8,128)(2,1)S(1)} %get-tuple-element.49), channel_id=1, source_target_pairs={{0,6},{1,7},{2,4},{3,5},{4,2},{5,3},{6,0},{7,1},{8,14},{9,15},{10,... | collective-permute-start | bytes 737288 | tf_op jit(solution)/shard_map/ppermute | solution.py:210
  62.2 14.2 %collective-permute-start.17 = (bf16[256,512]{1,0:T(8,128)(2,1)S(1)}, bf16[256,512]{1,0:T(8,128)(2,1)S(1)}, u32[]{:S(2)}, u32[]{:S(2)}) collective-permute-start(bf16[256,512]{1,0:T(8,128)(2,1)S(1)} %combine.5), channel_id=1, source_target_pairs={{0,8},{16,24},{1,9},{17,25},{2,10},{18,26},{3,11},{19,27},{4,12},{... | collective-permute-start | bytes 786440 | tf_op jit(solution)/shard_map/ppermute | solution.py:317
  65.8 10.6 %collective-permute-start.16 = (bf16[256,512]{1,0:T(8,128)(2,1)S(1)}, bf16[256,512]{1,0:T(8,128)(2,1)S(1)}, u32[]{:S(2)}, u32[]{:S(2)}) collective-permute-start(bf16[256,512]{1,0:T(8,128)(2,1)S(1)} %combine.5), channel_id=1, source_target_pairs={{0,24},{8,16},{16,8},{24,0},{1,25},{9,17},{17,9},{25,1},{2,26},{10... | collective-permute-start | bytes 786440 | tf_op jit(solution)/shard_map/ppermute | solution.py:316
  71.4 21.4 %collective-permute-start.12 = (bf16[256,640]{1,0:T(8,128)(2,1)S(1)}, bf16[256,640]{1,0:T(8,128)(2,1)S(1)}, u32[]{:S(2)}, u32[]{:S(2)}) collective-permute-start(bf16[256,640]{1,0:T(8,128)(2,1)S(1)} %combine.4.refs_5_), channel_id=1, source_target_pairs={{0,8},{16,24},{1,9},{17,25},{2,10},{18,26},{3,11},{19,27},{4,12},{... | collective-permute-start | bytes 983048 | tf_op jit(solution)/shard_map/ppermute | solution.py:317
  74.9 17.9 %collective-permute-start.11 = (bf16[256,640]{1,0:T(8,128)(2,1)S(1)}, bf16[256,640]{1,0:T(8,128)(2,1)S(1)}, u32[]{:S(2)}, u32[]{:S(2)}) collective-permute-start(bf16[256,640]{1,0:T(8,128)(2,1)S(1)} %combine.4.refs_5_), channel_id=1, source_target_pairs={{0,24},{8,16},{16,8},{24,0},{1,25},{9,17},{17,9},{25,1},{2,26},{10... | collective-permute-start | bytes 983048 | tf_op jit(solution)/shard_map/ppermute | solution.py:316
  77.4 7.8 %collective-permute-start.18 = (bf16[192,512]{1,0:T(8,128)(2,1)S(1)}, bf16[192,512]{1,0:T(8,128)(2,1)S(1)}, u32[]{:S(2)}, u32[]{:S(2)}) collective-permute-start(bf16[192,512]{1,0:T(8,128)(2,1)S(1)} %get-tuple-element.55), channel_id=1, source_target_pairs={{0,2},{1,3},{2,0},{3,1},{4,6},{5,7},{6,4},{7,5},{8,10},{9,11},{10,... | collective-permute-start | bytes 589832 | tf_op jit(solution)/shard_map/ppermute | solution.py:210
  79.0 9.4 %collective-permute-start.19 = (bf16[192,512]{1,0:T(8,128)(2,1)S(1)}, bf16[192,512]{1,0:T(8,128)(2,1)S(1)}, u32[]{:S(2)}, u32[]{:S(2)}) collective-permute-start(bf16[192,512]{1,0:T(8,128)(2,1)S(1)} %get-tuple-element.56), channel_id=1, source_target_pairs={{0,4},{1,5},{2,6},{3,7},{4,0},{5,1},{6,2},{7,3},{8,12},{9,13},{10,... | collective-permute-start | bytes 589832 | tf_op jit(solution)/shard_map/ppermute | solution.py:210
  79.6 8.8 %collective-permute-start.20 = (bf16[192,512]{1,0:T(8,128)(2,1)S(1)}, bf16[192,512]{1,0:T(8,128)(2,1)S(1)}, u32[]{:S(2)}, u32[]{:S(2)}) collective-permute-start(bf16[192,512]{1,0:T(8,128)(2,1)S(1)} %get-tuple-element.57), channel_id=1, source_target_pairs={{0,6},{1,7},{2,4},{3,5},{4,2},{5,3},{6,0},{7,1},{8,14},{9,15},{10,... | collective-permute-start | bytes 589832 | tf_op jit(solution)/shard_map/ppermute | solution.py:210
  88.8 13.3 %collective-permute-start.25 = (bf16[256,512]{1,0:T(8,128)(2,1)S(1)}, bf16[256,512]{1,0:T(8,128)(2,1)S(1)}, u32[]{:S(2)}, u32[]{:S(2)}) collective-permute-start(bf16[256,512]{1,0:T(8,128)(2,1)S(1)} %combine.6.refs_5_), channel_id=1, source_target_pairs={{0,8},{16,24},{1,9},{17,25},{2,10},{18,26},{3,11},{19,27},{4,12},{... | collective-permute-start | bytes 786440 | tf_op jit(solution)/shard_map/ppermute | solution.py:317
  92.8 9.3 %collective-permute-start.24 = (bf16[256,512]{1,0:T(8,128)(2,1)S(1)}, bf16[256,512]{1,0:T(8,128)(2,1)S(1)}, u32[]{:S(2)}, u32[]{:S(2)}) collective-permute-start(bf16[256,512]{1,0:T(8,128)(2,1)S(1)} %combine.6.refs_5_), channel_id=1, source_target_pairs={{0,24},{8,16},{16,8},{24,0},{1,25},{9,17},{17,9},{25,1},{2,26},{10... | collective-permute-start | bytes 786440 | tf_op jit(solution)/shard_map/ppermute | solution.py:316
  93.9 5.2 %collective-permute-start.21 = (bf16[192,384]{1,0:T(8,128)(2,1)S(1)}, bf16[192,384]{1,0:T(8,128)(2,1)S(1)}, u32[]{:S(2)}, u32[]{:S(2)}) collective-permute-start(bf16[192,384]{1,0:T(8,128)(2,1)S(1)} %get-tuple-element.59), channel_id=1, source_target_pairs={{0,2},{1,3},{2,0},{3,1},{4,6},{5,7},{6,4},{7,5},{8,10},{9,11},{10,... | collective-permute-start | bytes 442376 | tf_op jit(solution)/shard_map/ppermute | solution.py:210
  94.6 5.1 %collective-permute-start.22 = (bf16[192,384]{1,0:T(8,128)(2,1)S(1)}, bf16[192,384]{1,0:T(8,128)(2,1)S(1)}, u32[]{:S(2)}, u32[]{:S(2)}) collective-permute-start(bf16[192,384]{1,0:T(8,128)(2,1)S(1)} %get-tuple-element.60), channel_id=1, source_target_pairs={{0,4},{1,5},{2,6},{3,7},{4,0},{5,1},{6,2},{7,3},{8,12},{9,13},{10,... | collective-permute-start | bytes 442376 | tf_op jit(solution)/shard_map/ppermute | solution.py:210
  96.1 6.0 %collective-permute-start.23 = (bf16[192,384]{1,0:T(8,128)(2,1)S(1)}, bf16[192,384]{1,0:T(8,128)(2,1)S(1)}, u32[]{:S(2)}, u32[]{:S(2)}) collective-permute-start(bf16[192,384]{1,0:T(8,128)(2,1)S(1)} %get-tuple-element.61), channel_id=1, source_target_pairs={{0,6},{1,7},{2,4},{3,5},{4,2},{5,3},{6,0},{7,1},{8,14},{9,15},{10,... | collective-permute-start | bytes 442376 | tf_op jit(solution)/shard_map/ppermute | solution.py:210
  102.5 7.7 %collective-permute-start.27 = (bf16[256,384]{1,0:T(8,128)(2,1)S(1)}, bf16[256,384]{1,0:T(8,128)(2,1)S(1)}, u32[]{:S(2)}, u32[]{:S(2)}) collective-permute-start(bf16[256,384]{1,0:T(8,128)(2,1)S(1)} %combine.7), channel_id=1, source_target_pairs={{0,8},{16,24},{1,9},{17,25},{2,10},{18,26},{3,11},{19,27},{4,12},{... | collective-permute-start | bytes 589832 | tf_op jit(solution)/shard_map/ppermute | solution.py:317
  105.5 7.6 %collective-permute-start.26 = (bf16[256,384]{1,0:T(8,128)(2,1)S(1)}, bf16[256,384]{1,0:T(8,128)(2,1)S(1)}, u32[]{:S(2)}, u32[]{:S(2)}) collective-permute-start(bf16[256,384]{1,0:T(8,128)(2,1)S(1)} %combine.7), channel_id=1, source_target_pairs={{0,24},{8,16},{16,8},{24,0},{1,25},{9,17},{17,9},{25,1},{2,26},{10... | collective-permute-start | bytes 589832 | tf_op jit(solution)/shard_map/ppermute | solution.py:316

commit v4 on v3

--- a/solution.py
+++ b/solution.py
@@ -11,7 +11,7 @@
 ANY = pl.BlockSpec(memory_space=pl.ANY)
 BF16 = jnp.bfloat16
 F32 = jnp.float32
-IN_PARTS = (10, 6)
+IN_PARTS = (5, 7, 4)
 OUT_PARTS = (4, 5, 4, 3)
 
 
@@ -217,28 +217,31 @@
     def sendable(ends):
         return [jax.ShapeDtypeStruct((2 * slots, ends[1] - ends[0]), BF16)] * chips
 
-    pieces = 4
-    sent = pl.pallas_call(
-        lambda *refs: dispatch_kernel(experts, slots, pieces, incoming, *refs),
-        out_shape=[shape for ends in incoming for shape in sendable(ends)],
-        in_specs=[SMEM, SMEM, HBM, HBM, HBM, HBM],
-        out_specs=[HBM] * (chips * len(incoming)),
-        scratch_shapes=[
-            pltpu.VMEM((topk, tokens), jnp.int32),
-            pltpu.VMEM((1, width), F32),
-            pltpu.VMEM((tokens, width), BF16),
-            pltpu.VMEM((tokens, width), BF16),
-            pltpu.VMEM((tokens, width), BF16),
-        ]
-        + [pltpu.VMEM((rows, ends[1] - ends[0]), BF16) for ends in incoming]
-        + [
-            pltpu.SemaphoreType.DMA((2, pieces)),
-            pltpu.SemaphoreType.DMA((2,)),
-            pltpu.SemaphoreType.DMA((chips * len(incoming),)),
-        ],
-        compiler_params=params(62),
-        name="dispatch",
-    )(late, me, ids, skip_gain, acts[0], skip_rows[0])
+    pieces = 2
+    def dispatch(columns, mib):
+        return pl.pallas_call(
+            lambda *refs: dispatch_kernel(experts, slots, pieces, columns, *refs),
+            out_shape=[shape for ends in columns for shape in sendable(ends)],
+            in_specs=[SMEM, SMEM, HBM, HBM, HBM, HBM],
+            out_specs=[HBM] * (chips * len(columns)),
+            scratch_shapes=[
+                pltpu.VMEM((topk, tokens), jnp.int32),
+                pltpu.VMEM((1, width), F32),
+                pltpu.VMEM((tokens, width), BF16),
+                pltpu.VMEM((tokens, width), BF16),
+                pltpu.VMEM((tokens, width), BF16),
+            ]
+            + [pltpu.VMEM((rows, ends[1] - ends[0]), BF16) for ends in columns]
+            + [
+                pltpu.SemaphoreType.DMA((2, pieces)),
+                pltpu.SemaphoreType.DMA((2,)),
+                pltpu.SemaphoreType.DMA((chips * len(columns),)),
+            ],
+            compiler_params=params(mib),
+            name="dispatch",
+        )(late, me, ids, skip_gain, acts[0], skip_rows[0])
+
+    sent = [*dispatch(incoming[:1], 62), *dispatch(incoming[1:], 24)]
 
     def hold(block):
         return pl.pallas_call(

time: 114 us -> 113 us (level)
  waiting for transfers between devices: 39.7 us -> 32.8 us
  Pallas kernels: 25.2 us -> 28.4 us
  starting transfers between devices: 42.3 us -> 44.8 us
    ppermute x18 -> x21, waiting for transfers between devices: 36.7 us -> 29.2 us  [exchange(): lax.ppermute(blocks[k], 'expert', [(i, i ^ 2 * k) for i in range(devices)])]
    ppermute x18 -> x21, starting transfers between devices: 22.4 us -> 25.3 us  [exchange(): lax.ppermute(blocks[k], 'expert', [(i, i ^ 2 * k) for i in range(devices)])]
    pallas_call x1 -> x2, Pallas kernels: 5.39 us -> 7.96 us  [dispatch(): pl.pallas_call(lambda *refs: dispatch_kernel(experts, slots, pieces, colu...]
    pallas_call x2 -> x3, Pallas kernels: 4.24 us -> 4.86 us  [local(): pl.pallas_call(lambda *refs, c=c, ends=ends, last=last: first_kernel(chip...]
    unnamed x18 -> x16, local copies, waits for them, and re-layouts: 5.87 us -> 5.45 us
  transfers between devices with their start and end apart: 28 -> 31, of which waited for: 12 -> 15; matrix products, arithmetic and copies ran while one was open for 0% -> 0% of each run, Pallas kernels for 18% -> 22%
where the time goes in v4:
time: 113 us; the launch traced here: 112 us
  starting transfers between devices  44.8 us (40%)
  waiting for transfers between devices  32.8 us (29%)
  Pallas kernels  28.4 us (25%)
  local copies, waits for them, and re-layouts  5.45 us (5%)
    ppermute x21, waiting for transfers between devices, exchange(): lax.ppermute(blocks[k], 'expert', [(i, i ^ 2 * k) for i in range(devices)])  29.2 us
    ppermute x21, starting transfers between devices, exchange(): lax.ppermute(blocks[k], 'expert', [(i, i ^ 2 * k) for i in range(devices)])  25.3 us
    ppermute x4, starting transfers between devices, local(): ahead = lax.ppermute(y, 'section', onward) if onward else across  14.3 us
    pallas_call x2, Pallas kernels, dispatch(): pl.pallas_call(lambda *refs: dispatch_kernel(experts, slots, pieces, colu...  7.96 us
    unnamed x16, local copies, waits for them, and re-layouts  5.45 us
    pallas_call x3, Pallas kernels, local(): pl.pallas_call(lambda *refs, c=c, ends=ends, last=last: first_kernel(chip...  4.86 us
    ppermute x4, starting transfers between devices, local(): across = lax.ppermute(y, 'section', mirror)  4.55 us
    pallas_call x2, Pallas kernels, hold(): pl.pallas_call(hold_kernel, out_shape=jax.ShapeDtypeStruct(block.shape, b...  4.54 us
  transfers between devices with their start and end apart: 31, of which 15 were waited for; matrix products, arithmetic and copies ran while one was open for 0% of the time, Pallas kernels for 22%

profile of v4, /device:TPU:0, one launch (start us, length us, event | category | flops | bytes accessed | tf_op | source)
XLA Modules:
  0.0 112.3 jit_solution(3566694954777579946)
XLA Ops:
  0.6 0.5 collective-permute-start.3
  1.2 3.9 %dispatch.3 = (bf16[192,640]{1,0:T(8,128)(2,1)}, bf16[192,640]{1,0:T(8,128)(2,1)}, bf16[192,640]{1,0:T(8,128)(2,1)}, bf16[192,640]{1,0:T(8,128)(2,1)}) custom-call(s32[1]{0:T(128)} %bitcast.1.refs_0_, s32[1]{0:T(128)} %bitcast.2.refs_1_, s32[2,256]{1,0:T(2,128)} %bitcast.31, f32[1,2048]{1,0:T(1,128)} %refs_3_.5, bf16[256,2048]{1,0:T(8,128)(2,1)} %bitcast.24, ...), custom_call_target="tpu_custom_call" | custom-call | tf_op jit(solution)/shard_map/dispatch/pallas_call | solution.py:222
  5.2 3.0 %collective-permute-start.7 = (bf16[192,640]{1,0:T(8,128)(2,1)}, bf16[192,640]{1,0:T(8,128)(2,1)S(1)}, u32[]{:S(2)}, u32[]{:S(2)}) collective-permute-start(bf16[192,640]{1,0:T(8,128)(2,1)} %get-tuple-element.51), channel_id=1, source_target_pairs={{0,2},{1,3},{2,0},{3,1},{4,6},{5,7},{6,4},{7,5},{8,10},{9,11},{10,... | collective-permute-start | bytes 737288 | tf_op jit(solution)/shard_map/ppermute | solution.py:210
  8.2 1.5 %collective-permute-start.8 = (bf16[192,640]{1,0:T(8,128)(2,1)}, bf16[192,640]{1,0:T(8,128)(2,1)S(1)}, u32[]{:S(2)}, u32[]{:S(2)}) collective-permute-start(bf16[192,640]{1,0:T(8,128)(2,1)} %get-tuple-element.52), channel_id=1, source_target_pairs={{0,4},{1,5},{2,6},{3,7},{4,0},{5,1},{6,2},{7,3},{8,12},{9,13},{10,... | collective-permute-start | bytes 737288 | tf_op jit(solution)/shard_map/ppermute | solution.py:210
  9.7 1.2 %copy-done.2 = bf16[1,256,2048]{2,1,0:T(8,128)(2,1)S(1)} copy-done((bf16[1,256,2048]{2,1,0:T(8,128)(2,1)S(1)}, bf16[1,256,2048]{2,1,0:T(8,128)(2,1)}, u32[]{:S(2)}) %copy-start.2) | copy-done | bytes 1048600
  10.9 1.2 %copy-done.3 = bf16[1,256,2048]{2,1,0:T(8,128)(2,1)S(1)} copy-done((bf16[1,256,2048]{2,1,0:T(8,128)(2,1)S(1)}, bf16[1,256,2048]{2,1,0:T(8,128)(2,1)}, u32[]{:S(2)}) %copy-start.3) | copy-done | bytes 1048600
  12.1 0.7 copy-done.5
  12.8 0.7 copy-done.7
  13.5 4.0 %dispatch.2 = (bf16[192,896]{1,0:T(8,128)(2,1)S(1)}, bf16[192,896]{1,0:T(8,128)(2,1)S(1)}, bf16[192,896]{1,0:T(8,128)(2,1)S(1)}, bf16[192,896]{1,0:T(8,128)(2,1)...) custom-call(s32[1]{0:T(128)} %bitcast.1.refs_0_, ...), custom_call_target="tpu_custom_call" | custom-call | tf_op jit(solution)/shard_map/dispatch/pallas_call | solution.py:222
  17.6 2.0 %collective-permute-start.4 = (bf16[192,896]{1,0:T(8,128)(2,1)S(1)}, bf16[192,896]{1,0:T(8,128)(2,1)S(1)}, u32[]{:S(2)}, u32[]{:S(2)}) collective-permute-start(bf16[192,896]{1,0:T(8,128)(2,1)S(1)} %get-tuple-element.47), channel_id=1, source_target_pairs={{0,2},{1,3},{2,0},{3,1},{4,6},{5,7},{6,4},{7,5},{8,10},{9,11},{10,... | collective-permute-start | bytes 1032200 | tf_op jit(solution)/shard_map/ppermute | solution.py:210
  19.6 1.7 %collective-permute-done.8.refs_2_ = bf16[192,640]{1,0:T(8,128)(2,1)S(1)} collective-permute-done((bf16[192,640]{1,0:T(8,128)(2,1)}, bf16[192,640]{1,0:T(8,128)(2,1)S(1)}, u32[]{:S(2)}, u32[]{:S(2)}) %collective-permute-start.8) | collective-permute-done | bytes 245792 | tf_op jit(solution)/shard_map/ppermute | solution.py:210
  21.3 1.5 %collective-permute-start.5 = (bf16[192,896]{1,0:T(8,128)(2,1)S(1)}, bf16[192,896]{1,0:T(8,128)(2,1)S(1)}, u32[]{:S(2)}, u32[]{:S(2)}) collective-permute-start(bf16[192,896]{1,0:T(8,128)(2,1)S(1)} %get-tuple-element.48), channel_id=1, source_target_pairs={{0,4},{1,5},{2,6},{3,7},{4,0},{5,1},{6,2},{7,3},{8,12},{9,13},{10,... | collective-permute-start | bytes 1032200 | tf_op jit(solution)/shard_map/ppermute | solution.py:210
  22.9 5.8 %collective-permute-done.4.refs_1_ = bf16[192,896]{1,0:T(8,128)(2,1)S(1)} collective-permute-done((bf16[192,896]{1,0:T(8,128)(2,1)S(1)}, bf16[192,896]{1,0:T(8,128)(2,1)S(1)}, u32[]{:S(2)}, u32[]{:S(2)}) %collective-permute-start.4) | collective-permute-done | bytes 344096 | tf_op jit(solution)/shard_map/ppermute | solution.py:210
  28.6 2.0 %collective-permute-start = (bf16[192,512]{1,0:T(8,128)(2,1)S(1)}, bf16[192,512]{1,0:T(8,128)(2,1)S(1)}, u32[]{:S(2)}, u32[]{:S(2)}) collective-permute-start(bf16[192,512]{1,0:T(8,128)(2,1)S(1)} %get-tuple-element.43), channel_id=1, source_target_pairs={{0,2},{1,3},{2,0},{3,1},{4,6},{5,7},{6,4},{7,5},{8,10},{9,11},{10,... | collective-permute-start | bytes 589832 | tf_op jit(solution)/shard_map/ppermute | solution.py:210
  30.6 1.5 %collective-permute-start.1 = (bf16[192,512]{1,0:T(8,128)(2,1)S(1)}, bf16[192,512]{1,0:T(8,128)(2,1)S(1)}, u32[]{:S(2)}, u32[]{:S(2)}) collective-permute-start(bf16[192,512]{1,0:T(8,128)(2,1)S(1)} %get-tuple-element.44), channel_id=1, source_target_pairs={{0,4},{1,5},{2,6},{3,7},{4,0},{5,1},{6,2},{7,3},{8,12},{9,13},{10,... | collective-permute-start | bytes 589832 | tf_op jit(solution)/shard_map/ppermute | solution.py:210
  32.2 1.9 %gates.1 = (bf16[256,768]{1,0:T(8,128)(2,1)S(1)}, f32[256,2048]{1,0:T(8,128)S(1)}) custom-call(s32[1]{0:T(128)} %bitcast.1.refs_0_, s32[1]{0:T(128)} %bitcast.2.refs_1_, s32[2,256]{1,0:T(2,128)S(1)} %bitcast.33, f32[1,2048]{1,0:T(1,128)S(1)} %copy-done.5, bf16[256,2048]{1,0:T(8,128)(2,1)S(1)} %bitcast.26, bf16[256,2048]{1,0:T(8,128)(2,1)S(1)} %bitcast.29, ...), custom_call_target="tpu_custom_call" | custom-call | tf_op jit(solution)/shard_map/gates/pallas_call | solution.py:260
  34.1 2.2 %hold.2.refs_5_ = bf16[2048,1024]{1,0:T(8,128)(2,1)S(1)} custom-call(bf16[2048,1024]{1,0:T(8,128)(2,1)} %collective-permute-done.3.source), custom_call_target="tpu_custom_call" | custom-call | tf_op jit(solution)/shard_map/hold/pallas_call | solution.py:247
  36.3 2.3 %hold.3.refs_7_.refs_2_ = bf16[1024,2048]{1,0:T(8,128)(2,1)S(1)} custom-call(bf16[1024,2048]{1,0:T(8,128)(2,1)} %collective-permute-done.10.source), custom_call_target="tpu_custom_call" | custom-call | tf_op jit(solution)/shard_map/hold/pallas_call | solution.py:247
  38.7 1.1 copy-done.1
  39.8 1.4 %first_matmul.3.refs_6_ = f32[768,1024]{1,0:T(8,128)S(1)} custom-call(bf16[192,640]{1,0:T(8,128)(2,1)S(1)} %copy-done.4, bf16[192,640]{1,0:T(8,128)(2,1)S(1)} %collective-permute-done.7.refs_1_, bf16[192,640]{1,0:T(8,128)(2,1)S(1)} %collective-permute-done.8.refs_2_, bf16[192,640]{1,0:T(8,128)(2,1)S(1)} %collective-permute-done.9.refs_3_, ...), custom_call_target="tpu_custom_call" | custom-call | tf_op jit(solution)/shard_map/first_matmul/pallas_call | solution.py:276
  41.2 1.6 %collective-permute-done.5.refs_2_ = bf16[192,896]{1,0:T(8,128)(2,1)S(1)} collective-permute-done((bf16[192,896]{1,0:T(8,128)(2,1)S(1)}, bf16[192,896]{1,0:T(8,128)(2,1)S(1)}, u32[]{:S(2)}, u32[]{:S(2)}) %collective-permute-start.5) | collective-permute-done | bytes 344096 | tf_op jit(solution)/shard_map/ppermute | solution.py:210
  42.8 1.8 %first_matmul.4.refs_6_ = f32[768,1024]{1,0:T(8,128)S(1)} custom-call(bf16[192,896]{1,0:T(8,128)(2,1)S(1)} %get-tuple-element.46.refs_0_, bf16[192,896]{1,0:T(8,128)(2,1)S(1)} %collective-permute-done.4.refs_1_, bf16[192,896]{1,0:T(8,128)(2,1)S(1)} %collective-permute-done.5.refs_2_, bf16[192,896]{1,0:T(8,128)(2,1)S(1)} %collective-permute-done.6.refs_3_, ...), custom_call_target="tpu_custom_call" | custom-call | tf_op jit(solution)/shard_map/first_matmul/pallas_call | solution.py:276
  44.6 1.2 %collective-permute-done.1.refs_2_ = bf16[192,512]{1,0:T(8,128)(2,1)S(1)} collective-permute-done((bf16[192,512]{1,0:T(8,128)(2,1)S(1)}, bf16[192,512]{1,0:T(8,128)(2,1)S(1)}, u32[]{:S(2)}, u32[]{:S(2)}) %collective-permute-start.1) | collective-permute-done | bytes 196640 | tf_op jit(solution)/shard_map/ppermute | solution.py:210
  45.8 1.7 %first_matmul.5.refs_0_ = bf16[768,1024]{1,0:T(8,128)(2,1)S(1)} custom-call(bf16[192,512]{1,0:T(8,128)(2,1)S(1)} %get-tuple-element.42.refs_0_, bf16[192,512]{1,0:T(8,128)(2,1)S(1)} %collective-permute-done.refs_1_, bf16[192,512]{1,0:T(8,128)(2,1)S(1)} %collective-permute-done.1.refs_2_, bf16[192,512]{1,0:T(8,128)(2,1)S(1)} %collective-permute-done.2.refs_3_, ...), custom_call_target="tpu_custom_call" | custom-call | tf_op jit(solution)/shard_map/first_matmul/pallas_call | solution.py:276
  47.4 0.5 copy-done
  48.0 1.0 second_matmul.5
  49.0 1.8 %collective-permute-start.17 = (bf16[192,512]{1,0:T(8,128)(2,1)S(1)}, bf16[192,512]{1,0:T(8,128)(2,1)S(1)}, u32[]{:S(2)}, u32[]{:S(2)}) collective-permute-start(bf16[192,512]{1,0:T(8,128)(2,1)S(1)} %get-tuple-element.60), channel_id=1, source_target_pairs={{0,4},{1,5},{2,6},{3,7},{4,0},{5,1},{6,2},{7,3},{8,12},{9,13},{10,... | collective-permute-start | bytes 589832 | tf_op jit(solution)/shard_map/ppermute | solution.py:210
  50.8 1.7 %collective-permute-start.18 = (bf16[192,512]{1,0:T(8,128)(2,1)S(1)}, bf16[192,512]{1,0:T(8,128)(2,1)S(1)}, u32[]{:S(2)}, u32[]{:S(2)}) collective-permute-start(bf16[192,512]{1,0:T(8,128)(2,1)S(1)} %get-tuple-element.61), channel_id=1, source_target_pairs={{0,6},{1,7},{2,4},{3,5},{4,2},{5,3},{6,0},{7,1},{8,14},{9,15},{10,... | collective-permute-start | bytes 589832 | tf_op jit(solution)/shard_map/ppermute | solution.py:210
  52.5 1.4 %second_matmul.4 = (bf16[192,640]{1,0:T(8,128)(2,1)S(1)}, bf16[192,640]{1,0:T(8,128)(2,1)S(1)}, bf16[192,640]{1,0:T(8,128)(2,1)S(1)}, bf16[192,640]{1,0:T(8,128)(2,1)S(1)}) custom-call(bf16[768,1024]{1,0:T(8,128)(2,1)S(1)} %first_matmul.5.refs_0_, bf16[1024,2048]{1,0:T(8,128)(2,1)S(1)} %bitcast.17, bf16[1024,2048]{1,0:T(8,128)(2,1)S(1)} %hold.3.refs_7_.refs_2_), custom_call_target="tpu_custom_call" | custom-call | tf_op jit(solution)/shard_map/second_matmul/pallas_call | solution.py:299
  54.2 1.5 %collective-permute-start.12 = (bf16[192,640]{1,0:T(8,128)(2,1)S(1)}, bf16[192,640]{1,0:T(8,128)(2,1)S(1)}, u32[]{:S(2)}, u32[]{:S(2)}) collective-permute-start(bf16[192,640]{1,0:T(8,128)(2,1)S(1)} %get-tuple-element.56), channel_id=1, source_target_pairs={{0,4},{1,5},{2,6},{3,7},{4,0},{5,1},{6,2},{7,3},{8,12},{9,13},{10,... | collective-permute-start | bytes 737288 | tf_op jit(solution)/shard_map/ppermute | solution.py:210
  55.8 1.1 collective-permute-done.16.refs_3_
  56.8 1.1 collective-permute-start.13
  58.0 1.3 %collective-permute-done.17.refs_4_ = bf16[192,512]{1,0:T(8,128)(2,1)S(1)} collective-permute-done((bf16[192,512]{1,0:T(8,128)(2,1)S(1)}, bf16[192,512]{1,0:T(8,128)(2,1)S(1)}, u32[]{:S(2)}, u32[]{:S(2)}) %collective-permute-start.17) | collective-permute-done | bytes 196640 | tf_op jit(solution)/shard_map/ppermute | solution.py:210
  59.2 3.1 %collective-permute-done.18.refs_5_ = bf16[192,512]{1,0:T(8,128)(2,1)S(1)} collective-permute-done((bf16[192,512]{1,0:T(8,128)(2,1)S(1)}, bf16[192,512]{1,0:T(8,128)(2,1)S(1)}, u32[]{:S(2)}, u32[]{:S(2)}) %collective-permute-start.18) | collective-permute-done | bytes 196640 | tf_op jit(solution)/shard_map/ppermute | solution.py:210
  62.7 1.9 %collective-permute-start.20 = (bf16[256,512]{1,0:T(8,128)(2,1)S(1)}, bf16[256,512]{1,0:T(8,128)(2,1)S(1)}, u32[]{:S(2)}, u32[]{:S(2)}) collective-permute-start(bf16[256,512]{1,0:T(8,128)(2,1)S(1)} %combine.5), channel_id=1, source_target_pairs={{0,8},{16,24},{1,9},{17,25},{2,10},{18,26},{3,11},{19,27},{4,12},{... | collective-permute-start | bytes 786440 | tf_op jit(solution)/shard_map/ppermute | solution.py:320
  64.6 1.5 %collective-permute-start.19 = (bf16[256,512]{1,0:T(8,128)(2,1)S(1)}, bf16[256,512]{1,0:T(8,128)(2,1)S(1)}, u32[]{:S(2)}, u32[]{:S(2)}) collective-permute-start(bf16[256,512]{1,0:T(8,128)(2,1)S(1)} %combine.5), channel_id=1, source_target_pairs={{0,24},{8,16},{16,8},{24,0},{1,25},{9,17},{17,9},{25,1},{2,26},{10... | collective-permute-start | bytes 786440 | tf_op jit(solution)/shard_map/ppermute | solution.py:319
  66.1 1.8 %collective-permute-done.12.refs_4_ = bf16[192,640]{1,0:T(8,128)(2,1)S(1)} collective-permute-done((bf16[192,640]{1,0:T(8,128)(2,1)S(1)}, bf16[192,640]{1,0:T(8,128)(2,1)S(1)}, u32[]{:S(2)}, u32[]{:S(2)}) %collective-permute-start.12) | collective-permute-done | bytes 245792 | tf_op jit(solution)/shard_map/ppermute | solution.py:210
  67.9 1.8 %collective-permute-done.13.refs_5_ = bf16[192,640]{1,0:T(8,128)(2,1)S(1)} collective-permute-done((bf16[192,640]{1,0:T(8,128)(2,1)S(1)}, bf16[192,640]{1,0:T(8,128)(2,1)S(1)}, u32[]{:S(2)}, u32[]{:S(2)}) %collective-permute-start.13) | collective-permute-done | bytes 245792 | tf_op jit(solution)/shard_map/ppermute | solution.py:210
  69.7 0.5 combine.4.refs_5_
  70.2 3.2 %collective-permute-start.15 = (bf16[256,640]{1,0:T(8,128)(2,1)S(1)}, bf16[256,640]{1,0:T(8,128)(2,1)S(1)}, u32[]{:S(2)}, u32[]{:S(2)}) collective-permute-start(bf16[256,640]{1,0:T(8,128)(2,1)S(1)} %combine.4.refs_5_), channel_id=1, source_target_pairs={{0,8},{16,24},{1,9},{17,25},{2,10},{18,26},{3,11},{19,27},{4,12},{... | collective-permute-start | bytes 983048 | tf_op jit(solution)/shard_map/ppermute | solution.py:320
  73.4 1.5 %collective-permute-start.14 = (bf16[256,640]{1,0:T(8,128)(2,1)S(1)}, bf16[256,640]{1,0:T(8,128)(2,1)S(1)}, u32[]{:S(2)}, u32[]{:S(2)}) collective-permute-start(bf16[256,640]{1,0:T(8,128)(2,1)S(1)} %combine.4.refs_5_), channel_id=1, source_target_pairs={{0,24},{8,16},{16,8},{24,0},{1,25},{9,17},{17,9},{25,1},{2,26},{10... | collective-permute-start | bytes 983048 | tf_op jit(solution)/shard_map/ppermute | solution.py:319
  74.9 1.0 second_matmul.6
  75.8 0.8 collective-permute-start.21
  76.6 1.5 %collective-permute-start.22 = (bf16[192,512]{1,0:T(8,128)(2,1)S(1)}, bf16[192,512]{1,0:T(8,128)(2,1)S(1)}, u32[]{:S(2)}, u32[]{:S(2)}) collective-permute-start(bf16[192,512]{1,0:T(8,128)(2,1)S(1)} %get-tuple-element.64), channel_id=1, source_target_pairs={{0,4},{1,5},{2,6},{3,7},{4,0},{5,1},{6,2},{7,3},{8,12},{9,13},{10,... | collective-permute-start | bytes 589832 | tf_op jit(solution)/shard_map/ppermute | solution.py:210
  78.1 1.3 %collective-permute-start.23 = (bf16[192,512]{1,0:T(8,128)(2,1)S(1)}, bf16[192,512]{1,0:T(8,128)(2,1)S(1)}, u32[]{:S(2)}, u32[]{:S(2)}) collective-permute-start(bf16[192,512]{1,0:T(8,128)(2,1)S(1)} %get-tuple-element.65), channel_id=1, source_target_pairs={{0,6},{1,7},{2,4},{3,5},{4,2},{5,3},{6,0},{7,1},{8,14},{9,15},{10,... | collective-permute-start | bytes 589832 | tf_op jit(solution)/shard_map/ppermute | solution.py:210
  79.4 3.2 %collective-permute-done.21.refs_3_ = bf16[192,512]{1,0:T(8,128)(2,1)S(1)} collective-permute-done((bf16[192,512]{1,0:T(8,128)(2,1)S(1)}, bf16[192,512]{1,0:T(8,128)(2,1)S(1)}, u32[]{:S(2)}, u32[]{:S(2)}) %collective-permute-start.21) | collective-permute-done | bytes 196640 | tf_op jit(solution)/shard_map/ppermute | solution.py:210
  82.6 2.4 %collective-permute-done.22.refs_4_ = bf16[192,512]{1,0:T(8,128)(2,1)S(1)} collective-permute-done((bf16[192,512]{1,0:T(8,128)(2,1)S(1)}, bf16[192,512]{1,0:T(8,128)(2,1)S(1)}, u32[]{:S(2)}, u32[]{:S(2)}) %collective-permute-start.22) | collective-permute-done | bytes 196640 | tf_op jit(solution)/shard_map/ppermute | solution.py:210
  85.0 0.4 combine.6.refs_5_
  85.4 5.7 %collective-permute-start.28 = (bf16[256,512]{1,0:T(8,128)(2,1)S(1)}, bf16[256,512]{1,0:T(8,128)(2,1)S(1)}, u32[]{:S(2)}, u32[]{:S(2)}) collective-permute-start(bf16[256,512]{1,0:T(8,128)(2,1)S(1)} %combine.6.refs_5_), channel_id=1, source_target_pairs={{0,8},{16,24},{1,9},{17,25},{2,10},{18,26},{3,11},{19,27},{4,12},{... | collective-permute-start | bytes 786440 | tf_op jit(solution)/shard_map/ppermute | solution.py:320
  91.2 1.0 second_matmul.7
  92.2 0.7 collective-permute-start.24
  92.9 1.0 collective-permute-start.25
  93.9 1.9 %collective-permute-start.26 = (bf16[192,384]{1,0:T(8,128)(2,1)S(1)}, bf16[192,384]{1,0:T(8,128)(2,1)S(1)}, u32[]{:S(2)}, u32[]{:S(2)}) collective-permute-start(bf16[192,384]{1,0:T(8,128)(2,1)S(1)} %get-tuple-element.69), channel_id=1, source_target_pairs={{0,6},{1,7},{2,4},{3,5},{4,2},{5,3},{6,0},{7,1},{8,14},{9,15},{10,... | collective-permute-start | bytes 442376 | tf_op jit(solution)/shard_map/ppermute | solution.py:210
  95.7 1.7 %collective-permute-done.24.refs_3_ = bf16[192,384]{1,0:T(8,128)(2,1)S(1)} collective-permute-done((bf16[192,384]{1,0:T(8,128)(2,1)S(1)}, bf16[192,384]{1,0:T(8,128)(2,1)S(1)}, u32[]{:S(2)}, u32[]{:S(2)}) %collective-permute-start.24) | collective-permute-done | bytes 147488 | tf_op jit(solution)/shard_map/ppermute | solution.py:210
  97.4 0.6 collective-permute-done.25.refs_4_
  98.0 1.9 %collective-permute-done.26.refs_5_ = bf16[192,384]{1,0:T(8,128)(2,1)S(1)} collective-permute-done((bf16[192,384]{1,0:T(8,128)(2,1)S(1)}, bf16[192,384]{1,0:T(8,128)(2,1)S(1)}, u32[]{:S(2)}, u32[]{:S(2)}) %collective-permute-start.26) | collective-permute-done | bytes 147488 | tf_op jit(solution)/shard_map/ppermute | solution.py:210
  99.9 0.4 combine.7
  100.3 3.6 %collective-permute-start.30 = (bf16[256,384]{1,0:T(8,128)(2,1)S(1)}, bf16[256,384]{1,0:T(8,128)(2,1)S(1)}, u32[]{:S(2)}, u32[]{:S(2)}) collective-permute-start(bf16[256,384]{1,0:T(8,128)(2,1)S(1)} %combine.7), channel_id=1, source_target_pairs={{0,8},{16,24},{1,9},{17,25},{2,10},{18,26},{3,11},{19,27},{4,12},{... | collective-permute-start | bytes 589832 | tf_op jit(solution)/shard_map/ppermute | solution.py:320
  103.9 1.6 %collective-permute-start.29 = (bf16[256,384]{1,0:T(8,128)(2,1)S(1)}, bf16[256,384]{1,0:T(8,128)(2,1)S(1)}, u32[]{:S(2)}, u32[]{:S(2)}) collective-permute-start(bf16[256,384]{1,0:T(8,128)(2,1)S(1)} %combine.7), channel_id=1, source_target_pairs={{0,24},{8,16},{16,8},{24,0},{1,25},{9,17},{17,9},{25,1},{2,26},{10... | collective-permute-start | bytes 589832 | tf_op jit(solution)/shard_map/ppermute | solution.py:319
  105.5 0.8 place.4
  106.3 0.9 place.5
  107.1 0.8 place.6
  108.0 3.6 %collective-permute-done.29.refs_1_ = bf16[256,384]{1,0:T(8,128)(2,1)S(1)} collective-permute-done((bf16[256,384]{1,0:T(8,128)(2,1)S(1)}, bf16[256,384]{1,0:T(8,128)(2,1)S(1)}, u32[]{:S(2)}, u32[]{:S(2)}) %collective-permute-start.29) | collective-permute-done | bytes 196640 | tf_op jit(solution)/shard_map/ppermute | solution.py:319
  111.5 0.8 place.7
  (34 shorter events, 1.1 us)
Async XLA Ops:
  0.6 31.5 %copy-start.6 = (bf16[1,2048,8]{1,2,0:T(8,128)(2,1)S(1)}, bf16[1,2048,8]{1,2,0:T(8,128)(2,1)}, u32[]{:S(2)}) copy-start(bf16[1,2048,8]{1,2,0:T(8,128)(2,1)} %param.9) | copy-start | bytes 98308
  0.6 30.0 %collective-permute-start.3 = (bf16[2048,1024]{1,0:T(8,128)(2,1)}, bf16[2048,1024]{1,0:T(8,128)(2,1)}, u32[]{:S(2)}, u32[]{:S(2)}) collective-permute-start(bf16[2048,1024]{1,0:T(8,128)(2,1)} %bitcast.20), channel_id=1, source_target_pairs={{0,1},{1,0},{2,3},{3,2},{4,5},{5,4},{6,7},{7,6},{8,9},{9,8},{10,11... | collective-permute-start | bytes 12582920 | tf_op jit(solution)/shard_map/ppermute | solution.py:206
  1.2 31.0 %collective-permute-start.10 = (bf16[1024,2048]{1,0:T(8,128)(2,1)}, bf16[1024,2048]{1,0:T(8,128)(2,1)}, u32[]{:S(2)}, u32[]{:S(2)}) collective-permute-start(bf16[1024,2048]{1,0:T(8,128)(2,1)} %bitcast.15), channel_id=1, source_target_pairs={{0,1},{1,0},{2,3},{3,2},{4,5},{5,4},{6,7},{7,6},{8,9},{9,8},{10,11... | collective-permute-start | bytes 12582920 | tf_op jit(solution)/shard_map/ppermute | solution.py:206
  5.2 12.4 %collective-permute-start.7 = (bf16[192,640]{1,0:T(8,128)(2,1)}, bf16[192,640]{1,0:T(8,128)(2,1)S(1)}, u32[]{:S(2)}, u32[]{:S(2)}) collective-permute-start(bf16[192,640]{1,0:T(8,128)(2,1)} %get-tuple-element.51), channel_id=1, source_target_pairs={{0,2},{1,3},{2,0},{3,1},{4,6},{5,7},{6,4},{7,5},{8,10},{9,11},{10,... | collective-permute-start | bytes 737288 | tf_op jit(solution)/shard_map/ppermute | solution.py:210
  8.2 13.1 %collective-permute-start.8 = (bf16[192,640]{1,0:T(8,128)(2,1)}, bf16[192,640]{1,0:T(8,128)(2,1)S(1)}, u32[]{:S(2)}, u32[]{:S(2)}) collective-permute-start(bf16[192,640]{1,0:T(8,128)(2,1)} %get-tuple-element.52), channel_id=1, source_target_pairs={{0,4},{1,5},{2,6},{3,7},{4,0},{5,1},{6,2},{7,3},{8,12},{9,13},{10,... | collective-permute-start | bytes 737288 | tf_op jit(solution)/shard_map/ppermute | solution.py:210
  9.7 13.1 %collective-permute-start.9 = (bf16[192,640]{1,0:T(8,128)(2,1)}, bf16[192,640]{1,0:T(8,128)(2,1)S(1)}, u32[]{:S(2)}, u32[]{:S(2)}) collective-permute-start(bf16[192,640]{1,0:T(8,128)(2,1)} %get-tuple-element.53), channel_id=1, source_target_pairs={{0,6},{1,7},{2,4},{3,5},{4,2},{5,3},{6,0},{7,1},{8,14},{9,15},{10,... | collective-permute-start | bytes 737288 | tf_op jit(solution)/shard_map/ppermute | solution.py:210
  9.7 1.2 %copy-start.2 = (bf16[1,256,2048]{2,1,0:T(8,128)(2,1)S(1)}, bf16[1,256,2048]{2,1,0:T(8,128)(2,1)}, u32[]{:S(2)}) copy-start(bf16[1,256,2048]{2,1,0:T(8,128)(2,1)} %param.7) | copy-start | bytes 3145732
  10.9 1.2 %copy-start.3 = (bf16[1,256,2048]{2,1,0:T(8,128)(2,1)S(1)}, bf16[1,256,2048]{2,1,0:T(8,128)(2,1)}, u32[]{:S(2)}) copy-start(bf16[1,256,2048]{2,1,0:T(8,128)(2,1)} %param.11) | copy-start | bytes 3145732
  12.1 0.7 copy-start.5
  12.8 0.7 copy-start.7
  17.6 11.1 %collective-permute-start.4 = (bf16[192,896]{1,0:T(8,128)(2,1)S(1)}, bf16[192,896]{1,0:T(8,128)(2,1)S(1)}, u32[]{:S(2)}, u32[]{:S(2)}) collective-permute-start(bf16[192,896]{1,0:T(8,128)(2,1)S(1)} %get-tuple-element.47), channel_id=1, source_target_pairs={{0,2},{1,3},{2,0},{3,1},{4,6},{5,7},{6,4},{7,5},{8,10},{9,11},{10,... | collective-permute-start | bytes 1032200 | tf_op jit(solution)/shard_map/ppermute | solution.py:210
  21.3 21.5 %collective-permute-start.5 = (bf16[192,896]{1,0:T(8,128)(2,1)S(1)}, bf16[192,896]{1,0:T(8,128)(2,1)S(1)}, u32[]{:S(2)}, u32[]{:S(2)}) collective-permute-start(bf16[192,896]{1,0:T(8,128)(2,1)S(1)} %get-tuple-element.48), channel_id=1, source_target_pairs={{0,4},{1,5},{2,6},{3,7},{4,0},{5,1},{6,2},{7,3},{8,12},{9,13},{10,... | collective-permute-start | bytes 1032200 | tf_op jit(solution)/shard_map/ppermute | solution.py:210
  22.8 20.0 %collective-permute-start.6 = (bf16[192,896]{1,0:T(8,128)(2,1)S(1)}, bf16[192,896]{1,0:T(8,128)(2,1)S(1)}, u32[]{:S(2)}, u32[]{:S(2)}) collective-permute-start(bf16[192,896]{1,0:T(8,128)(2,1)S(1)} %get-tuple-element.49), channel_id=1, source_target_pairs={{0,6},{1,7},{2,4},{3,5},{4,2},{5,3},{6,0},{7,1},{8,14},{9,15},{10,... | collective-permute-start | bytes 1032200 | tf_op jit(solution)/shard_map/ppermute | solution.py:210
  28.6 16.0 %collective-permute-start = (bf16[192,512]{1,0:T(8,128)(2,1)S(1)}, bf16[192,512]{1,0:T(8,128)(2,1)S(1)}, u32[]{:S(2)}, u32[]{:S(2)}) collective-permute-start(bf16[192,512]{1,0:T(8,128)(2,1)S(1)} %get-tuple-element.43), channel_id=1, source_target_pairs={{0,2},{1,3},{2,0},{3,1},{4,6},{5,7},{6,4},{7,5},{8,10},{9,11},{10,... | collective-permute-start | bytes 589832 | tf_op jit(solution)/shard_map/ppermute | solution.py:210
  30.6 15.2 %collective-permute-start.1 = (bf16[192,512]{1,0:T(8,128)(2,1)S(1)}, bf16[192,512]{1,0:T(8,128)(2,1)S(1)}, u32[]{:S(2)}, u32[]{:S(2)}) collective-permute-start(bf16[192,512]{1,0:T(8,128)(2,1)S(1)} %get-tuple-element.44), channel_id=1, source_target_pairs={{0,4},{1,5},{2,6},{3,7},{4,0},{5,1},{6,2},{7,3},{8,12},{9,13},{10,... | collective-permute-start | bytes 589832 | tf_op jit(solution)/shard_map/ppermute | solution.py:210
  32.1 13.6 %collective-permute-start.2 = (bf16[192,512]{1,0:T(8,128)(2,1)S(1)}, bf16[192,512]{1,0:T(8,128)(2,1)S(1)}, u32[]{:S(2)}, u32[]{:S(2)}) collective-permute-start(bf16[192,512]{1,0:T(8,128)(2,1)S(1)} %get-tuple-element.45), channel_id=1, source_target_pairs={{0,6},{1,7},{2,4},{3,5},{4,2},{5,3},{6,0},{7,1},{8,14},{9,15},{10,... | collective-permute-start | bytes 589832 | tf_op jit(solution)/shard_map/ppermute | solution.py:210
  36.3 3.5 %copy-start.1 = (bf16[1,1,2048,1024]{3,2,1,0:T(8,128)(2,1)S(1)}, bf16[1,1,2048,1024]{3,2,1,0:T(8,128)(2,1)}, u32[]{:S(2)}) copy-start(bf16[1,1,2048,1024]{3,2,1,0:T(8,128)(2,1)} %param.12) | copy-start | bytes 12582916
  36.3 3.5 %copy-start.4 = (bf16[192,640]{1,0:T(8,128)(2,1)S(1)}, bf16[192,640]{1,0:T(8,128)(2,1)}, u32[]{:S(2)}) copy-start(bf16[192,640]{1,0:T(8,128)(2,1)} %get-tuple-element.50.refs_0_) | copy-start | bytes 737284
  45.8 2.2 %copy-start = (bf16[1,1,1024,2048]{3,2,1,0:T(8,128)(2,1)S(1)}, bf16[1,1,1024,2048]{3,2,1,0:T(8,128)(2,1)}, u32[]{:S(2)}) copy-start(bf16[1,1,1024,2048]{3,2,1,0:T(8,128)(2,1)} %param.13) | copy-start | bytes 12582916
  48.9 7.9 %collective-permute-start.16 = (bf16[192,512]{1,0:T(8,128)(2,1)S(1)}, bf16[192,512]{1,0:T(8,128)(2,1)S(1)}, u32[]{:S(2)}, u32[]{:S(2)}) collective-permute-start(bf16[192,512]{1,0:T(8,128)(2,1)S(1)} %get-tuple-element.59), channel_id=1, source_target_pairs={{0,2},{1,3},{2,0},{3,1},{4,6},{5,7},{6,4},{7,5},{8,10},{9,11},{10,... | collective-permute-start | bytes 589832 | tf_op jit(solution)/shard_map/ppermute | solution.py:210
  49.0 10.2 %collective-permute-start.17 = (bf16[192,512]{1,0:T(8,128)(2,1)S(1)}, bf16[192,512]{1,0:T(8,128)(2,1)S(1)}, u32[]{:S(2)}, u32[]{:S(2)}) collective-permute-start(bf16[192,512]{1,0:T(8,128)(2,1)S(1)} %get-tuple-element.60), channel_id=1, source_target_pairs={{0,4},{1,5},{2,6},{3,7},{4,0},{5,1},{6,2},{7,3},{8,12},{9,13},{10,... | collective-permute-start | bytes 589832 | tf_op jit(solution)/shard_map/ppermute | solution.py:210
  50.8 11.5 %collective-permute-start.18 = (bf16[192,512]{1,0:T(8,128)(2,1)S(1)}, bf16[192,512]{1,0:T(8,128)(2,1)S(1)}, u32[]{:S(2)}, u32[]{:S(2)}) collective-permute-start(bf16[192,512]{1,0:T(8,128)(2,1)S(1)} %get-tuple-element.61), channel_id=1, source_target_pairs={{0,6},{1,7},{2,4},{3,5},{4,2},{5,3},{6,0},{7,1},{8,14},{9,15},{10,... | collective-permute-start | bytes 589832 | tf_op jit(solution)/shard_map/ppermute | solution.py:210
  53.9 12.2 %collective-permute-start.11 = (bf16[192,640]{1,0:T(8,128)(2,1)S(1)}, bf16[192,640]{1,0:T(8,128)(2,1)S(1)}, u32[]{:S(2)}, u32[]{:S(2)}) collective-permute-start(bf16[192,640]{1,0:T(8,128)(2,1)S(1)} %get-tuple-element.55), channel_id=1, source_target_pairs={{0,2},{1,3},{2,0},{3,1},{4,6},{5,7},{6,4},{7,5},{8,10},{9,11},{10,... | collective-permute-start | bytes 737288 | tf_op jit(solution)/shard_map/ppermute | solution.py:210
  54.2 13.7 %collective-permute-start.12 = (bf16[192,640]{1,0:T(8,128)(2,1)S(1)}, bf16[192,640]{1,0:T(8,128)(2,1)S(1)}, u32[]{:S(2)}, u32[]{:S(2)}) collective-permute-start(bf16[192,640]{1,0:T(8,128)(2,1)S(1)} %get-tuple-element.56), channel_id=1, source_target_pairs={{0,4},{1,5},{2,6},{3,7},{4,0},{5,1},{6,2},{7,3},{8,12},{9,13},{10,... | collective-permute-start | bytes 737288 | tf_op jit(solution)/shard_map/ppermute | solution.py:210
  56.8 12.9 %collective-permute-start.13 = (bf16[192,640]{1,0:T(8,128)(2,1)S(1)}, bf16[192,640]{1,0:T(8,128)(2,1)S(1)}, u32[]{:S(2)}, u32[]{:S(2)}) collective-permute-start(bf16[192,640]{1,0:T(8,128)(2,1)S(1)} %get-tuple-element.57), channel_id=1, source_target_pairs={{0,6},{1,7},{2,4},{3,5},{4,2},{5,3},{6,0},{7,1},{8,14},{9,15},{10,... | collective-permute-start | bytes 737288 | tf_op jit(solution)/shard_map/ppermute | solution.py:210
  62.7 12.1 %collective-permute-start.20 = (bf16[256,512]{1,0:T(8,128)(2,1)S(1)}, bf16[256,512]{1,0:T(8,128)(2,1)S(1)}, u32[]{:S(2)}, u32[]{:S(2)}) collective-permute-start(bf16[256,512]{1,0:T(8,128)(2,1)S(1)} %combine.5), channel_id=1, source_target_pairs={{0,8},{16,24},{1,9},{17,25},{2,10},{18,26},{3,11},{19,27},{4,12},{... | collective-permute-start | bytes 786440 | tf_op jit(solution)/shard_map/ppermute | solution.py:320
  64.6 10.3 %collective-permute-start.19 = (bf16[256,512]{1,0:T(8,128)(2,1)S(1)}, bf16[256,512]{1,0:T(8,128)(2,1)S(1)}, u32[]{:S(2)}, u32[]{:S(2)}) collective-permute-start(bf16[256,512]{1,0:T(8,128)(2,1)S(1)} %combine.5), channel_id=1, source_target_pairs={{0,24},{8,16},{16,8},{24,0},{1,25},{9,17},{17,9},{25,1},{2,26},{10... | collective-permute-start | bytes 786440 | tf_op jit(solution)/shard_map/ppermute | solution.py:319
  70.2 21.0 %collective-permute-start.15 = (bf16[256,640]{1,0:T(8,128)(2,1)S(1)}, bf16[256,640]{1,0:T(8,128)(2,1)S(1)}, u32[]{:S(2)}, u32[]{:S(2)}) collective-permute-start(bf16[256,640]{1,0:T(8,128)(2,1)S(1)} %combine.4.refs_5_), channel_id=1, source_target_pairs={{0,8},{16,24},{1,9},{17,25},{2,10},{18,26},{3,11},{19,27},{4,12},{... | collective-permute-start | bytes 983048 | tf_op jit(solution)/shard_map/ppermute | solution.py:320
  73.4 17.8 %collective-permute-start.14 = (bf16[256,640]{1,0:T(8,128)(2,1)S(1)}, bf16[256,640]{1,0:T(8,128)(2,1)S(1)}, u32[]{:S(2)}, u32[]{:S(2)}) collective-permute-start(bf16[256,640]{1,0:T(8,128)(2,1)S(1)} %combine.4.refs_5_), channel_id=1, source_target_pairs={{0,24},{8,16},{16,8},{24,0},{1,25},{9,17},{17,9},{25,1},{2,26},{10... | collective-permute-start | bytes 983048 | tf_op jit(solution)/shard_map/ppermute | solution.py:319
  75.8 6.7 %collective-permute-start.21 = (bf16[192,512]{1,0:T(8,128)(2,1)S(1)}, bf16[192,512]{1,0:T(8,128)(2,1)S(1)}, u32[]{:S(2)}, u32[]{:S(2)}) collective-permute-start(bf16[192,512]{1,0:T(8,128)(2,1)S(1)} %get-tuple-element.63), channel_id=1, source_target_pairs={{0,2},{1,3},{2,0},{3,1},{4,6},{5,7},{6,4},{7,5},{8,10},{9,11},{10,... | collective-permute-start | bytes 589832 | tf_op jit(solution)/shard_map/ppermute | solution.py:210
  76.6 8.4 %collective-permute-start.22 = (bf16[192,512]{1,0:T(8,128)(2,1)S(1)}, bf16[192,512]{1,0:T(8,128)(2,1)S(1)}, u32[]{:S(2)}, u32[]{:S(2)}) collective-permute-start(bf16[192,512]{1,0:T(8,128)(2,1)S(1)} %get-tuple-element.64), channel_id=1, source_target_pairs={{0,4},{1,5},{2,6},{3,7},{4,0},{5,1},{6,2},{7,3},{8,12},{9,13},{10,... | collective-permute-start | bytes 589832 | tf_op jit(solution)/shard_map/ppermute | solution.py:210
  78.1 6.9 %collective-permute-start.23 = (bf16[192,512]{1,0:T(8,128)(2,1)S(1)}, bf16[192,512]{1,0:T(8,128)(2,1)S(1)}, u32[]{:S(2)}, u32[]{:S(2)}) collective-permute-start(bf16[192,512]{1,0:T(8,128)(2,1)S(1)} %get-tuple-element.65), channel_id=1, source_target_pairs={{0,6},{1,7},{2,4},{3,5},{4,2},{5,3},{6,0},{7,1},{8,14},{9,15},{10,... | collective-permute-start | bytes 589832 | tf_op jit(solution)/shard_map/ppermute | solution.py:210
  85.4 14.5 %collective-permute-start.28 = (bf16[256,512]{1,0:T(8,128)(2,1)S(1)}, bf16[256,512]{1,0:T(8,128)(2,1)S(1)}, u32[]{:S(2)}, u32[]{:S(2)}) collective-permute-start(bf16[256,512]{1,0:T(8,128)(2,1)S(1)} %combine.6.refs_5_), channel_id=1, source_target_pairs={{0,8},{16,24},{1,9},{17,25},{2,10},{18,26},{3,11},{19,27},{4,12},{... | collective-permute-start | bytes 786440 | tf_op jit(solution)/shard_map/ppermute | solution.py:320
  91.1 8.8 %collective-permute-start.27 = (bf16[256,512]{1,0:T(8,128)(2,1)S(1)}, bf16[256,512]{1,0:T(8,128)(2,1)S(1)}, u32[]{:S(2)}, u32[]{:S(2)}) collective-permute-start(bf16[256,512]{1,0:T(8,128)(2,1)S(1)} %combine.6.refs_5_), channel_id=1, source_target_pairs={{0,24},{8,16},{16,8},{24,0},{1,25},{9,17},{17,9},{25,1},{2,26},{10... | collective-permute-start | bytes 786440 | tf_op jit(solution)/shard_map/ppermute | solution.py:319
  92.2 5.2 %collective-permute-start.24 = (bf16[192,384]{1,0:T(8,128)(2,1)S(1)}, bf16[192,384]{1,0:T(8,128)(2,1)S(1)}, u32[]{:S(2)}, u32[]{:S(2)}) collective-permute-start(bf16[192,384]{1,0:T(8,128)(2,1)S(1)} %get-tuple-element.67), channel_id=1, source_target_pairs={{0,2},{1,3},{2,0},{3,1},{4,6},{5,7},{6,4},{7,5},{8,10},{9,11},{10,... | collective-permute-start | bytes 442376 | tf_op jit(solution)/shard_map/ppermute | solution.py:210
  92.9 5.1 %collective-permute-start.25 = (bf16[192,384]{1,0:T(8,128)(2,1)S(1)}, bf16[192,384]{1,0:T(8,128)(2,1)S(1)}, u32[]{:S(2)}, u32[]{:S(2)}) collective-permute-start(bf16[192,384]{1,0:T(8,128)(2,1)S(1)} %get-tuple-element.68), channel_id=1, source_target_pairs={{0,4},{1,5},{2,6},{3,7},{4,0},{5,1},{6,2},{7,3},{8,12},{9,13},{10,... | collective-permute-start | bytes 442376 | tf_op jit(solution)/shard_map/ppermute | solution.py:210
  93.9 6.0 %collective-permute-start.26 = (bf16[192,384]{1,0:T(8,128)(2,1)S(1)}, bf16[192,384]{1,0:T(8,128)(2,1)S(1)}, u32[]{:S(2)}, u32[]{:S(2)}) collective-permute-start(bf16[192,384]{1,0:T(8,128)(2,1)S(1)} %get-tuple-element.69), channel_id=1, source_target_pairs={{0,6},{1,7},{2,4},{3,5},{4,2},{5,3},{6,0},{7,1},{8,14},{9,15},{10,... | collective-permute-start | bytes 442376 | tf_op jit(solution)/shard_map/ppermute | solution.py:210
  100.3 7.7 %collective-permute-start.30 = (bf16[256,384]{1,0:T(8,128)(2,1)S(1)}, bf16[256,384]{1,0:T(8,128)(2,1)S(1)}, u32[]{:S(2)}, u32[]{:S(2)}) collective-permute-start(bf16[256,384]{1,0:T(8,128)(2,1)S(1)} %combine.7), channel_id=1, source_target_pairs={{0,8},{16,24},{1,9},{17,25},{2,10},{18,26},{3,11},{19,27},{4,12},{... | collective-permute-start | bytes 589832 | tf_op jit(solution)/shard_map/ppermute | solution.py:320
  103.9 7.6 %collective-permute-start.29 = (bf16[256,384]{1,0:T(8,128)(2,1)S(1)}, bf16[256,384]{1,0:T(8,128)(2,1)S(1)}, u32[]{:S(2)}, u32[]{:S(2)}) collective-permute-start(bf16[256,384]{1,0:T(8,128)(2,1)S(1)} %combine.7), channel_id=1, source_target_pairs={{0,24},{8,16},{16,8},{24,0},{1,25},{9,17},{17,9},{25,1},{2,26},{10... | collective-permute-start | bytes 589832 | tf_op jit(solution)/shard_map/ppermute | solution.py:319

commit v5 on v4

--- a/solution.py
+++ b/solution.py
@@ -12,7 +12,7 @@
 BF16 = jnp.bfloat16
 F32 = jnp.float32
 IN_PARTS = (5, 7, 4)
-OUT_PARTS = (4, 5, 4, 3)
+OUT_PARTS = (5, 7, 4)
 
 
 def cut(width, parts):
@@ -305,16 +305,15 @@
             name="second_matmul",
         )(hidden, second, other_second, *after)
         back = exchange(worked)
-        later = gone[c - 1] if c == len(outgoing) - 1 else []
         y = pl.pallas_call(
             lambda *refs, ends=ends: combine_kernel(chips, ends, *refs),
             out_shape=jax.ShapeDtypeStruct((tokens, ends[1] - ends[0]), BF16),
-            in_specs=[VMEM] * (chips + 2) + [ANY] * len(later),
+            in_specs=[VMEM] * (chips + 2),
             out_specs=VMEM,
             scratch_shapes=[pltpu.VMEM((rows, ends[1] - ends[0]), BF16)],
             compiler_params=params(16),
             name="combine",
-        )(h_rows, mix, *back, *later)
+        )(h_rows, mix, *back)
         made.append(y)
         across = lax.ppermute(y, "section", mirror)
         ahead = lax.ppermute(y, "section", onward) if onward else across

time: 113 us -> 111 us (0.982)
  starting transfers between devices: 44.8 us -> 34 us
  waiting for transfers between devices: 32.8 us -> 42.3 us
    ppermute x4 -> x3, starting transfers between devices: 14.3 us -> 8.7 us  [local(): ahead = lax.ppermute(y, 'section', onward) if onward else across]
    ppermute x4 -> x3, waiting for transfers between devices: 0.01 us -> 4.59 us  [local(): ahead = lax.ppermute(y, 'section', onward) if onward else across]
    ppermute x4 -> x3, waiting for transfers between devices: 3.58 us -> 7.23 us  [local(): across = lax.ppermute(y, 'section', mirror)]
    ppermute x21 -> x18, starting transfers between devices: 25.3 us -> 21.7 us  [exchange(): lax.ppermute(blocks[k], 'expert', [(i, i ^ 2 * k) for i in range(devices)])]
    ppermute x4 -> x3, starting transfers between devices: 4.55 us -> 3.01 us  [local(): across = lax.ppermute(y, 'section', mirror)]
    ppermute x21 -> x18, waiting for transfers between devices: 29.2 us -> 30.5 us  [exchange(): lax.ppermute(blocks[k], 'expert', [(i, i ^ 2 * k) for i in range(devices)])]
    pallas_call x4 -> x3, Pallas kernels: 3.23 us -> 2.59 us  [local(): pl.pallas_call(lambda *refs, ends=ends: place_kernel(ends, *refs), out_sh...]
    pallas_call x4 -> x3, Pallas kernels: 4.31 us -> 4.14 us  [local(): pl.pallas_call(lambda *refs, ends=ends: second_kernel(chips, slots, ends,...]
  transfers between devices with their start and end apart: 31 -> 26, of which waited for: 15 -> 15; matrix products, arithmetic and copies ran while one was open for 0% -> 0% of each run, Pallas kernels for 22% -> 21%
where the time goes in v5:
time: 111 us; the launch traced here: 110 us
  waiting for transfers between devices  42.3 us (38%)
  starting transfers between devices  34 us (31%)
  Pallas kernels  27.4 us (25%)
  local copies, waits for them, and re-layouts  5.44 us (5%)
    ppermute x18, waiting for transfers between devices, exchange(): lax.ppermute(blocks[k], 'expert', [(i, i ^ 2 * k) for i in range(devices)])  30.5 us
    ppermute x18, starting transfers between devices, exchange(): lax.ppermute(blocks[k], 'expert', [(i, i ^ 2 * k) for i in range(devices)])  21.7 us
    ppermute x3, starting transfers between devices, local(): ahead = lax.ppermute(y, 'section', onward) if onward else across  8.7 us
    pallas_call x2, Pallas kernels, dispatch(): pl.pallas_call(lambda *refs: dispatch_kernel(experts, slots, pieces, colu...  7.98 us
    ppermute x3, waiting for transfers between devices, local(): across = lax.ppermute(y, 'section', mirror)  7.23 us
    unnamed x16, local copies, waits for them, and re-layouts  5.44 us
    pallas_call x3, Pallas kernels, local(): pl.pallas_call(lambda *refs, c=c, ends=ends, last=last: first_kernel(chip...  4.86 us
    ppermute x3, waiting for transfers between devices, local(): ahead = lax.ppermute(y, 'section', onward) if onward else across  4.59 us
  transfers between devices with their start and end apart: 26, of which 15 were waited for; matrix products, arithmetic and copies ran while one was open for 0% of the time, Pallas kernels for 21%

profile of v5, /device:TPU:0, one launch (start us, length us, event | category | flops | bytes accessed | tf_op | source)
XLA Modules:
  0.0 110.1 jit_solution(15344088886364080334)
XLA Ops:
  0.6 0.5 collective-permute-start.3
  1.2 0.1 collective-permute-start.10
  1.2 3.9 %dispatch.3 = (bf16[192,640]{1,0:T(8,128)(2,1)}, bf16[192,640]{1,0:T(8,128)(2,1)}, bf16[192,640]{1,0:T(8,128)(2,1)}, bf16[192,640]{1,0:T(8,128)(2,1)}) custom-call(s32[1]{0:T(128)} %bitcast.1.refs_0_, s32[1]{0:T(128)} %bitcast.2.refs_1_, s32[2,256]{1,0:T(2,128)} %bitcast.30, f32[1,2048]{1,0:T(1,128)} %refs_3_.5, bf16[256,2048]{1,0:T(8,128)(2,1)} %bitcast.23, ...), custom_call_target="tpu_custom_call" | custom-call | tf_op jit(solution)/shard_map/dispatch/pallas_call | solution.py:222
  5.2 3.0 %collective-permute-start.7 = (bf16[192,640]{1,0:T(8,128)(2,1)}, bf16[192,640]{1,0:T(8,128)(2,1)S(1)}, u32[]{:S(2)}, u32[]{:S(2)}) collective-permute-start(bf16[192,640]{1,0:T(8,128)(2,1)} %get-tuple-element.45), channel_id=1, source_target_pairs={{0,2},{1,3},{2,0},{3,1},{4,6},{5,7},{6,4},{7,5},{8,10},{9,11},{10,... | collective-permute-start | bytes 737288 | tf_op jit(solution)/shard_map/ppermute | solution.py:210
  8.2 1.5 %collective-permute-start.8 = (bf16[192,640]{1,0:T(8,128)(2,1)}, bf16[192,640]{1,0:T(8,128)(2,1)S(1)}, u32[]{:S(2)}, u32[]{:S(2)}) collective-permute-start(bf16[192,640]{1,0:T(8,128)(2,1)} %get-tuple-element.46), channel_id=1, source_target_pairs={{0,4},{1,5},{2,6},{3,7},{4,0},{5,1},{6,2},{7,3},{8,12},{9,13},{10,... | collective-permute-start | bytes 737288 | tf_op jit(solution)/shard_map/ppermute | solution.py:210
  9.7 0.0 collective-permute-start.9
  9.7 1.2 %copy-done.2 = bf16[1,256,2048]{2,1,0:T(8,128)(2,1)S(1)} copy-done((bf16[1,256,2048]{2,1,0:T(8,128)(2,1)S(1)}, bf16[1,256,2048]{2,1,0:T(8,128)(2,1)}, u32[]{:S(2)}) %copy-start.2) | copy-done | bytes 1048600
  10.9 1.2 %copy-done.3 = bf16[1,256,2048]{2,1,0:T(8,128)(2,1)S(1)} copy-done((bf16[1,256,2048]{2,1,0:T(8,128)(2,1)S(1)}, bf16[1,256,2048]{2,1,0:T(8,128)(2,1)}, u32[]{:S(2)}) %copy-start.3) | copy-done | bytes 1048600
  12.2 0.7 copy-done.5
  12.9 0.7 copy-done.7
  13.5 4.0 %dispatch.2 = (bf16[192,896]{1,0:T(8,128)(2,1)S(1)}, bf16[192,896]{1,0:T(8,128)(2,1)S(1)}, bf16[192,896]{1,0:T(8,128)(2,1)S(1)}, bf16[192,896]{1,0:T(8,128)(2,1)...) custom-call(s32[1]{0:T(128)} %bitcast.1.refs_0_, ...), custom_call_target="tpu_custom_call" | custom-call | tf_op jit(solution)/shard_map/dispatch/pallas_call | solution.py:222
  17.6 2.0 %collective-permute-start.4 = (bf16[192,896]{1,0:T(8,128)(2,1)S(1)}, bf16[192,896]{1,0:T(8,128)(2,1)S(1)}, u32[]{:S(2)}, u32[]{:S(2)}) collective-permute-start(bf16[192,896]{1,0:T(8,128)(2,1)S(1)} %get-tuple-element.41), channel_id=1, source_target_pairs={{0,2},{1,3},{2,0},{3,1},{4,6},{5,7},{6,4},{7,5},{8,10},{9,11},{10,... | collective-permute-start | bytes 1032200 | tf_op jit(solution)/shard_map/ppermute | solution.py:210
  19.6 1.7 %collective-permute-done.8.refs_2_ = bf16[192,640]{1,0:T(8,128)(2,1)S(1)} collective-permute-done((bf16[192,640]{1,0:T(8,128)(2,1)}, bf16[192,640]{1,0:T(8,128)(2,1)S(1)}, u32[]{:S(2)}, u32[]{:S(2)}) %collective-permute-start.8) | collective-permute-done | bytes 245792 | tf_op jit(solution)/shard_map/ppermute | solution.py:210
  21.3 1.5 %collective-permute-start.5 = (bf16[192,896]{1,0:T(8,128)(2,1)S(1)}, bf16[192,896]{1,0:T(8,128)(2,1)S(1)}, u32[]{:S(2)}, u32[]{:S(2)}) collective-permute-start(bf16[192,896]{1,0:T(8,128)(2,1)S(1)} %get-tuple-element.42), channel_id=1, source_target_pairs={{0,4},{1,5},{2,6},{3,7},{4,0},{5,1},{6,2},{7,3},{8,12},{9,13},{10,... | collective-permute-start | bytes 1032200 | tf_op jit(solution)/shard_map/ppermute | solution.py:210
  22.8 0.0 collective-permute-start.6
  22.9 5.8 %collective-permute-done.4.refs_1_ = bf16[192,896]{1,0:T(8,128)(2,1)S(1)} collective-permute-done((bf16[192,896]{1,0:T(8,128)(2,1)S(1)}, bf16[192,896]{1,0:T(8,128)(2,1)S(1)}, u32[]{:S(2)}, u32[]{:S(2)}) %collective-permute-start.4) | collective-permute-done | bytes 344096 | tf_op jit(solution)/shard_map/ppermute | solution.py:210
  28.7 1.9 %collective-permute-start = (bf16[192,512]{1,0:T(8,128)(2,1)S(1)}, bf16[192,512]{1,0:T(8,128)(2,1)S(1)}, u32[]{:S(2)}, u32[]{:S(2)}) collective-permute-start(bf16[192,512]{1,0:T(8,128)(2,1)S(1)} %get-tuple-element.37), channel_id=1, source_target_pairs={{0,2},{1,3},{2,0},{3,1},{4,6},{5,7},{6,4},{7,5},{8,10},{9,11},{10,... | collective-permute-start | bytes 589832 | tf_op jit(solution)/shard_map/ppermute | solution.py:210
  30.6 1.5 %collective-permute-start.1 = (bf16[192,512]{1,0:T(8,128)(2,1)S(1)}, bf16[192,512]{1,0:T(8,128)(2,1)S(1)}, u32[]{:S(2)}, u32[]{:S(2)}) collective-permute-start(bf16[192,512]{1,0:T(8,128)(2,1)S(1)} %get-tuple-element.38), channel_id=1, source_target_pairs={{0,4},{1,5},{2,6},{3,7},{4,0},{5,1},{6,2},{7,3},{8,12},{9,13},{10,... | collective-permute-start | bytes 589832 | tf_op jit(solution)/shard_map/ppermute | solution.py:210
  32.1 0.0 collective-permute-start.2
  32.2 1.9 %gates.1 = (bf16[256,768]{1,0:T(8,128)(2,1)S(1)}, f32[256,2048]{1,0:T(8,128)S(1)}) custom-call(s32[1]{0:T(128)} %bitcast.1.refs_0_, s32[1]{0:T(128)} %bitcast.2.refs_1_, s32[2,256]{1,0:T(2,128)S(1)} %bitcast.32, f32[1,2048]{1,0:T(1,128)S(1)} %copy-done.5, bf16[256,2048]{1,0:T(8,128)(2,1)S(1)} %bitcast.25, bf16[256,2048]{1,0:T(8,128)(2,1)S(1)} %bitcast.28, ...), custom_call_target="tpu_custom_call" | custom-call | tf_op jit(solution)/shard_map/gates/pallas_call | solution.py:260
  34.1 2.2 %hold.2.refs_5_ = bf16[2048,1024]{1,0:T(8,128)(2,1)S(1)} custom-call(bf16[2048,1024]{1,0:T(8,128)(2,1)} %collective-permute-done.3.source), custom_call_target="tpu_custom_call" | custom-call | tf_op jit(solution)/shard_map/hold/pallas_call | solution.py:247
  36.3 2.3 %hold.3.refs_7_.refs_2_ = bf16[1024,2048]{1,0:T(8,128)(2,1)S(1)} custom-call(bf16[1024,2048]{1,0:T(8,128)(2,1)} %collective-permute-done.10.source), custom_call_target="tpu_custom_call" | custom-call | tf_op jit(solution)/shard_map/hold/pallas_call | solution.py:247
  38.7 1.1 copy-done
  39.8 1.4 %first_matmul.3.refs_6_ = f32[768,1024]{1,0:T(8,128)S(1)} custom-call(bf16[192,640]{1,0:T(8,128)(2,1)S(1)} %copy-done.4, bf16[192,640]{1,0:T(8,128)(2,1)S(1)} %collective-permute-done.7.refs_1_, bf16[192,640]{1,0:T(8,128)(2,1)S(1)} %collective-permute-done.8.refs_2_, bf16[192,640]{1,0:T(8,128)(2,1)S(1)} %collective-permute-done.9.refs_3_, ...), custom_call_target="tpu_custom_call" | custom-call | tf_op jit(solution)/shard_map/first_matmul/pallas_call | solution.py:276
  41.2 1.6 %collective-permute-done.5.refs_2_ = bf16[192,896]{1,0:T(8,128)(2,1)S(1)} collective-permute-done((bf16[192,896]{1,0:T(8,128)(2,1)S(1)}, bf16[192,896]{1,0:T(8,128)(2,1)S(1)}, u32[]{:S(2)}, u32[]{:S(2)}) %collective-permute-start.5) | collective-permute-done | bytes 344096 | tf_op jit(solution)/shard_map/ppermute | solution.py:210
  42.8 1.8 %first_matmul.4.refs_6_ = f32[768,1024]{1,0:T(8,128)S(1)} custom-call(bf16[192,896]{1,0:T(8,128)(2,1)S(1)} %get-tuple-element.40.refs_0_, bf16[192,896]{1,0:T(8,128)(2,1)S(1)} %collective-permute-done.4.refs_1_, bf16[192,896]{1,0:T(8,128)(2,1)S(1)} %collective-permute-done.5.refs_2_, bf16[192,896]{1,0:T(8,128)(2,1)S(1)} %collective-permute-done.6.refs_3_, ...), custom_call_target="tpu_custom_call" | custom-call | tf_op jit(solution)/shard_map/first_matmul/pallas_call | solution.py:276
  44.6 1.2 %collective-permute-done.1.refs_2_ = bf16[192,512]{1,0:T(8,128)(2,1)S(1)} collective-permute-done((bf16[192,512]{1,0:T(8,128)(2,1)S(1)}, bf16[192,512]{1,0:T(8,128)(2,1)S(1)}, u32[]{:S(2)}, u32[]{:S(2)}) %collective-permute-start.1) | collective-permute-done | bytes 196640 | tf_op jit(solution)/shard_map/ppermute | solution.py:210
  45.8 1.7 %first_matmul.5.refs_0_ = bf16[768,1024]{1,0:T(8,128)(2,1)S(1)} custom-call(bf16[192,512]{1,0:T(8,128)(2,1)S(1)} %get-tuple-element.36.refs_0_, bf16[192,512]{1,0:T(8,128)(2,1)S(1)} %collective-permute-done.refs_1_, bf16[192,512]{1,0:T(8,128)(2,1)S(1)} %collective-permute-done.1.refs_2_, bf16[192,512]{1,0:T(8,128)(2,1)S(1)} %collective-permute-done.2.refs_3_, ...), custom_call_target="tpu_custom_call" | custom-call | tf_op jit(solution)/shard_map/first_matmul/pallas_call | solution.py:276
  47.4 0.5 copy-done.1
  48.0 1.4 %second_matmul.3 = (bf16[192,640]{1,0:T(8,128)(2,1)S(1)}, bf16[192,640]{1,0:T(8,128)(2,1)S(1)}, bf16[192,640]{1,0:T(8,128)(2,1)S(1)}, bf16[192,640]{1,0:T(8,128)(2,1)S(1)}) custom-call(bf16[768,1024]{1,0:T(8,128)(2,1)S(1)} %first_matmul.5.refs_0_, bf16[1024,2048]{1,0:T(8,128)(2,1)S(1)} %bitcast.20, bf16[1024,2048]{1,0:T(8,128)(2,1)S(1)} %hold.3.refs_7_.refs_2_), custom_call_target="tpu_custom_call" | custom-call | tf_op jit(solution)/shard_map/second_matmul/pallas_call | solution.py:299
  49.3 0.1 collective-permute-start.11
  49.4 1.8 %collective-permute-start.12 = (bf16[192,640]{1,0:T(8,128)(2,1)S(1)}, bf16[192,640]{1,0:T(8,128)(2,1)S(1)}, u32[]{:S(2)}, u32[]{:S(2)}) collective-permute-start(bf16[192,640]{1,0:T(8,128)(2,1)S(1)} %get-tuple-element.50), channel_id=1, source_target_pairs={{0,4},{1,5},{2,6},{3,7},{4,0},{5,1},{6,2},{7,3},{8,12},{9,13},{10,... | collective-permute-start | bytes 737288 | tf_op jit(solution)/shard_map/ppermute | solution.py:210
  51.2 1.7 %collective-permute-start.13 = (bf16[192,640]{1,0:T(8,128)(2,1)S(1)}, bf16[192,640]{1,0:T(8,128)(2,1)S(1)}, u32[]{:S(2)}, u32[]{:S(2)}) collective-permute-start(bf16[192,640]{1,0:T(8,128)(2,1)S(1)} %get-tuple-element.51), channel_id=1, source_target_pairs={{0,6},{1,7},{2,4},{3,5},{4,2},{5,3},{6,0},{7,1},{8,14},{9,15},{10,... | collective-permute-start | bytes 737288 | tf_op jit(solution)/shard_map/ppermute | solution.py:210
  52.9 1.8 %second_matmul.4 = (bf16[192,896]{1,0:T(8,128)(2,1)S(1)}, bf16[192,896]{1,0:T(8,128)(2,1)S(1)}, bf16[192,896]{1,0:T(8,128)(2,1)S(1)}, bf16[192,896]{1,0:T(8,128)(2,1)S(1)}) custom-call(bf16[768,1024]{1,0:T(8,128)(2,1)S(1)} %first_matmul.5.refs_0_, bf16[1024,2048]{1,0:T(8,128)(2,1)S(1)} %bitcast.21, bf16[1024,2048]{1,0:T(8,128)(2,1)S(1)} %hold.3.refs_7_.refs_2_), custom_call_target="tpu_custom_call" | custom-call | tf_op jit(solution)/shard_map/second_matmul/pallas_call | solution.py:299
  54.7 0.3 collective-permute-start.16
  55.0 1.5 %collective-permute-start.17 = (bf16[192,896]{1,0:T(8,128)(2,1)S(1)}, bf16[192,896]{1,0:T(8,128)(2,1)S(1)}, u32[]{:S(2)}, u32[]{:S(2)}) collective-permute-start(bf16[192,896]{1,0:T(8,128)(2,1)S(1)} %get-tuple-element.54), channel_id=1, source_target_pairs={{0,4},{1,5},{2,6},{3,7},{4,0},{5,1},{6,2},{7,3},{8,12},{9,13},{10,... | collective-permute-start | bytes 1032200 | tf_op jit(solution)/shard_map/ppermute | solution.py:210
  56.6 1.7 %collective-permute-done.11.refs_3_ = bf16[192,640]{1,0:T(8,128)(2,1)S(1)} collective-permute-done((bf16[192,640]{1,0:T(8,128)(2,1)S(1)}, bf16[192,640]{1,0:T(8,128)(2,1)S(1)}, u32[]{:S(2)}, u32[]{:S(2)}) %collective-permute-start.11) | collective-permute-done | bytes 245792 | tf_op jit(solution)/shard_map/ppermute | solution.py:210
  58.3 1.1 %collective-permute-start.18 = (bf16[192,896]{1,0:T(8,128)(2,1)S(1)}, bf16[192,896]{1,0:T(8,128)(2,1)S(1)}, u32[]{:S(2)}, u32[]{:S(2)}) collective-permute-start(bf16[192,896]{1,0:T(8,128)(2,1)S(1)} %get-tuple-element.55), channel_id=1, source_target_pairs={{0,6},{1,7},{2,4},{3,5},{4,2},{5,3},{6,0},{7,1},{8,14},{9,15},{10,... | collective-permute-start | bytes 1032200 | tf_op jit(solution)/shard_map/ppermute | solution.py:210
  59.4 0.8 collective-permute-done.12.refs_4_
  60.2 4.6 %collective-permute-done.13.refs_5_ = bf16[192,640]{1,0:T(8,128)(2,1)S(1)} collective-permute-done((bf16[192,640]{1,0:T(8,128)(2,1)S(1)}, bf16[192,640]{1,0:T(8,128)(2,1)S(1)}, u32[]{:S(2)}, u32[]{:S(2)}) %collective-permute-start.13) | collective-permute-done | bytes 245792 | tf_op jit(solution)/shard_map/ppermute | solution.py:210
  64.8 0.5 combine.3
  65.2 2.0 %collective-permute-start.15 = (bf16[256,640]{1,0:T(8,128)(2,1)S(1)}, bf16[256,640]{1,0:T(8,128)(2,1)S(1)}, u32[]{:S(2)}, u32[]{:S(2)}) collective-permute-start(bf16[256,640]{1,0:T(8,128)(2,1)S(1)} %combine.3), channel_id=1, source_target_pairs={{0,8},{16,24},{1,9},{17,25},{2,10},{18,26},{3,11},{19,27},{4,12},{... | collective-permute-start | bytes 983048 | tf_op jit(solution)/shard_map/ppermute | solution.py:319
  67.3 1.5 %collective-permute-start.14 = (bf16[256,640]{1,0:T(8,128)(2,1)S(1)}, bf16[256,640]{1,0:T(8,128)(2,1)S(1)}, u32[]{:S(2)}, u32[]{:S(2)}) collective-permute-start(bf16[256,640]{1,0:T(8,128)(2,1)S(1)} %combine.3), channel_id=1, source_target_pairs={{0,24},{8,16},{16,8},{24,0},{1,25},{9,17},{17,9},{25,1},{2,26},{10... | collective-permute-start | bytes 983048 | tf_op jit(solution)/shard_map/ppermute | solution.py:318
  68.7 2.0 %collective-permute-done.16.refs_3_ = bf16[192,896]{1,0:T(8,128)(2,1)S(1)} collective-permute-done((bf16[192,896]{1,0:T(8,128)(2,1)S(1)}, bf16[192,896]{1,0:T(8,128)(2,1)S(1)}, u32[]{:S(2)}, u32[]{:S(2)}) %collective-permute-start.16) | collective-permute-done | bytes 344096 | tf_op jit(solution)/shard_map/ppermute | solution.py:210
  70.8 3.9 %collective-permute-done.17.refs_4_ = bf16[192,896]{1,0:T(8,128)(2,1)S(1)} collective-permute-done((bf16[192,896]{1,0:T(8,128)(2,1)S(1)}, bf16[192,896]{1,0:T(8,128)(2,1)S(1)}, u32[]{:S(2)}, u32[]{:S(2)}) %collective-permute-start.17) | collective-permute-done | bytes 344096 | tf_op jit(solution)/shard_map/ppermute | solution.py:210
  74.6 1.8 %collective-permute-done.18.refs_5_ = bf16[192,896]{1,0:T(8,128)(2,1)S(1)} collective-permute-done((bf16[192,896]{1,0:T(8,128)(2,1)S(1)}, bf16[192,896]{1,0:T(8,128)(2,1)S(1)}, u32[]{:S(2)}, u32[]{:S(2)}) %collective-permute-start.18) | collective-permute-done | bytes 344096 | tf_op jit(solution)/shard_map/ppermute | solution.py:210
  76.5 0.6 combine.4.refs_5_
  77.1 3.1 %collective-permute-start.25 = (bf16[256,896]{1,0:T(8,128)(2,1)S(1)}, bf16[256,896]{1,0:T(8,128)(2,1)S(1)}, u32[]{:S(2)}, u32[]{:S(2)}) collective-permute-start(bf16[256,896]{1,0:T(8,128)(2,1)S(1)} %combine.4.refs_5_), channel_id=1, source_target_pairs={{0,8},{16,24},{1,9},{17,25},{2,10},{18,26},{3,11},{19,27},{4,12},{... | collective-permute-start | bytes 1376264 | tf_op jit(solution)/shard_map/ppermute | solution.py:319
  80.2 1.4 %collective-permute-start.24 = (bf16[256,896]{1,0:T(8,128)(2,1)S(1)}, bf16[256,896]{1,0:T(8,128)(2,1)S(1)}, u32[]{:S(2)}, u32[]{:S(2)}) collective-permute-start(bf16[256,896]{1,0:T(8,128)(2,1)S(1)} %combine.4.refs_5_), channel_id=1, source_target_pairs={{0,24},{8,16},{16,8},{24,0},{1,25},{9,17},{17,9},{25,1},{2,26},{10... | collective-permute-start | bytes 1376264 | tf_op jit(solution)/shard_map/ppermute | solution.py:318
  81.6 1.0 second_matmul.5
  82.6 0.6 collective-permute-start.19
  83.2 1.7 %collective-permute-start.20 = (bf16[192,512]{1,0:T(8,128)(2,1)S(1)}, bf16[192,512]{1,0:T(8,128)(2,1)S(1)}, u32[]{:S(2)}, u32[]{:S(2)}) collective-permute-start(bf16[192,512]{1,0:T(8,128)(2,1)S(1)} %get-tuple-element.58), channel_id=1, source_target_pairs={{0,4},{1,5},{2,6},{3,7},{4,0},{5,1},{6,2},{7,3},{8,12},{9,13},{10,... | collective-permute-start | bytes 589832 | tf_op jit(solution)/shard_map/ppermute | solution.py:210
  84.9 1.2 %collective-permute-start.21 = (bf16[192,512]{1,0:T(8,128)(2,1)S(1)}, bf16[192,512]{1,0:T(8,128)(2,1)S(1)}, u32[]{:S(2)}, u32[]{:S(2)}) collective-permute-start(bf16[192,512]{1,0:T(8,128)(2,1)S(1)} %get-tuple-element.59), channel_id=1, source_target_pairs={{0,6},{1,7},{2,4},{3,5},{4,2},{5,3},{6,0},{7,1},{8,14},{9,15},{10,... | collective-permute-start | bytes 589832 | tf_op jit(solution)/shard_map/ppermute | solution.py:210
  86.1 3.3 %collective-permute-done.19.refs_3_ = bf16[192,512]{1,0:T(8,128)(2,1)S(1)} collective-permute-done((bf16[192,512]{1,0:T(8,128)(2,1)S(1)}, bf16[192,512]{1,0:T(8,128)(2,1)S(1)}, u32[]{:S(2)}, u32[]{:S(2)}) %collective-permute-start.19) | collective-permute-done | bytes 196640 | tf_op jit(solution)/shard_map/ppermute | solution.py:210
  89.4 2.2 %collective-permute-done.20.refs_4_ = bf16[192,512]{1,0:T(8,128)(2,1)S(1)} collective-permute-done((bf16[192,512]{1,0:T(8,128)(2,1)S(1)}, bf16[192,512]{1,0:T(8,128)(2,1)S(1)}, u32[]{:S(2)}, u32[]{:S(2)}) %collective-permute-start.20) | collective-permute-done | bytes 196640 | tf_op jit(solution)/shard_map/ppermute | solution.py:210
  91.6 0.4 combine.5
  92.0 3.6 %collective-permute-start.23 = (bf16[256,512]{1,0:T(8,128)(2,1)S(1)}, bf16[256,512]{1,0:T(8,128)(2,1)S(1)}, u32[]{:S(2)}, u32[]{:S(2)}) collective-permute-start(bf16[256,512]{1,0:T(8,128)(2,1)S(1)} %combine.5), channel_id=1, source_target_pairs={{0,8},{16,24},{1,9},{17,25},{2,10},{18,26},{3,11},{19,27},{4,12},{... | collective-permute-start | bytes 786440 | tf_op jit(solution)/shard_map/ppermute | solution.py:319
  95.6 0.1 collective-permute-start.22
  95.7 0.8 place.3
  96.5 4.4 %collective-permute-done.24.refs_1_ = bf16[256,896]{1,0:T(8,128)(2,1)S(1)} collective-permute-done((bf16[256,896]{1,0:T(8,128)(2,1)S(1)}, bf16[256,896]{1,0:T(8,128)(2,1)S(1)}, u32[]{:S(2)}, u32[]{:S(2)}) %collective-permute-start.24) | collective-permute-done | bytes 458784 | tf_op jit(solution)/shard_map/ppermute | solution.py:318
  101.0 0.9 place.4
  101.9 4.6 %collective-permute-done.23.refs_2_ = bf16[256,512]{1,0:T(8,128)(2,1)S(1)} collective-permute-done((bf16[256,512]{1,0:T(8,128)(2,1)S(1)}, bf16[256,512]{1,0:T(8,128)(2,1)S(1)}, u32[]{:S(2)}, u32[]{:S(2)}) %collective-permute-start.23) | collective-permute-done | bytes 262176 | tf_op jit(solution)/shard_map/ppermute | solution.py:319
  106.5 2.8 %collective-permute-done.22.refs_1_ = bf16[256,512]{1,0:T(8,128)(2,1)S(1)} collective-permute-done((bf16[256,512]{1,0:T(8,128)(2,1)S(1)}, bf16[256,512]{1,0:T(8,128)(2,1)S(1)}, u32[]{:S(2)}, u32[]{:S(2)}) %collective-permute-start.22) | collective-permute-done | bytes 262176 | tf_op jit(solution)/shard_map/ppermute | solution.py:318
  109.3 0.8 place.5
  (21 shorter events, 0.1 us)
Async XLA Ops:
  0.6 31.5 %copy-start.6 = (bf16[1,2048,8]{1,2,0:T(8,128)(2,1)S(1)}, bf16[1,2048,8]{1,2,0:T(8,128)(2,1)}, u32[]{:S(2)}) copy-start(bf16[1,2048,8]{1,2,0:T(8,128)(2,1)} %param.9) | copy-start | bytes 98308
  0.6 30.0 %collective-permute-start.3 = (bf16[2048,1024]{1,0:T(8,128)(2,1)}, bf16[2048,1024]{1,0:T(8,128)(2,1)}, u32[]{:S(2)}, u32[]{:S(2)}) collective-permute-start(bf16[2048,1024]{1,0:T(8,128)(2,1)} %bitcast.15), channel_id=1, source_target_pairs={{0,1},{1,0},{2,3},{3,2},{4,5},{5,4},{6,7},{7,6},{8,9},{9,8},{10,11... | collective-permute-start | bytes 12582920 | tf_op jit(solution)/shard_map/ppermute | solution.py:206
  1.2 31.0 %collective-permute-start.10 = (bf16[1024,2048]{1,0:T(8,128)(2,1)}, bf16[1024,2048]{1,0:T(8,128)(2,1)}, u32[]{:S(2)}, u32[]{:S(2)}) collective-permute-start(bf16[1024,2048]{1,0:T(8,128)(2,1)} %bitcast.19), channel_id=1, source_target_pairs={{0,1},{1,0},{2,3},{3,2},{4,5},{5,4},{6,7},{7,6},{8,9},{9,8},{10,11... | collective-permute-start | bytes 12582920 | tf_op jit(solution)/shard_map/ppermute | solution.py:206
  5.2 12.4 %collective-permute-start.7 = (bf16[192,640]{1,0:T(8,128)(2,1)}, bf16[192,640]{1,0:T(8,128)(2,1)S(1)}, u32[]{:S(2)}, u32[]{:S(2)}) collective-permute-start(bf16[192,640]{1,0:T(8,128)(2,1)} %get-tuple-element.45), channel_id=1, source_target_pairs={{0,2},{1,3},{2,0},{3,1},{4,6},{5,7},{6,4},{7,5},{8,10},{9,11},{10,... | collective-permute-start | bytes 737288 | tf_op jit(solution)/shard_map/ppermute | solution.py:210
  8.2 13.1 %collective-permute-start.8 = (bf16[192,640]{1,0:T(8,128)(2,1)}, bf16[192,640]{1,0:T(8,128)(2,1)S(1)}, u32[]{:S(2)}, u32[]{:S(2)}) collective-permute-start(bf16[192,640]{1,0:T(8,128)(2,1)} %get-tuple-element.46), channel_id=1, source_target_pairs={{0,4},{1,5},{2,6},{3,7},{4,0},{5,1},{6,2},{7,3},{8,12},{9,13},{10,... | collective-permute-start | bytes 737288 | tf_op jit(solution)/shard_map/ppermute | solution.py:210
  9.7 13.1 %collective-permute-start.9 = (bf16[192,640]{1,0:T(8,128)(2,1)}, bf16[192,640]{1,0:T(8,128)(2,1)S(1)}, u32[]{:S(2)}, u32[]{:S(2)}) collective-permute-start(bf16[192,640]{1,0:T(8,128)(2,1)} %get-tuple-element.47), channel_id=1, source_target_pairs={{0,6},{1,7},{2,4},{3,5},{4,2},{5,3},{6,0},{7,1},{8,14},{9,15},{10,... | collective-permute-start | bytes 737288 | tf_op jit(solution)/shard_map/ppermute | solution.py:210
  9.7 1.2 %copy-start.2 = (bf16[1,256,2048]{2,1,0:T(8,128)(2,1)S(1)}, bf16[1,256,2048]{2,1,0:T(8,128)(2,1)}, u32[]{:S(2)}) copy-start(bf16[1,256,2048]{2,1,0:T(8,128)(2,1)} %param.7) | copy-start | bytes 3145732
  10.9 1.2 %copy-start.3 = (bf16[1,256,2048]{2,1,0:T(8,128)(2,1)S(1)}, bf16[1,256,2048]{2,1,0:T(8,128)(2,1)}, u32[]{:S(2)}) copy-start(bf16[1,256,2048]{2,1,0:T(8,128)(2,1)} %param.11) | copy-start | bytes 3145732
  12.2 0.7 copy-start.5
  12.9 0.7 copy-start.7
  17.6 11.1 %collective-permute-start.4 = (bf16[192,896]{1,0:T(8,128)(2,1)S(1)}, bf16[192,896]{1,0:T(8,128)(2,1)S(1)}, u32[]{:S(2)}, u32[]{:S(2)}) collective-permute-start(bf16[192,896]{1,0:T(8,128)(2,1)S(1)} %get-tuple-element.41), channel_id=1, source_target_pairs={{0,2},{1,3},{2,0},{3,1},{4,6},{5,7},{6,4},{7,5},{8,10},{9,11},{10,... | collective-permute-start | bytes 1032200 | tf_op jit(solution)/shard_map/ppermute | solution.py:210
  21.3 21.5 %collective-permute-start.5 = (bf16[192,896]{1,0:T(8,128)(2,1)S(1)}, bf16[192,896]{1,0:T(8,128)(2,1)S(1)}, u32[]{:S(2)}, u32[]{:S(2)}) collective-permute-start(bf16[192,896]{1,0:T(8,128)(2,1)S(1)} %get-tuple-element.42), channel_id=1, source_target_pairs={{0,4},{1,5},{2,6},{3,7},{4,0},{5,1},{6,2},{7,3},{8,12},{9,13},{10,... | collective-permute-start | bytes 1032200 | tf_op jit(solution)/shard_map/ppermute | solution.py:210
  22.8 20.0 %collective-permute-start.6 = (bf16[192,896]{1,0:T(8,128)(2,1)S(1)}, bf16[192,896]{1,0:T(8,128)(2,1)S(1)}, u32[]{:S(2)}, u32[]{:S(2)}) collective-permute-start(bf16[192,896]{1,0:T(8,128)(2,1)S(1)} %get-tuple-element.43), channel_id=1, source_target_pairs={{0,6},{1,7},{2,4},{3,5},{4,2},{5,3},{6,0},{7,1},{8,14},{9,15},{10,... | collective-permute-start | bytes 1032200 | tf_op jit(solution)/shard_map/ppermute | solution.py:210
  28.7 15.9 %collective-permute-start = (bf16[192,512]{1,0:T(8,128)(2,1)S(1)}, bf16[192,512]{1,0:T(8,128)(2,1)S(1)}, u32[]{:S(2)}, u32[]{:S(2)}) collective-permute-start(bf16[192,512]{1,0:T(8,128)(2,1)S(1)} %get-tuple-element.37), channel_id=1, source_target_pairs={{0,2},{1,3},{2,0},{3,1},{4,6},{5,7},{6,4},{7,5},{8,10},{9,11},{10,... | collective-permute-start | bytes 589832 | tf_op jit(solution)/shard_map/ppermute | solution.py:210
  30.6 15.2 %collective-permute-start.1 = (bf16[192,512]{1,0:T(8,128)(2,1)S(1)}, bf16[192,512]{1,0:T(8,128)(2,1)S(1)}, u32[]{:S(2)}, u32[]{:S(2)}) collective-permute-start(bf16[192,512]{1,0:T(8,128)(2,1)S(1)} %get-tuple-element.38), channel_id=1, source_target_pairs={{0,4},{1,5},{2,6},{3,7},{4,0},{5,1},{6,2},{7,3},{8,12},{9,13},{10,... | collective-permute-start | bytes 589832 | tf_op jit(solution)/shard_map/ppermute | solution.py:210
  32.1 13.6 %collective-permute-start.2 = (bf16[192,512]{1,0:T(8,128)(2,1)S(1)}, bf16[192,512]{1,0:T(8,128)(2,1)S(1)}, u32[]{:S(2)}, u32[]{:S(2)}) collective-permute-start(bf16[192,512]{1,0:T(8,128)(2,1)S(1)} %get-tuple-element.39), channel_id=1, source_target_pairs={{0,6},{1,7},{2,4},{3,5},{4,2},{5,3},{6,0},{7,1},{8,14},{9,15},{10,... | collective-permute-start | bytes 589832 | tf_op jit(solution)/shard_map/ppermute | solution.py:210
  36.3 3.5 %copy-start = (bf16[1,1,2048,1024]{3,2,1,0:T(8,128)(2,1)S(1)}, bf16[1,1,2048,1024]{3,2,1,0:T(8,128)(2,1)}, u32[]{:S(2)}) copy-start(bf16[1,1,2048,1024]{3,2,1,0:T(8,128)(2,1)} %param.12) | copy-start | bytes 12582916
  36.3 3.5 %copy-start.4 = (bf16[192,640]{1,0:T(8,128)(2,1)S(1)}, bf16[192,640]{1,0:T(8,128)(2,1)}, u32[]{:S(2)}) copy-start(bf16[192,640]{1,0:T(8,128)(2,1)} %get-tuple-element.44.refs_0_) | copy-start | bytes 737284
  45.8 2.2 %copy-start.1 = (bf16[1,1,1024,2048]{3,2,1,0:T(8,128)(2,1)S(1)}, bf16[1,1,1024,2048]{3,2,1,0:T(8,128)(2,1)}, u32[]{:S(2)}) copy-start(bf16[1,1,1024,2048]{3,2,1,0:T(8,128)(2,1)} %param.13) | copy-start | bytes 12582916
  49.3 9.0 %collective-permute-start.11 = (bf16[192,640]{1,0:T(8,128)(2,1)S(1)}, bf16[192,640]{1,0:T(8,128)(2,1)S(1)}, u32[]{:S(2)}, u32[]{:S(2)}) collective-permute-start(bf16[192,640]{1,0:T(8,128)(2,1)S(1)} %get-tuple-element.49), channel_id=1, source_target_pairs={{0,2},{1,3},{2,0},{3,1},{4,6},{5,7},{6,4},{7,5},{8,10},{9,11},{10,... | collective-permute-start | bytes 737288 | tf_op jit(solution)/shard_map/ppermute | solution.py:210
  49.4 10.8 %collective-permute-start.12 = (bf16[192,640]{1,0:T(8,128)(2,1)S(1)}, bf16[192,640]{1,0:T(8,128)(2,1)S(1)}, u32[]{:S(2)}, u32[]{:S(2)}) collective-permute-start(bf16[192,640]{1,0:T(8,128)(2,1)S(1)} %get-tuple-element.50), channel_id=1, source_target_pairs={{0,4},{1,5},{2,6},{3,7},{4,0},{5,1},{6,2},{7,3},{8,12},{9,13},{10,... | collective-permute-start | bytes 737288 | tf_op jit(solution)/shard_map/ppermute | solution.py:210
  51.2 13.5 %collective-permute-start.13 = (bf16[192,640]{1,0:T(8,128)(2,1)S(1)}, bf16[192,640]{1,0:T(8,128)(2,1)S(1)}, u32[]{:S(2)}, u32[]{:S(2)}) collective-permute-start(bf16[192,640]{1,0:T(8,128)(2,1)S(1)} %get-tuple-element.51), channel_id=1, source_target_pairs={{0,6},{1,7},{2,4},{3,5},{4,2},{5,3},{6,0},{7,1},{8,14},{9,15},{10,... | collective-permute-start | bytes 737288 | tf_op jit(solution)/shard_map/ppermute | solution.py:210
  54.7 16.1 %collective-permute-start.16 = (bf16[192,896]{1,0:T(8,128)(2,1)S(1)}, bf16[192,896]{1,0:T(8,128)(2,1)S(1)}, u32[]{:S(2)}, u32[]{:S(2)}) collective-permute-start(bf16[192,896]{1,0:T(8,128)(2,1)S(1)} %get-tuple-element.53), channel_id=1, source_target_pairs={{0,2},{1,3},{2,0},{3,1},{4,6},{5,7},{6,4},{7,5},{8,10},{9,11},{10,... | collective-permute-start | bytes 1032200 | tf_op jit(solution)/shard_map/ppermute | solution.py:210
  55.0 19.6 %collective-permute-start.17 = (bf16[192,896]{1,0:T(8,128)(2,1)S(1)}, bf16[192,896]{1,0:T(8,128)(2,1)S(1)}, u32[]{:S(2)}, u32[]{:S(2)}) collective-permute-start(bf16[192,896]{1,0:T(8,128)(2,1)S(1)} %get-tuple-element.54), channel_id=1, source_target_pairs={{0,4},{1,5},{2,6},{3,7},{4,0},{5,1},{6,2},{7,3},{8,12},{9,13},{10,... | collective-permute-start | bytes 1032200 | tf_op jit(solution)/shard_map/ppermute | solution.py:210
  58.3 18.2 %collective-permute-start.18 = (bf16[192,896]{1,0:T(8,128)(2,1)S(1)}, bf16[192,896]{1,0:T(8,128)(2,1)S(1)}, u32[]{:S(2)}, u32[]{:S(2)}) collective-permute-start(bf16[192,896]{1,0:T(8,128)(2,1)S(1)} %get-tuple-element.55), channel_id=1, source_target_pairs={{0,6},{1,7},{2,4},{3,5},{4,2},{5,3},{6,0},{7,1},{8,14},{9,15},{10,... | collective-permute-start | bytes 1032200 | tf_op jit(solution)/shard_map/ppermute | solution.py:210
  65.2 16.4 %collective-permute-start.15 = (bf16[256,640]{1,0:T(8,128)(2,1)S(1)}, bf16[256,640]{1,0:T(8,128)(2,1)S(1)}, u32[]{:S(2)}, u32[]{:S(2)}) collective-permute-start(bf16[256,640]{1,0:T(8,128)(2,1)S(1)} %combine.3), channel_id=1, source_target_pairs={{0,8},{16,24},{1,9},{17,25},{2,10},{18,26},{3,11},{19,27},{4,12},{... | collective-permute-start | bytes 983048 | tf_op jit(solution)/shard_map/ppermute | solution.py:319
  67.3 14.3 %collective-permute-start.14 = (bf16[256,640]{1,0:T(8,128)(2,1)S(1)}, bf16[256,640]{1,0:T(8,128)(2,1)S(1)}, u32[]{:S(2)}, u32[]{:S(2)}) collective-permute-start(bf16[256,640]{1,0:T(8,128)(2,1)S(1)} %combine.3), channel_id=1, source_target_pairs={{0,24},{8,16},{16,8},{24,0},{1,25},{9,17},{17,9},{25,1},{2,26},{10... | collective-permute-start | bytes 983048 | tf_op jit(solution)/shard_map/ppermute | solution.py:318
  77.1 19.5 %collective-permute-start.25 = (bf16[256,896]{1,0:T(8,128)(2,1)S(1)}, bf16[256,896]{1,0:T(8,128)(2,1)S(1)}, u32[]{:S(2)}, u32[]{:S(2)}) collective-permute-start(bf16[256,896]{1,0:T(8,128)(2,1)S(1)} %combine.4.refs_5_), channel_id=1, source_target_pairs={{0,8},{16,24},{1,9},{17,25},{2,10},{18,26},{3,11},{19,27},{4,12},{... | collective-permute-start | bytes 1376264 | tf_op jit(solution)/shard_map/ppermute | solution.py:319
  80.2 20.8 %collective-permute-start.24 = (bf16[256,896]{1,0:T(8,128)(2,1)S(1)}, bf16[256,896]{1,0:T(8,128)(2,1)S(1)}, u32[]{:S(2)}, u32[]{:S(2)}) collective-permute-start(bf16[256,896]{1,0:T(8,128)(2,1)S(1)} %combine.4.refs_5_), channel_id=1, source_target_pairs={{0,24},{8,16},{16,8},{24,0},{1,25},{9,17},{17,9},{25,1},{2,26},{10... | collective-permute-start | bytes 1376264 | tf_op jit(solution)/shard_map/ppermute | solution.py:318
  82.6 6.8 %collective-permute-start.19 = (bf16[192,512]{1,0:T(8,128)(2,1)S(1)}, bf16[192,512]{1,0:T(8,128)(2,1)S(1)}, u32[]{:S(2)}, u32[]{:S(2)}) collective-permute-start(bf16[192,512]{1,0:T(8,128)(2,1)S(1)} %get-tuple-element.57), channel_id=1, source_target_pairs={{0,2},{1,3},{2,0},{3,1},{4,6},{5,7},{6,4},{7,5},{8,10},{9,11},{10,... | collective-permute-start | bytes 589832 | tf_op jit(solution)/shard_map/ppermute | solution.py:210
  83.2 8.4 %collective-permute-start.20 = (bf16[192,512]{1,0:T(8,128)(2,1)S(1)}, bf16[192,512]{1,0:T(8,128)(2,1)S(1)}, u32[]{:S(2)}, u32[]{:S(2)}) collective-permute-start(bf16[192,512]{1,0:T(8,128)(2,1)S(1)} %get-tuple-element.58), channel_id=1, source_target_pairs={{0,4},{1,5},{2,6},{3,7},{4,0},{5,1},{6,2},{7,3},{8,12},{9,13},{10,... | collective-permute-start | bytes 589832 | tf_op jit(solution)/shard_map/ppermute | solution.py:210
  84.9 6.7 %collective-permute-start.21 = (bf16[192,512]{1,0:T(8,128)(2,1)S(1)}, bf16[192,512]{1,0:T(8,128)(2,1)S(1)}, u32[]{:S(2)}, u32[]{:S(2)}) collective-permute-start(bf16[192,512]{1,0:T(8,128)(2,1)S(1)} %get-tuple-element.59), channel_id=1, source_target_pairs={{0,6},{1,7},{2,4},{3,5},{4,2},{5,3},{6,0},{7,1},{8,14},{9,15},{10,... | collective-permute-start | bytes 589832 | tf_op jit(solution)/shard_map/ppermute | solution.py:210
  92.0 14.5 %collective-permute-start.23 = (bf16[256,512]{1,0:T(8,128)(2,1)S(1)}, bf16[256,512]{1,0:T(8,128)(2,1)S(1)}, u32[]{:S(2)}, u32[]{:S(2)}) collective-permute-start(bf16[256,512]{1,0:T(8,128)(2,1)S(1)} %combine.5), channel_id=1, source_target_pairs={{0,8},{16,24},{1,9},{17,25},{2,10},{18,26},{3,11},{19,27},{4,12},{... | collective-permute-start | bytes 786440 | tf_op jit(solution)/shard_map/ppermute | solution.py:319
  95.6 13.7 %collective-permute-start.22 = (bf16[256,512]{1,0:T(8,128)(2,1)S(1)}, bf16[256,512]{1,0:T(8,128)(2,1)S(1)}, u32[]{:S(2)}, u32[]{:S(2)}) collective-permute-start(bf16[256,512]{1,0:T(8,128)(2,1)S(1)} %combine.5), channel_id=1, source_target_pairs={{0,24},{8,16},{16,8},{24,0},{1,25},{9,17},{17,9},{25,1},{2,26},{10... | collective-permute-start | bytes 786440 | tf_op jit(solution)/shard_map/ppermute | solution.py:318

commit v6 on v5

--- a/solution.py
+++ b/solution.py
@@ -11,7 +11,7 @@
 ANY = pl.BlockSpec(memory_space=pl.ANY)
 BF16 = jnp.bfloat16
 F32 = jnp.float32
-IN_PARTS = (5, 7, 4)
+IN_PARTS = (6, 8, 2)
 OUT_PARTS = (5, 7, 4)
 
 
@@ -143,6 +143,13 @@
             out_ref[part, j : j + tile] = jax.nn.gelu(total, approximate=True).astype(BF16) if last else total
 
 
+def bridge_kernel(chips, slots, incoming, outgoing, tile, *refs):
+    blocks, first_refs, second_refs = refs[:chips], refs[chips : chips + 3], refs[chips + 3 : chips + 5]
+    hidden_ref, out_refs, held = refs[-chips - 2], refs[-chips - 1 : -1], refs[-1]
+    first_kernel(chips, slots, incoming, tile, False, True, *blocks, *first_refs, hidden_ref, held)
+    second_kernel(chips, slots, outgoing, hidden_ref, *second_refs, *out_refs)
+
+
 def second_kernel(chips, slots, columns, hidden_ref, own_ref, other_ref, *refs):
     size = chips * slots
     out_refs = refs[-chips:]
@@ -273,18 +280,28 @@
     for c, ends in enumerate(incoming):
         arrived = exchange(sent[c * chips : (c + 1) * chips])
         last = c == len(incoming) - 1
+        tile = min(512, hidden_width)
+        held = pltpu.VMEM((2, chips * slots, ends[1] - ends[0]), BF16)
+        if last:
+            hidden, *early = pl.pallas_call(
+                lambda *refs, ends=ends: bridge_kernel(chips, slots, ends, outgoing[0], tile, *refs),
+                out_shape=[jax.ShapeDtypeStruct((rows, hidden_width), BF16)] + sendable(outgoing[0]),
+                in_specs=[VMEM] * (chips + 5),
+                out_specs=[VMEM] * (chips + 1),
+                scratch_shapes=[held],
+                compiler_params=params(16),
+                name="bridge",
+            )(*arrived, first, other_first, total, second, other_second)
+            continue
         total = pl.pallas_call(
-            lambda *refs, c=c, ends=ends, last=last: first_kernel(
-                chips, slots, ends, min(512, hidden_width), c == 0, last, *refs
-            ),
-            out_shape=jax.ShapeDtypeStruct((rows, hidden_width), BF16 if last else F32),
+            lambda *refs, c=c, ends=ends: first_kernel(chips, slots, ends, tile, c == 0, False, *refs),
+            out_shape=jax.ShapeDtypeStruct((rows, hidden_width), F32),
             in_specs=[VMEM] * (chips + 2) + [ANY if c == 0 else VMEM, ANY],
             out_specs=VMEM,
-            scratch_shapes=[pltpu.VMEM((2, chips * slots, ends[1] - ends[0]), BF16)],
+            scratch_shapes=[held],
             compiler_params=params(16),
             name="first_matmul",
         )(*arrived, first, other_first, total, mix if c == 0 else other_second)
-    hidden = total
 
     mirror = [(s, sections - 1 - s) for s in range(sections)]
     same = [s for s in range(sections) if (s - 1) % sections == sections - 1 - s]
@@ -296,7 +313,7 @@
     made, gone, placed = [], [], []
     for c, ends in enumerate(outgoing):
         after = gone[c - 2] + [made[c - 1]] if c >= 2 else []
-        worked = pl.pallas_call(
+        worked = early if c == 0 else pl.pallas_call(
             lambda *refs, ends=ends: second_kernel(chips, slots, ends, *refs),
             out_shape=sendable(ends),
             in_specs=[VMEM] * 3 + [ANY] * len(after),

time: 111 us -> 110 us (level); the launches traced: 110 us -> 108 us
  waiting for transfers between devices: 42.3 us -> 36.6 us
  starting transfers between devices: 34 us -> 38.4 us
    ppermute x18, waiting for transfers between devices: 30.5 us -> 26.7 us  [exchange(): lax.ppermute(blocks[k], 'expert', [(i, i ^ 2 * k) for i in range(devices)])]
    ppermute x18, starting transfers between devices: 21.7 us -> 24.8 us  [exchange(): lax.ppermute(blocks[k], 'expert', [(i, i ^ 2 * k) for i in range(devices)])]
    ppermute x3, waiting for transfers between devices: 4.59 us -> 2.88 us  [local(): ahead = lax.ppermute(y, 'section', onward) if onward else across]
    pallas_call x3 -> x2, Pallas kernels: 4.14 us -> 2.76 us  [local(): pl.pallas_call(lambda *refs, ends=ends: second_kernel(chips, slots, ends,...]
    ppermute x3, starting transfers between devices: 8.7 us -> 9.99 us  [local(): ahead = lax.ppermute(y, 'section', onward) if onward else across]
  transfers between devices with their start and end apart: 26 -> 26, of which waited for: 15 -> 14; matrix products, arithmetic and copies ran while one was open for 0% -> 0% of each run, Pallas kernels for 21% -> 22%
where the time goes in v6:
time: 110 us; the launch traced here: 108 us
  starting transfers between devices  38.4 us (35%)
  waiting for transfers between devices  36.6 us (33%)
  Pallas kernels  26.7 us (24%)
  local copies, waits for them, and re-layouts  5.3 us (5%)
    ppermute x18, waiting for transfers between devices, exchange(): lax.ppermute(blocks[k], 'expert', [(i, i ^ 2 * k) for i in range(devices)])  26.7 us
    ppermute x18, starting transfers between devices, exchange(): lax.ppermute(blocks[k], 'expert', [(i, i ^ 2 * k) for i in range(devices)])  24.8 us
    ppermute x3, starting transfers between devices, local(): ahead = lax.ppermute(y, 'section', onward) if onward else across  9.99 us
    pallas_call x2, Pallas kernels, dispatch(): pl.pallas_call(lambda *refs: dispatch_kernel(experts, slots, pieces, colu...  7.8 us
    ppermute x3, waiting for transfers between devices, local(): across = lax.ppermute(y, 'section', mirror)  6.99 us
    unnamed x16, local copies, waits for them, and re-layouts  5.3 us
    pallas_call x2, Pallas kernels, hold(): pl.pallas_call(hold_kernel, out_shape=jax.ShapeDtypeStruct(block.shape, b...  4.54 us
    pallas_call x2, Pallas kernels, local(): pl.pallas_call(lambda *refs, c=c, ends=ends: first_kernel(chips, slots, e...  3.17 us
  transfers between devices with their start and end apart: 26, of which 14 were waited for; matrix products, arithmetic and copies ran while one was open for 0% of the time, Pallas kernels for 22%

profile of v6, /device:TPU:0, one launch (start us, length us, event | category | flops | bytes accessed | tf_op | source)
XLA Modules:
  0.0 107.9 jit_solution(5806980681961059254)
XLA Ops:
  0.6 0.5 collective-permute-start.3
  1.2 0.1 collective-permute-start.10
  1.2 4.0 %dispatch.3 = (bf16[192,768]{1,0:T(8,128)(2,1)}, bf16[192,768]{1,0:T(8,128)(2,1)}, bf16[192,768]{1,0:T(8,128)(2,1)}, bf16[192,768]{1,0:T(8,128)(2,1)}) custom-call(s32[1]{0:T(128)} %bitcast.1.refs_0_, s32[1]{0:T(128)} %bitcast.2.refs_1_, s32[2,256]{1,0:T(2,128)} %bitcast.30, f32[1,2048]{1,0:T(1,128)} %refs_3_.5, bf16[256,2048]{1,0:T(8,128)(2,1)} %bitcast.23, ...), custom_call_target="tpu_custom_call" | custom-call | tf_op jit(solution)/shard_map/dispatch/pallas_call | solution.py:229
  5.2 3.0 %collective-permute-start.7 = (bf16[192,768]{1,0:T(8,128)(2,1)}, bf16[192,768]{1,0:T(8,128)(2,1)S(1)}, u32[]{:S(2)}, u32[]{:S(2)}) collective-permute-start(bf16[192,768]{1,0:T(8,128)(2,1)} %get-tuple-element.46), channel_id=1, source_target_pairs={{0,2},{1,3},{2,0},{3,1},{4,6},{5,7},{6,4},{7,5},{8,10},{9,11},{10,... | collective-permute-start | bytes 884744 | tf_op jit(solution)/shard_map/ppermute | solution.py:217
  8.2 1.5 %collective-permute-start.8 = (bf16[192,768]{1,0:T(8,128)(2,1)}, bf16[192,768]{1,0:T(8,128)(2,1)S(1)}, u32[]{:S(2)}, u32[]{:S(2)}) collective-permute-start(bf16[192,768]{1,0:T(8,128)(2,1)} %get-tuple-element.47), channel_id=1, source_target_pairs={{0,4},{1,5},{2,6},{3,7},{4,0},{5,1},{6,2},{7,3},{8,12},{9,13},{10,... | collective-permute-start | bytes 884744 | tf_op jit(solution)/shard_map/ppermute | solution.py:217
  9.7 0.0 collective-permute-start.9
  9.8 1.2 %copy-done.2 = bf16[1,256,2048]{2,1,0:T(8,128)(2,1)S(1)} copy-done((bf16[1,256,2048]{2,1,0:T(8,128)(2,1)S(1)}, bf16[1,256,2048]{2,1,0:T(8,128)(2,1)}, u32[]{:S(2)}) %copy-start.2) | copy-done | bytes 1048600
  11.0 1.2 %copy-done.3 = bf16[1,256,2048]{2,1,0:T(8,128)(2,1)S(1)} copy-done((bf16[1,256,2048]{2,1,0:T(8,128)(2,1)S(1)}, bf16[1,256,2048]{2,1,0:T(8,128)(2,1)}, u32[]{:S(2)}) %copy-start.3) | copy-done | bytes 1048600
  12.2 0.7 copy-done.5
  12.9 0.7 copy-done.7
  13.6 3.8 %dispatch.2 = (bf16[192,1024]{1,0:T(8,128)(2,1)S(1)}, bf16[192,1024]{1,0:T(8,128)(2,1)S(1)}, bf16[192,1024]{1,0:T(8,128)(2,1)S(1)}, bf16[192,1024]{1,0:T(8,128)(...) custom-call(s32[1]{0:T(128)} %bitcast.1.refs_0_, ...), custom_call_target="tpu_custom_call" | custom-call | tf_op jit(solution)/shard_map/dispatch/pallas_call | solution.py:229
  17.4 2.0 %collective-permute-start.4 = (bf16[192,1024]{1,0:T(8,128)(2,1)S(1)}, bf16[192,1024]{1,0:T(8,128)(2,1)S(1)}, u32[]{:S(2)}, u32[]{:S(2)}) collective-permute-start(bf16[192,1024]{1,0:T(8,128)(2,1)S(1)} %get-tuple-element.42), channel_id=1, source_target_pairs={{0,2},{1,3},{2,0},{3,1},{4,6},{5,7},{6,4},{7,5},{8,10},{9,11},{10,... | collective-permute-start | bytes 1179656 | tf_op jit(solution)/shard_map/ppermute | solution.py:217
  19.4 3.4 %collective-permute-done.8.refs_2_ = bf16[192,768]{1,0:T(8,128)(2,1)S(1)} collective-permute-done((bf16[192,768]{1,0:T(8,128)(2,1)}, bf16[192,768]{1,0:T(8,128)(2,1)S(1)}, u32[]{:S(2)}, u32[]{:S(2)}) %collective-permute-start.8) | collective-permute-done | bytes 294944 | tf_op jit(solution)/shard_map/ppermute | solution.py:217
  22.8 2.2 %collective-permute-start.5 = (bf16[192,1024]{1,0:T(8,128)(2,1)S(1)}, bf16[192,1024]{1,0:T(8,128)(2,1)S(1)}, u32[]{:S(2)}, u32[]{:S(2)}) collective-permute-start(bf16[192,1024]{1,0:T(8,128)(2,1)S(1)} %get-tuple-element.43), channel_id=1, source_target_pairs={{0,4},{1,5},{2,6},{3,7},{4,0},{5,1},{6,2},{7,3},{8,12},{9,13},{10,... | collective-permute-start | bytes 1179656 | tf_op jit(solution)/shard_map/ppermute | solution.py:217
  25.0 0.6 collective-permute-start.6
  25.6 5.5 %collective-permute-done.4.refs_1_ = bf16[192,1024]{1,0:T(8,128)(2,1)S(1)} collective-permute-done((bf16[192,1024]{1,0:T(8,128)(2,1)S(1)}, bf16[192,1024]{1,0:T(8,128)(2,1)S(1)}, u32[]{:S(2)}, u32[]{:S(2)}) %collective-permute-start.4) | collective-permute-done | bytes 393248 | tf_op jit(solution)/shard_map/ppermute | solution.py:217
  31.0 2.1 %collective-permute-start = (bf16[192,256]{1,0:T(8,128)(2,1)S(1)}, bf16[192,256]{1,0:T(8,128)(2,1)S(1)}, u32[]{:S(2)}, u32[]{:S(2)}) collective-permute-start(bf16[192,256]{1,0:T(8,128)(2,1)S(1)} %get-tuple-element.38), channel_id=1, source_target_pairs={{0,2},{1,3},{2,0},{3,1},{4,6},{5,7},{6,4},{7,5},{8,10},{9,11},{10,... | collective-permute-start | bytes 294920 | tf_op jit(solution)/shard_map/ppermute | solution.py:217
  33.1 1.5 %collective-permute-start.1 = (bf16[192,256]{1,0:T(8,128)(2,1)S(1)}, bf16[192,256]{1,0:T(8,128)(2,1)S(1)}, u32[]{:S(2)}, u32[]{:S(2)}) collective-permute-start(bf16[192,256]{1,0:T(8,128)(2,1)S(1)} %get-tuple-element.39), channel_id=1, source_target_pairs={{0,4},{1,5},{2,6},{3,7},{4,0},{5,1},{6,2},{7,3},{8,12},{9,13},{10,... | collective-permute-start | bytes 294920 | tf_op jit(solution)/shard_map/ppermute | solution.py:217
  34.6 0.0 collective-permute-start.2
  34.7 1.9 %gates.1 = (bf16[256,768]{1,0:T(8,128)(2,1)S(1)}, f32[256,2048]{1,0:T(8,128)S(1)}) custom-call(s32[1]{0:T(128)} %bitcast.1.refs_0_, s32[1]{0:T(128)} %bitcast.2.refs_1_, s32[2,256]{1,0:T(2,128)S(1)} %bitcast.32, f32[1,2048]{1,0:T(1,128)S(1)} %copy-done.5, bf16[256,2048]{1,0:T(8,128)(2,1)S(1)} %bitcast.25, bf16[256,2048]{1,0:T(8,128)(2,1)S(1)} %bitcast.28, ...), custom_call_target="tpu_custom_call" | custom-call | tf_op jit(solution)/shard_map/gates/pallas_call | solution.py:267
  36.6 2.2 %hold.2.refs_5_ = bf16[2048,1024]{1,0:T(8,128)(2,1)S(1)} custom-call(bf16[2048,1024]{1,0:T(8,128)(2,1)} %collective-permute-done.3.source), custom_call_target="tpu_custom_call" | custom-call | tf_op jit(solution)/shard_map/hold/pallas_call | solution.py:254
  38.8 0.0 copy-start
  38.8 2.3 %hold.3.refs_7_.refs_8_.refs_2_ = bf16[1024,2048]{1,0:T(8,128)(2,1)S(1)} custom-call(bf16[1024,2048]{1,0:T(8,128)(2,1)} %collective-permute-done.10.source), custom_call_target="tpu_custom_call" | custom-call | tf_op jit(solution)/shard_map/hold/pallas_call | solution.py:254
  41.2 1.1 copy-done
  42.2 0.0 copy-done.4
  42.3 1.4 %first_matmul.2.refs_6_ = f32[768,1024]{1,0:T(8,128)S(1)} custom-call(bf16[192,768]{1,0:T(8,128)(2,1)S(1)} %copy-done.4, bf16[192,768]{1,0:T(8,128)(2,1)S(1)} %collective-permute-done.7.refs_1_, bf16[192,768]{1,0:T(8,128)(2,1)S(1)} %collective-permute-done.8.refs_2_, bf16[192,768]{1,0:T(8,128)(2,1)S(1)} %collective-permute-done.9.refs_3_, ...), custom_call_target="tpu_custom_call" | custom-call | tf_op jit(solution)/shard_map/first_matmul/pallas_call | solution.py:296
  43.7 0.8 collective-permute-done.5.refs_2_
  44.5 1.8 %first_matmul.3.refs_6_ = f32[768,1024]{1,0:T(8,128)S(1)} custom-call(bf16[192,1024]{1,0:T(8,128)(2,1)S(1)} %get-tuple-element.41.refs_0_, bf16[192,1024]{1,0:T(8,128)(2,1)S(1)} %collective-permute-done.4.refs_1_, bf16[192,1024]{1,0:T(8,128)(2,1)S(1)} %collective-permute-done.5.refs_2_, bf16[192,1024]{1,0:T(8,128)(2,1)S(1)} %collective-permute-done.6.refs_3_, ...), custom_call_target="tpu_custom_call" | custom-call | tf_op jit(solution)/shard_map/first_matmul/pallas_call | solution.py:296
  46.3 0.4 copy-done.1
  46.7 2.5 %bridge.1 = (bf16[768,1024]{1,0:T(8,128)(2,1)S(1)}, bf16[192,640]{1,0:T(8,128)(2,1)S(1)}, bf16[192,640]{1,0:T(8,128)(2,1)S(1)}, bf16[192,640]{1,0:T(8,128)(2,1)S(1)}, bf16[192,640]{1,0:T(8,128)(2,1)S(1)}) custom-call(bf16[192,256]{1,0:T(8,128)(2,1)S(1)} %get-tuple-element.37.refs_0_, bf16[192,256]{1,0:T(8,128)(2,1)S(1)} %collective-permute-done.refs_1_, ...), custom_call_target="tpu_custom_call" | custom-call | tf_op jit(solution)/shard_map/bridge/pallas_call | solution.py:286
  49.2 1.2 %collective-permute-start.11 = (bf16[192,640]{1,0:T(8,128)(2,1)S(1)}, bf16[192,640]{1,0:T(8,128)(2,1)S(1)}, u32[]{:S(2)}, u32[]{:S(2)}) collective-permute-start(bf16[192,640]{1,0:T(8,128)(2,1)S(1)} %get-tuple-element.51), channel_id=1, source_target_pairs={{0,2},{1,3},{2,0},{3,1},{4,6},{5,7},{6,4},{7,5},{8,10},{9,11},{10,... | collective-permute-start | bytes 737288 | tf_op jit(solution)/shard_map/ppermute | solution.py:217
  50.4 1.5 %collective-permute-start.12 = (bf16[192,640]{1,0:T(8,128)(2,1)S(1)}, bf16[192,640]{1,0:T(8,128)(2,1)S(1)}, u32[]{:S(2)}, u32[]{:S(2)}) collective-permute-start(bf16[192,640]{1,0:T(8,128)(2,1)S(1)} %get-tuple-element.52), channel_id=1, source_target_pairs={{0,4},{1,5},{2,6},{3,7},{4,0},{5,1},{6,2},{7,3},{8,12},{9,13},{10,... | collective-permute-start | bytes 737288 | tf_op jit(solution)/shard_map/ppermute | solution.py:217
  51.9 0.9 collective-permute-start.13
  52.8 1.8 %second_matmul.2 = (bf16[192,896]{1,0:T(8,128)(2,1)S(1)}, bf16[192,896]{1,0:T(8,128)(2,1)S(1)}, bf16[192,896]{1,0:T(8,128)(2,1)S(1)}, bf16[192,896]{1,0:T(8,128)(2,1)S(1)}) custom-call(bf16[768,1024]{1,0:T(8,128)(2,1)S(1)} %get-tuple-element.49.refs_0_, bf16[1024,2048]{1,0:T(8,128)(2,1)S(1)} %bitcast.21, bf16[1024,2048]{1,0:T(8,128)(2,1)S(1)} %hold.3.refs_7_.refs_8_.refs_2_), custom_call_target="tpu_custom_call" | custom-call | tf_op jit(solution)/shard_map/second_matmul/pallas_call | solution.py:316
  54.6 1.2 %collective-permute-start.16 = (bf16[192,896]{1,0:T(8,128)(2,1)S(1)}, bf16[192,896]{1,0:T(8,128)(2,1)S(1)}, u32[]{:S(2)}, u32[]{:S(2)}) collective-permute-start(bf16[192,896]{1,0:T(8,128)(2,1)S(1)} %get-tuple-element.55), channel_id=1, source_target_pairs={{0,2},{1,3},{2,0},{3,1},{4,6},{5,7},{6,4},{7,5},{8,10},{9,11},{10,... | collective-permute-start | bytes 1032200 | tf_op jit(solution)/shard_map/ppermute | solution.py:217
  55.8 1.5 %collective-permute-start.17 = (bf16[192,896]{1,0:T(8,128)(2,1)S(1)}, bf16[192,896]{1,0:T(8,128)(2,1)S(1)}, u32[]{:S(2)}, u32[]{:S(2)}) collective-permute-start(bf16[192,896]{1,0:T(8,128)(2,1)S(1)} %get-tuple-element.56), channel_id=1, source_target_pairs={{0,4},{1,5},{2,6},{3,7},{4,0},{5,1},{6,2},{7,3},{8,12},{9,13},{10,... | collective-permute-start | bytes 1032200 | tf_op jit(solution)/shard_map/ppermute | solution.py:217
  57.3 0.9 collective-permute-done.11.refs_3_
  58.2 2.1 %collective-permute-start.18 = (bf16[192,896]{1,0:T(8,128)(2,1)S(1)}, bf16[192,896]{1,0:T(8,128)(2,1)S(1)}, u32[]{:S(2)}, u32[]{:S(2)}) collective-permute-start(bf16[192,896]{1,0:T(8,128)(2,1)S(1)} %get-tuple-element.57), channel_id=1, source_target_pairs={{0,6},{1,7},{2,4},{3,5},{4,2},{5,3},{6,0},{7,1},{8,14},{9,15},{10,... | collective-permute-start | bytes 1032200 | tf_op jit(solution)/shard_map/ppermute | solution.py:217
  60.3 1.7 %collective-permute-done.12.refs_4_ = bf16[192,640]{1,0:T(8,128)(2,1)S(1)} collective-permute-done((bf16[192,640]{1,0:T(8,128)(2,1)S(1)}, bf16[192,640]{1,0:T(8,128)(2,1)S(1)}, u32[]{:S(2)}, u32[]{:S(2)}) %collective-permute-start.12) | collective-permute-done | bytes 245792 | tf_op jit(solution)/shard_map/ppermute | solution.py:217
  62.0 2.8 %collective-permute-done.13.refs_5_ = bf16[192,640]{1,0:T(8,128)(2,1)S(1)} collective-permute-done((bf16[192,640]{1,0:T(8,128)(2,1)S(1)}, bf16[192,640]{1,0:T(8,128)(2,1)S(1)}, u32[]{:S(2)}, u32[]{:S(2)}) %collective-permute-start.13) | collective-permute-done | bytes 245792 | tf_op jit(solution)/shard_map/ppermute | solution.py:217
  64.7 0.5 combine.3
  65.2 2.8 %collective-permute-start.15 = (bf16[256,640]{1,0:T(8,128)(2,1)S(1)}, bf16[256,640]{1,0:T(8,128)(2,1)S(1)}, u32[]{:S(2)}, u32[]{:S(2)}) collective-permute-start(bf16[256,640]{1,0:T(8,128)(2,1)S(1)} %combine.3), channel_id=1, source_target_pairs={{0,8},{16,24},{1,9},{17,25},{2,10},{18,26},{3,11},{19,27},{4,12},{... | collective-permute-start | bytes 983048 | tf_op jit(solution)/shard_map/ppermute | solution.py:336
  68.0 1.5 %collective-permute-start.14 = (bf16[256,640]{1,0:T(8,128)(2,1)S(1)}, bf16[256,640]{1,0:T(8,128)(2,1)S(1)}, u32[]{:S(2)}, u32[]{:S(2)}) collective-permute-start(bf16[256,640]{1,0:T(8,128)(2,1)S(1)} %combine.3), channel_id=1, source_target_pairs={{0,24},{8,16},{16,8},{24,0},{1,25},{9,17},{17,9},{25,1},{2,26},{10... | collective-permute-start | bytes 983048 | tf_op jit(solution)/shard_map/ppermute | solution.py:335
  69.5 1.3 %collective-permute-done.16.refs_3_ = bf16[192,896]{1,0:T(8,128)(2,1)S(1)} collective-permute-done((bf16[192,896]{1,0:T(8,128)(2,1)S(1)}, bf16[192,896]{1,0:T(8,128)(2,1)S(1)}, u32[]{:S(2)}, u32[]{:S(2)}) %collective-permute-start.16) | collective-permute-done | bytes 344096 | tf_op jit(solution)/shard_map/ppermute | solution.py:217
  70.8 4.7 %collective-permute-done.17.refs_4_ = bf16[192,896]{1,0:T(8,128)(2,1)S(1)} collective-permute-done((bf16[192,896]{1,0:T(8,128)(2,1)S(1)}, bf16[192,896]{1,0:T(8,128)(2,1)S(1)}, u32[]{:S(2)}, u32[]{:S(2)}) %collective-permute-start.17) | collective-permute-done | bytes 344096 | tf_op jit(solution)/shard_map/ppermute | solution.py:217
  75.6 0.6 combine.4.refs_5_
  76.1 3.5 %collective-permute-start.25 = (bf16[256,896]{1,0:T(8,128)(2,1)S(1)}, bf16[256,896]{1,0:T(8,128)(2,1)S(1)}, u32[]{:S(2)}, u32[]{:S(2)}) collective-permute-start(bf16[256,896]{1,0:T(8,128)(2,1)S(1)} %combine.4.refs_5_), channel_id=1, source_target_pairs={{0,8},{16,24},{1,9},{17,25},{2,10},{18,26},{3,11},{19,27},{4,12},{... | collective-permute-start | bytes 1376264 | tf_op jit(solution)/shard_map/ppermute | solution.py:336
  79.7 1.4 %collective-permute-start.24 = (bf16[256,896]{1,0:T(8,128)(2,1)S(1)}, bf16[256,896]{1,0:T(8,128)(2,1)S(1)}, u32[]{:S(2)}, u32[]{:S(2)}) collective-permute-start(bf16[256,896]{1,0:T(8,128)(2,1)S(1)} %combine.4.refs_5_), channel_id=1, source_target_pairs={{0,24},{8,16},{16,8},{24,0},{1,25},{9,17},{17,9},{25,1},{2,26},{10... | collective-permute-start | bytes 1376264 | tf_op jit(solution)/shard_map/ppermute | solution.py:335
  81.1 1.0 second_matmul.3
  82.1 1.4 %collective-permute-start.19 = (bf16[192,512]{1,0:T(8,128)(2,1)S(1)}, bf16[192,512]{1,0:T(8,128)(2,1)S(1)}, u32[]{:S(2)}, u32[]{:S(2)}) collective-permute-start(bf16[192,512]{1,0:T(8,128)(2,1)S(1)} %get-tuple-element.59), channel_id=1, source_target_pairs={{0,2},{1,3},{2,0},{3,1},{4,6},{5,7},{6,4},{7,5},{8,10},{9,11},{10,... | collective-permute-start | bytes 589832 | tf_op jit(solution)/shard_map/ppermute | solution.py:217
  83.5 0.7 collective-permute-start.20
  84.2 1.4 %collective-permute-start.21 = (bf16[192,512]{1,0:T(8,128)(2,1)S(1)}, bf16[192,512]{1,0:T(8,128)(2,1)S(1)}, u32[]{:S(2)}, u32[]{:S(2)}) collective-permute-start(bf16[192,512]{1,0:T(8,128)(2,1)S(1)} %get-tuple-element.61), channel_id=1, source_target_pairs={{0,6},{1,7},{2,4},{3,5},{4,2},{5,3},{6,0},{7,1},{8,14},{9,15},{10,... | collective-permute-start | bytes 589832 | tf_op jit(solution)/shard_map/ppermute | solution.py:217
  85.6 2.2 %collective-permute-done.19.refs_3_ = bf16[192,512]{1,0:T(8,128)(2,1)S(1)} collective-permute-done((bf16[192,512]{1,0:T(8,128)(2,1)S(1)}, bf16[192,512]{1,0:T(8,128)(2,1)S(1)}, u32[]{:S(2)}, u32[]{:S(2)}) %collective-permute-start.19) | collective-permute-done | bytes 196640 | tf_op jit(solution)/shard_map/ppermute | solution.py:217
  87.8 1.3 %collective-permute-done.20.refs_4_ = bf16[192,512]{1,0:T(8,128)(2,1)S(1)} collective-permute-done((bf16[192,512]{1,0:T(8,128)(2,1)S(1)}, bf16[192,512]{1,0:T(8,128)(2,1)S(1)}, u32[]{:S(2)}, u32[]{:S(2)}) %collective-permute-start.20) | collective-permute-done | bytes 196640 | tf_op jit(solution)/shard_map/ppermute | solution.py:217
  89.1 2.1 %collective-permute-done.21.refs_5_ = bf16[192,512]{1,0:T(8,128)(2,1)S(1)} collective-permute-done((bf16[192,512]{1,0:T(8,128)(2,1)S(1)}, bf16[192,512]{1,0:T(8,128)(2,1)S(1)}, u32[]{:S(2)}, u32[]{:S(2)}) %collective-permute-start.21) | collective-permute-done | bytes 196640 | tf_op jit(solution)/shard_map/ppermute | solution.py:217
  91.2 0.4 combine.5
  91.6 3.7 %collective-permute-start.23 = (bf16[256,512]{1,0:T(8,128)(2,1)S(1)}, bf16[256,512]{1,0:T(8,128)(2,1)S(1)}, u32[]{:S(2)}, u32[]{:S(2)}) collective-permute-start(bf16[256,512]{1,0:T(8,128)(2,1)S(1)} %combine.5), channel_id=1, source_target_pairs={{0,8},{16,24},{1,9},{17,25},{2,10},{18,26},{3,11},{19,27},{4,12},{... | collective-permute-start | bytes 786440 | tf_op jit(solution)/shard_map/ppermute | solution.py:336
  95.3 0.1 collective-permute-start.22
  95.4 0.8 place.3
  96.3 4.1 %collective-permute-done.24.refs_1_ = bf16[256,896]{1,0:T(8,128)(2,1)S(1)} collective-permute-done((bf16[256,896]{1,0:T(8,128)(2,1)S(1)}, bf16[256,896]{1,0:T(8,128)(2,1)S(1)}, u32[]{:S(2)}, u32[]{:S(2)}) %collective-permute-start.24) | collective-permute-done | bytes 458784 | tf_op jit(solution)/shard_map/ppermute | solution.py:335
  100.4 0.9 place.4
  101.4 2.9 %collective-permute-done.23.refs_2_ = bf16[256,512]{1,0:T(8,128)(2,1)S(1)} collective-permute-done((bf16[256,512]{1,0:T(8,128)(2,1)S(1)}, bf16[256,512]{1,0:T(8,128)(2,1)S(1)}, u32[]{:S(2)}, u32[]{:S(2)}) %collective-permute-start.23) | collective-permute-done | bytes 262176 | tf_op jit(solution)/shard_map/ppermute | solution.py:336
  104.2 2.9 %collective-permute-done.22.refs_1_ = bf16[256,512]{1,0:T(8,128)(2,1)S(1)} collective-permute-done((bf16[256,512]{1,0:T(8,128)(2,1)S(1)}, bf16[256,512]{1,0:T(8,128)(2,1)S(1)}, u32[]{:S(2)}, u32[]{:S(2)}) %collective-permute-start.22) | collective-permute-done | bytes 262176 | tf_op jit(solution)/shard_map/ppermute | solution.py:335
  107.1 0.8 place.5
  (20 shorter events, 0.0 us)
Async XLA Ops:
  0.6 34.0 %copy-start.6 = (bf16[1,2048,8]{1,2,0:T(8,128)(2,1)S(1)}, bf16[1,2048,8]{1,2,0:T(8,128)(2,1)}, u32[]{:S(2)}) copy-start(bf16[1,2048,8]{1,2,0:T(8,128)(2,1)} %param.9) | copy-start | bytes 98308
  0.6 32.5 %collective-permute-start.3 = (bf16[2048,1024]{1,0:T(8,128)(2,1)}, bf16[2048,1024]{1,0:T(8,128)(2,1)}, u32[]{:S(2)}, u32[]{:S(2)}) collective-permute-start(bf16[2048,1024]{1,0:T(8,128)(2,1)} %bitcast.15), channel_id=1, source_target_pairs={{0,1},{1,0},{2,3},{3,2},{4,5},{5,4},{6,7},{7,6},{8,9},{9,8},{10,11... | collective-permute-start | bytes 12582920 | tf_op jit(solution)/shard_map/ppermute | solution.py:213
  1.2 33.5 %collective-permute-start.10 = (bf16[1024,2048]{1,0:T(8,128)(2,1)}, bf16[1024,2048]{1,0:T(8,128)(2,1)}, u32[]{:S(2)}, u32[]{:S(2)}) collective-permute-start(bf16[1024,2048]{1,0:T(8,128)(2,1)} %bitcast.19), channel_id=1, source_target_pairs={{0,1},{1,0},{2,3},{3,2},{4,5},{5,4},{6,7},{7,6},{8,9},{9,8},{10,11... | collective-permute-start | bytes 12582920 | tf_op jit(solution)/shard_map/ppermute | solution.py:213
  5.2 12.2 %collective-permute-start.7 = (bf16[192,768]{1,0:T(8,128)(2,1)}, bf16[192,768]{1,0:T(8,128)(2,1)S(1)}, u32[]{:S(2)}, u32[]{:S(2)}) collective-permute-start(bf16[192,768]{1,0:T(8,128)(2,1)} %get-tuple-element.46), channel_id=1, source_target_pairs={{0,2},{1,3},{2,0},{3,1},{4,6},{5,7},{6,4},{7,5},{8,10},{9,11},{10,... | collective-permute-start | bytes 884744 | tf_op jit(solution)/shard_map/ppermute | solution.py:217
  8.2 14.6 %collective-permute-start.8 = (bf16[192,768]{1,0:T(8,128)(2,1)}, bf16[192,768]{1,0:T(8,128)(2,1)S(1)}, u32[]{:S(2)}, u32[]{:S(2)}) collective-permute-start(bf16[192,768]{1,0:T(8,128)(2,1)} %get-tuple-element.47), channel_id=1, source_target_pairs={{0,4},{1,5},{2,6},{3,7},{4,0},{5,1},{6,2},{7,3},{8,12},{9,13},{10,... | collective-permute-start | bytes 884744 | tf_op jit(solution)/shard_map/ppermute | solution.py:217
  9.7 15.2 %collective-permute-start.9 = (bf16[192,768]{1,0:T(8,128)(2,1)}, bf16[192,768]{1,0:T(8,128)(2,1)S(1)}, u32[]{:S(2)}, u32[]{:S(2)}) collective-permute-start(bf16[192,768]{1,0:T(8,128)(2,1)} %get-tuple-element.48), channel_id=1, source_target_pairs={{0,6},{1,7},{2,4},{3,5},{4,2},{5,3},{6,0},{7,1},{8,14},{9,15},{10,... | collective-permute-start | bytes 884744 | tf_op jit(solution)/shard_map/ppermute | solution.py:217
  9.8 1.2 %copy-start.2 = (bf16[1,256,2048]{2,1,0:T(8,128)(2,1)S(1)}, bf16[1,256,2048]{2,1,0:T(8,128)(2,1)}, u32[]{:S(2)}) copy-start(bf16[1,256,2048]{2,1,0:T(8,128)(2,1)} %param.7) | copy-start | bytes 3145732
  11.0 1.2 %copy-start.3 = (bf16[1,256,2048]{2,1,0:T(8,128)(2,1)S(1)}, bf16[1,256,2048]{2,1,0:T(8,128)(2,1)}, u32[]{:S(2)}) copy-start(bf16[1,256,2048]{2,1,0:T(8,128)(2,1)} %param.11) | copy-start | bytes 3145732
  12.2 0.7 copy-start.5
  12.9 0.7 copy-start.7
  17.4 13.6 %collective-permute-start.4 = (bf16[192,1024]{1,0:T(8,128)(2,1)S(1)}, bf16[192,1024]{1,0:T(8,128)(2,1)S(1)}, u32[]{:S(2)}, u32[]{:S(2)}) collective-permute-start(bf16[192,1024]{1,0:T(8,128)(2,1)S(1)} %get-tuple-element.42), channel_id=1, source_target_pairs={{0,2},{1,3},{2,0},{3,1},{4,6},{5,7},{6,4},{7,5},{8,10},{9,11},{10,... | collective-permute-start | bytes 1179656 | tf_op jit(solution)/shard_map/ppermute | solution.py:217
  22.8 21.7 %collective-permute-start.5 = (bf16[192,1024]{1,0:T(8,128)(2,1)S(1)}, bf16[192,1024]{1,0:T(8,128)(2,1)S(1)}, u32[]{:S(2)}, u32[]{:S(2)}) collective-permute-start(bf16[192,1024]{1,0:T(8,128)(2,1)S(1)} %get-tuple-element.43), channel_id=1, source_target_pairs={{0,4},{1,5},{2,6},{3,7},{4,0},{5,1},{6,2},{7,3},{8,12},{9,13},{10,... | collective-permute-start | bytes 1179656 | tf_op jit(solution)/shard_map/ppermute | solution.py:217
  25.0 19.5 %collective-permute-start.6 = (bf16[192,1024]{1,0:T(8,128)(2,1)S(1)}, bf16[192,1024]{1,0:T(8,128)(2,1)S(1)}, u32[]{:S(2)}, u32[]{:S(2)}) collective-permute-start(bf16[192,1024]{1,0:T(8,128)(2,1)S(1)} %get-tuple-element.44), channel_id=1, source_target_pairs={{0,6},{1,7},{2,4},{3,5},{4,2},{5,3},{6,0},{7,1},{8,14},{9,15},{10,... | collective-permute-start | bytes 1179656 | tf_op jit(solution)/shard_map/ppermute | solution.py:217
  31.0 15.3 %collective-permute-start = (bf16[192,256]{1,0:T(8,128)(2,1)S(1)}, bf16[192,256]{1,0:T(8,128)(2,1)S(1)}, u32[]{:S(2)}, u32[]{:S(2)}) collective-permute-start(bf16[192,256]{1,0:T(8,128)(2,1)S(1)} %get-tuple-element.38), channel_id=1, source_target_pairs={{0,2},{1,3},{2,0},{3,1},{4,6},{5,7},{6,4},{7,5},{8,10},{9,11},{10,... | collective-permute-start | bytes 294920 | tf_op jit(solution)/shard_map/ppermute | solution.py:217
  33.1 13.2 %collective-permute-start.1 = (bf16[192,256]{1,0:T(8,128)(2,1)S(1)}, bf16[192,256]{1,0:T(8,128)(2,1)S(1)}, u32[]{:S(2)}, u32[]{:S(2)}) collective-permute-start(bf16[192,256]{1,0:T(8,128)(2,1)S(1)} %get-tuple-element.39), channel_id=1, source_target_pairs={{0,4},{1,5},{2,6},{3,7},{4,0},{5,1},{6,2},{7,3},{8,12},{9,13},{10,... | collective-permute-start | bytes 294920 | tf_op jit(solution)/shard_map/ppermute | solution.py:217
  34.6 11.7 %collective-permute-start.2 = (bf16[192,256]{1,0:T(8,128)(2,1)S(1)}, bf16[192,256]{1,0:T(8,128)(2,1)S(1)}, u32[]{:S(2)}, u32[]{:S(2)}) collective-permute-start(bf16[192,256]{1,0:T(8,128)(2,1)S(1)} %get-tuple-element.40), channel_id=1, source_target_pairs={{0,6},{1,7},{2,4},{3,5},{4,2},{5,3},{6,0},{7,1},{8,14},{9,15},{10,... | collective-permute-start | bytes 294920 | tf_op jit(solution)/shard_map/ppermute | solution.py:217
  38.8 3.5 %copy-start = (bf16[1,1,2048,1024]{3,2,1,0:T(8,128)(2,1)S(1)}, bf16[1,1,2048,1024]{3,2,1,0:T(8,128)(2,1)}, u32[]{:S(2)}) copy-start(bf16[1,1,2048,1024]{3,2,1,0:T(8,128)(2,1)} %param.12) | copy-start | bytes 12582916
  38.8 3.5 %copy-start.4 = (bf16[192,768]{1,0:T(8,128)(2,1)S(1)}, bf16[192,768]{1,0:T(8,128)(2,1)}, u32[]{:S(2)}) copy-start(bf16[192,768]{1,0:T(8,128)(2,1)} %get-tuple-element.45.refs_0_) | copy-start | bytes 884740
  44.5 2.2 %copy-start.1 = (bf16[1,1,1024,2048]{3,2,1,0:T(8,128)(2,1)S(1)}, bf16[1,1,1024,2048]{3,2,1,0:T(8,128)(2,1)}, u32[]{:S(2)}) copy-start(bf16[1,1,1024,2048]{3,2,1,0:T(8,128)(2,1)} %param.13) | copy-start | bytes 12582916
  49.2 9.0 %collective-permute-start.11 = (bf16[192,640]{1,0:T(8,128)(2,1)S(1)}, bf16[192,640]{1,0:T(8,128)(2,1)S(1)}, u32[]{:S(2)}, u32[]{:S(2)}) collective-permute-start(bf16[192,640]{1,0:T(8,128)(2,1)S(1)} %get-tuple-element.51), channel_id=1, source_target_pairs={{0,2},{1,3},{2,0},{3,1},{4,6},{5,7},{6,4},{7,5},{8,10},{9,11},{10,... | collective-permute-start | bytes 737288 | tf_op jit(solution)/shard_map/ppermute | solution.py:217
  50.4 11.6 %collective-permute-start.12 = (bf16[192,640]{1,0:T(8,128)(2,1)S(1)}, bf16[192,640]{1,0:T(8,128)(2,1)S(1)}, u32[]{:S(2)}, u32[]{:S(2)}) collective-permute-start(bf16[192,640]{1,0:T(8,128)(2,1)S(1)} %get-tuple-element.52), channel_id=1, source_target_pairs={{0,4},{1,5},{2,6},{3,7},{4,0},{5,1},{6,2},{7,3},{8,12},{9,13},{10,... | collective-permute-start | bytes 737288 | tf_op jit(solution)/shard_map/ppermute | solution.py:217
  51.9 12.8 %collective-permute-start.13 = (bf16[192,640]{1,0:T(8,128)(2,1)S(1)}, bf16[192,640]{1,0:T(8,128)(2,1)S(1)}, u32[]{:S(2)}, u32[]{:S(2)}) collective-permute-start(bf16[192,640]{1,0:T(8,128)(2,1)S(1)} %get-tuple-element.53), channel_id=1, source_target_pairs={{0,6},{1,7},{2,4},{3,5},{4,2},{5,3},{6,0},{7,1},{8,14},{9,15},{10,... | collective-permute-start | bytes 737288 | tf_op jit(solution)/shard_map/ppermute | solution.py:217
  54.6 16.3 %collective-permute-start.16 = (bf16[192,896]{1,0:T(8,128)(2,1)S(1)}, bf16[192,896]{1,0:T(8,128)(2,1)S(1)}, u32[]{:S(2)}, u32[]{:S(2)}) collective-permute-start(bf16[192,896]{1,0:T(8,128)(2,1)S(1)} %get-tuple-element.55), channel_id=1, source_target_pairs={{0,2},{1,3},{2,0},{3,1},{4,6},{5,7},{6,4},{7,5},{8,10},{9,11},{10,... | collective-permute-start | bytes 1032200 | tf_op jit(solution)/shard_map/ppermute | solution.py:217
  55.8 19.8 %collective-permute-start.17 = (bf16[192,896]{1,0:T(8,128)(2,1)S(1)}, bf16[192,896]{1,0:T(8,128)(2,1)S(1)}, u32[]{:S(2)}, u32[]{:S(2)}) collective-permute-start(bf16[192,896]{1,0:T(8,128)(2,1)S(1)} %get-tuple-element.56), channel_id=1, source_target_pairs={{0,4},{1,5},{2,6},{3,7},{4,0},{5,1},{6,2},{7,3},{8,12},{9,13},{10,... | collective-permute-start | bytes 1032200 | tf_op jit(solution)/shard_map/ppermute | solution.py:217
  58.2 17.3 %collective-permute-start.18 = (bf16[192,896]{1,0:T(8,128)(2,1)S(1)}, bf16[192,896]{1,0:T(8,128)(2,1)S(1)}, u32[]{:S(2)}, u32[]{:S(2)}) collective-permute-start(bf16[192,896]{1,0:T(8,128)(2,1)S(1)} %get-tuple-element.57), channel_id=1, source_target_pairs={{0,6},{1,7},{2,4},{3,5},{4,2},{5,3},{6,0},{7,1},{8,14},{9,15},{10,... | collective-permute-start | bytes 1032200 | tf_op jit(solution)/shard_map/ppermute | solution.py:217
  65.2 15.9 %collective-permute-start.15 = (bf16[256,640]{1,0:T(8,128)(2,1)S(1)}, bf16[256,640]{1,0:T(8,128)(2,1)S(1)}, u32[]{:S(2)}, u32[]{:S(2)}) collective-permute-start(bf16[256,640]{1,0:T(8,128)(2,1)S(1)} %combine.3), channel_id=1, source_target_pairs={{0,8},{16,24},{1,9},{17,25},{2,10},{18,26},{3,11},{19,27},{4,12},{... | collective-permute-start | bytes 983048 | tf_op jit(solution)/shard_map/ppermute | solution.py:336
  68.0 13.1 %collective-permute-start.14 = (bf16[256,640]{1,0:T(8,128)(2,1)S(1)}, bf16[256,640]{1,0:T(8,128)(2,1)S(1)}, u32[]{:S(2)}, u32[]{:S(2)}) collective-permute-start(bf16[256,640]{1,0:T(8,128)(2,1)S(1)} %combine.3), channel_id=1, source_target_pairs={{0,24},{8,16},{16,8},{24,0},{1,25},{9,17},{17,9},{25,1},{2,26},{10... | collective-permute-start | bytes 983048 | tf_op jit(solution)/shard_map/ppermute | solution.py:335
  76.1 20.1 %collective-permute-start.25 = (bf16[256,896]{1,0:T(8,128)(2,1)S(1)}, bf16[256,896]{1,0:T(8,128)(2,1)S(1)}, u32[]{:S(2)}, u32[]{:S(2)}) collective-permute-start(bf16[256,896]{1,0:T(8,128)(2,1)S(1)} %combine.4.refs_5_), channel_id=1, source_target_pairs={{0,8},{16,24},{1,9},{17,25},{2,10},{18,26},{3,11},{19,27},{4,12},{... | collective-permute-start | bytes 1376264 | tf_op jit(solution)/shard_map/ppermute | solution.py:336
  79.7 20.8 %collective-permute-start.24 = (bf16[256,896]{1,0:T(8,128)(2,1)S(1)}, bf16[256,896]{1,0:T(8,128)(2,1)S(1)}, u32[]{:S(2)}, u32[]{:S(2)}) collective-permute-start(bf16[256,896]{1,0:T(8,128)(2,1)S(1)} %combine.4.refs_5_), channel_id=1, source_target_pairs={{0,24},{8,16},{16,8},{24,0},{1,25},{9,17},{17,9},{25,1},{2,26},{10... | collective-permute-start | bytes 1376264 | tf_op jit(solution)/shard_map/ppermute | solution.py:335
  82.1 5.7 %collective-permute-start.19 = (bf16[192,512]{1,0:T(8,128)(2,1)S(1)}, bf16[192,512]{1,0:T(8,128)(2,1)S(1)}, u32[]{:S(2)}, u32[]{:S(2)}) collective-permute-start(bf16[192,512]{1,0:T(8,128)(2,1)S(1)} %get-tuple-element.59), channel_id=1, source_target_pairs={{0,2},{1,3},{2,0},{3,1},{4,6},{5,7},{6,4},{7,5},{8,10},{9,11},{10,... | collective-permute-start | bytes 589832 | tf_op jit(solution)/shard_map/ppermute | solution.py:217
  83.5 5.7 %collective-permute-start.20 = (bf16[192,512]{1,0:T(8,128)(2,1)S(1)}, bf16[192,512]{1,0:T(8,128)(2,1)S(1)}, u32[]{:S(2)}, u32[]{:S(2)}) collective-permute-start(bf16[192,512]{1,0:T(8,128)(2,1)S(1)} %get-tuple-element.60), channel_id=1, source_target_pairs={{0,4},{1,5},{2,6},{3,7},{4,0},{5,1},{6,2},{7,3},{8,12},{9,13},{10,... | collective-permute-start | bytes 589832 | tf_op jit(solution)/shard_map/ppermute | solution.py:217
  84.2 7.0 %collective-permute-start.21 = (bf16[192,512]{1,0:T(8,128)(2,1)S(1)}, bf16[192,512]{1,0:T(8,128)(2,1)S(1)}, u32[]{:S(2)}, u32[]{:S(2)}) collective-permute-start(bf16[192,512]{1,0:T(8,128)(2,1)S(1)} %get-tuple-element.61), channel_id=1, source_target_pairs={{0,6},{1,7},{2,4},{3,5},{4,2},{5,3},{6,0},{7,1},{8,14},{9,15},{10,... | collective-permute-start | bytes 589832 | tf_op jit(solution)/shard_map/ppermute | solution.py:217
  91.6 12.6 %collective-permute-start.23 = (bf16[256,512]{1,0:T(8,128)(2,1)S(1)}, bf16[256,512]{1,0:T(8,128)(2,1)S(1)}, u32[]{:S(2)}, u32[]{:S(2)}) collective-permute-start(bf16[256,512]{1,0:T(8,128)(2,1)S(1)} %combine.5), channel_id=1, source_target_pairs={{0,8},{16,24},{1,9},{17,25},{2,10},{18,26},{3,11},{19,27},{4,12},{... | collective-permute-start | bytes 786440 | tf_op jit(solution)/shard_map/ppermute | solution.py:336
  95.3 11.8 %collective-permute-start.22 = (bf16[256,512]{1,0:T(8,128)(2,1)S(1)}, bf16[256,512]{1,0:T(8,128)(2,1)S(1)}, u32[]{:S(2)}, u32[]{:S(2)}) collective-permute-start(bf16[256,512]{1,0:T(8,128)(2,1)S(1)} %combine.5), channel_id=1, source_target_pairs={{0,24},{8,16},{16,8},{24,0},{1,25},{9,17},{17,9},{25,1},{2,26},{10... | collective-permute-start | bytes 786440 | tf_op jit(solution)/shard_map/ppermute | solution.py:335

commit v7 on v6

--- a/solution.py
+++ b/solution.py
@@ -213,10 +213,11 @@
         return lax.ppermute(block, "expert", [(i, i ^ 1) for i in range(devices)])
 
     def exchange(blocks):
-        return [blocks[0]] + [
-            lax.ppermute(blocks[k], "expert", [(i, i ^ (2 * k)) for i in range(devices)])
-            for k in range(1, chips)
-        ]
+        moved = {
+            k: lax.ppermute(blocks[k], "expert", [(i, i ^ (2 * k)) for i in range(devices)])
+            for k in range(chips - 1, 0, -1)
+        }
+        return [blocks[0]] + [moved[k] for k in range(1, chips)]
 
     incoming = cut(width, IN_PARTS)
     outgoing = cut(width, OUT_PARTS)

time: 110 us -> 110 us (level)
  no operation moved by 1% of the time
where the time goes in v7:
time: 110 us; the launch traced here: 108 us
  starting transfers between devices  38.4 us (35%)
  waiting for transfers between devices  36.6 us (33%)
  Pallas kernels  26.7 us (24%)
  local copies, waits for them, and re-layouts  5.3 us (5%)
    ppermute x18, waiting for transfers between devices, exchange(): lax.ppermute(blocks[k], 'expert', [(i, i ^ 2 * k) for i in range(devices)])  26.7 us
    ppermute x18, starting transfers between devices, exchange(): lax.ppermute(blocks[k], 'expert', [(i, i ^ 2 * k) for i in range(devices)])  24.8 us
    ppermute x3, starting transfers between devices, local(): ahead = lax.ppermute(y, 'section', onward) if onward else across  9.99 us
    pallas_call x2, Pallas kernels, dispatch(): pl.pallas_call(lambda *refs: dispatch_kernel(experts, slots, pieces, colu...  7.8 us
    ppermute x3, waiting for transfers between devices, local(): across = lax.ppermute(y, 'section', mirror)  6.99 us
    unnamed x16, local copies, waits for them, and re-layouts  5.3 us
    pallas_call x2, Pallas kernels, hold(): pl.pallas_call(hold_kernel, out_shape=jax.ShapeDtypeStruct(block.shape, b...  4.54 us
    pallas_call x2, Pallas kernels, local(): pl.pallas_call(lambda *refs, c=c, ends=ends: first_kernel(chips, slots, e...  3.17 us
  transfers between devices with their start and end apart: 26, of which 14 were waited for; matrix products, arithmetic and copies ran while one was open for 0% of the time, Pallas kernels for 22%

profile of v7, /device:TPU:0, one launch (start us, length us, event | category | flops | bytes accessed | tf_op | source)
XLA Modules:
  0.0 107.9 jit_solution(5806980681961059254)
XLA Ops:
  0.6 0.5 collective-permute-start.3
  1.2 0.1 collective-permute-start.10
  1.2 4.0 %dispatch.3 = (bf16[192,768]{1,0:T(8,128)(2,1)}, bf16[192,768]{1,0:T(8,128)(2,1)}, bf16[192,768]{1,0:T(8,128)(2,1)}, bf16[192,768]{1,0:T(8,128)(2,1)}) custom-call(s32[1]{0:T(128)} %bitcast.1.refs_0_, s32[1]{0:T(128)} %bitcast.2.refs_1_, s32[2,256]{1,0:T(2,128)} %bitcast.30, f32[1,2048]{1,0:T(1,128)} %refs_3_.5, bf16[256,2048]{1,0:T(8,128)(2,1)} %bitcast.23, ...), custom_call_target="tpu_custom_call" | custom-call | tf_op jit(solution)/shard_map/dispatch/pallas_call | solution.py:230
  5.2 3.0 %collective-permute-start.7 = (bf16[192,768]{1,0:T(8,128)(2,1)}, bf16[192,768]{1,0:T(8,128)(2,1)S(1)}, u32[]{:S(2)}, u32[]{:S(2)}) collective-permute-start(bf16[192,768]{1,0:T(8,128)(2,1)} %get-tuple-element.46), channel_id=1, source_target_pairs={{0,2},{1,3},{2,0},{3,1},{4,6},{5,7},{6,4},{7,5},{8,10},{9,11},{10,... | collective-permute-start | bytes 884744 | tf_op jit(solution)/shard_map/ppermute | solution.py:217
  8.2 1.5 %collective-permute-start.8 = (bf16[192,768]{1,0:T(8,128)(2,1)}, bf16[192,768]{1,0:T(8,128)(2,1)S(1)}, u32[]{:S(2)}, u32[]{:S(2)}) collective-permute-start(bf16[192,768]{1,0:T(8,128)(2,1)} %get-tuple-element.47), channel_id=1, source_target_pairs={{0,4},{1,5},{2,6},{3,7},{4,0},{5,1},{6,2},{7,3},{8,12},{9,13},{10,... | collective-permute-start | bytes 884744 | tf_op jit(solution)/shard_map/ppermute | solution.py:217
  9.7 0.0 collective-permute-start.9
  9.8 1.2 %copy-done.2 = bf16[1,256,2048]{2,1,0:T(8,128)(2,1)S(1)} copy-done((bf16[1,256,2048]{2,1,0:T(8,128)(2,1)S(1)}, bf16[1,256,2048]{2,1,0:T(8,128)(2,1)}, u32[]{:S(2)}) %copy-start.2) | copy-done | bytes 1048600
  11.0 1.2 %copy-done.3 = bf16[1,256,2048]{2,1,0:T(8,128)(2,1)S(1)} copy-done((bf16[1,256,2048]{2,1,0:T(8,128)(2,1)S(1)}, bf16[1,256,2048]{2,1,0:T(8,128)(2,1)}, u32[]{:S(2)}) %copy-start.3) | copy-done | bytes 1048600
  12.2 0.7 copy-done.5
  12.9 0.7 copy-done.7
  13.6 3.8 %dispatch.2 = (bf16[192,1024]{1,0:T(8,128)(2,1)S(1)}, bf16[192,1024]{1,0:T(8,128)(2,1)S(1)}, bf16[192,1024]{1,0:T(8,128)(2,1)S(1)}, bf16[192,1024]{1,0:T(8,128)(...) custom-call(s32[1]{0:T(128)} %bitcast.1.refs_0_, ...), custom_call_target="tpu_custom_call" | custom-call | tf_op jit(solution)/shard_map/dispatch/pallas_call | solution.py:230
  17.4 2.0 %collective-permute-start.4 = (bf16[192,1024]{1,0:T(8,128)(2,1)S(1)}, bf16[192,1024]{1,0:T(8,128)(2,1)S(1)}, u32[]{:S(2)}, u32[]{:S(2)}) collective-permute-start(bf16[192,1024]{1,0:T(8,128)(2,1)S(1)} %get-tuple-element.42), channel_id=1, source_target_pairs={{0,2},{1,3},{2,0},{3,1},{4,6},{5,7},{6,4},{7,5},{8,10},{9,11},{10,... | collective-permute-start | bytes 1179656 | tf_op jit(solution)/shard_map/ppermute | solution.py:217
  19.4 3.4 %collective-permute-done.8.refs_2_ = bf16[192,768]{1,0:T(8,128)(2,1)S(1)} collective-permute-done((bf16[192,768]{1,0:T(8,128)(2,1)}, bf16[192,768]{1,0:T(8,128)(2,1)S(1)}, u32[]{:S(2)}, u32[]{:S(2)}) %collective-permute-start.8) | collective-permute-done | bytes 294944 | tf_op jit(solution)/shard_map/ppermute | solution.py:217
  22.8 2.2 %collective-permute-start.5 = (bf16[192,1024]{1,0:T(8,128)(2,1)S(1)}, bf16[192,1024]{1,0:T(8,128)(2,1)S(1)}, u32[]{:S(2)}, u32[]{:S(2)}) collective-permute-start(bf16[192,1024]{1,0:T(8,128)(2,1)S(1)} %get-tuple-element.43), channel_id=1, source_target_pairs={{0,4},{1,5},{2,6},{3,7},{4,0},{5,1},{6,2},{7,3},{8,12},{9,13},{10,... | collective-permute-start | bytes 1179656 | tf_op jit(solution)/shard_map/ppermute | solution.py:217
  25.0 0.6 collective-permute-start.6
  25.6 5.5 %collective-permute-done.4.refs_1_ = bf16[192,1024]{1,0:T(8,128)(2,1)S(1)} collective-permute-done((bf16[192,1024]{1,0:T(8,128)(2,1)S(1)}, bf16[192,1024]{1,0:T(8,128)(2,1)S(1)}, u32[]{:S(2)}, u32[]{:S(2)}) %collective-permute-start.4) | collective-permute-done | bytes 393248 | tf_op jit(solution)/shard_map/ppermute | solution.py:217
  31.0 2.1 %collective-permute-start = (bf16[192,256]{1,0:T(8,128)(2,1)S(1)}, bf16[192,256]{1,0:T(8,128)(2,1)S(1)}, u32[]{:S(2)}, u32[]{:S(2)}) collective-permute-start(bf16[192,256]{1,0:T(8,128)(2,1)S(1)} %get-tuple-element.38), channel_id=1, source_target_pairs={{0,2},{1,3},{2,0},{3,1},{4,6},{5,7},{6,4},{7,5},{8,10},{9,11},{10,... | collective-permute-start | bytes 294920 | tf_op jit(solution)/shard_map/ppermute | solution.py:217
  33.1 1.5 %collective-permute-start.1 = (bf16[192,256]{1,0:T(8,128)(2,1)S(1)}, bf16[192,256]{1,0:T(8,128)(2,1)S(1)}, u32[]{:S(2)}, u32[]{:S(2)}) collective-permute-start(bf16[192,256]{1,0:T(8,128)(2,1)S(1)} %get-tuple-element.39), channel_id=1, source_target_pairs={{0,4},{1,5},{2,6},{3,7},{4,0},{5,1},{6,2},{7,3},{8,12},{9,13},{10,... | collective-permute-start | bytes 294920 | tf_op jit(solution)/shard_map/ppermute | solution.py:217
  34.6 0.0 collective-permute-start.2
  34.7 1.9 %gates.1 = (bf16[256,768]{1,0:T(8,128)(2,1)S(1)}, f32[256,2048]{1,0:T(8,128)S(1)}) custom-call(s32[1]{0:T(128)} %bitcast.1.refs_0_, s32[1]{0:T(128)} %bitcast.2.refs_1_, s32[2,256]{1,0:T(2,128)S(1)} %bitcast.32, f32[1,2048]{1,0:T(1,128)S(1)} %copy-done.5, bf16[256,2048]{1,0:T(8,128)(2,1)S(1)} %bitcast.25, bf16[256,2048]{1,0:T(8,128)(2,1)S(1)} %bitcast.28, ...), custom_call_target="tpu_custom_call" | custom-call | tf_op jit(solution)/shard_map/gates/pallas_call | solution.py:268
  36.6 2.2 %hold.2.refs_5_ = bf16[2048,1024]{1,0:T(8,128)(2,1)S(1)} custom-call(bf16[2048,1024]{1,0:T(8,128)(2,1)} %collective-permute-done.3.source), custom_call_target="tpu_custom_call" | custom-call | tf_op jit(solution)/shard_map/hold/pallas_call | solution.py:255
  38.8 0.0 copy-start
  38.8 2.3 %hold.3.refs_7_.refs_8_.refs_2_ = bf16[1024,2048]{1,0:T(8,128)(2,1)S(1)} custom-call(bf16[1024,2048]{1,0:T(8,128)(2,1)} %collective-permute-done.10.source), custom_call_target="tpu_custom_call" | custom-call | tf_op jit(solution)/shard_map/hold/pallas_call | solution.py:255
  41.2 1.1 copy-done
  42.2 0.0 copy-done.4
  42.3 1.4 %first_matmul.2.refs_6_ = f32[768,1024]{1,0:T(8,128)S(1)} custom-call(bf16[192,768]{1,0:T(8,128)(2,1)S(1)} %copy-done.4, bf16[192,768]{1,0:T(8,128)(2,1)S(1)} %collective-permute-done.7.refs_1_, bf16[192,768]{1,0:T(8,128)(2,1)S(1)} %collective-permute-done.8.refs_2_, bf16[192,768]{1,0:T(8,128)(2,1)S(1)} %collective-permute-done.9.refs_3_, ...), custom_call_target="tpu_custom_call" | custom-call | tf_op jit(solution)/shard_map/first_matmul/pallas_call | solution.py:297
  43.7 0.8 collective-permute-done.5.refs_2_
  44.5 1.8 %first_matmul.3.refs_6_ = f32[768,1024]{1,0:T(8,128)S(1)} custom-call(bf16[192,1024]{1,0:T(8,128)(2,1)S(1)} %get-tuple-element.41.refs_0_, bf16[192,1024]{1,0:T(8,128)(2,1)S(1)} %collective-permute-done.4.refs_1_, bf16[192,1024]{1,0:T(8,128)(2,1)S(1)} %collective-permute-done.5.refs_2_, bf16[192,1024]{1,0:T(8,128)(2,1)S(1)} %collective-permute-done.6.refs_3_, ...), custom_call_target="tpu_custom_call" | custom-call | tf_op jit(solution)/shard_map/first_matmul/pallas_call | solution.py:297
  46.3 0.4 copy-done.1
  46.7 2.5 %bridge.1 = (bf16[768,1024]{1,0:T(8,128)(2,1)S(1)}, bf16[192,640]{1,0:T(8,128)(2,1)S(1)}, bf16[192,640]{1,0:T(8,128)(2,1)S(1)}, bf16[192,640]{1,0:T(8,128)(2,1)S(1)}, bf16[192,640]{1,0:T(8,128)(2,1)S(1)}) custom-call(bf16[192,256]{1,0:T(8,128)(2,1)S(1)} %get-tuple-element.37.refs_0_, bf16[192,256]{1,0:T(8,128)(2,1)S(1)} %collective-permute-done.refs_1_, ...), custom_call_target="tpu_custom_call" | custom-call | tf_op jit(solution)/shard_map/bridge/pallas_call | solution.py:287
  49.2 1.2 %collective-permute-start.11 = (bf16[192,640]{1,0:T(8,128)(2,1)S(1)}, bf16[192,640]{1,0:T(8,128)(2,1)S(1)}, u32[]{:S(2)}, u32[]{:S(2)}) collective-permute-start(bf16[192,640]{1,0:T(8,128)(2,1)S(1)} %get-tuple-element.51), channel_id=1, source_target_pairs={{0,2},{1,3},{2,0},{3,1},{4,6},{5,7},{6,4},{7,5},{8,10},{9,11},{10,... | collective-permute-start | bytes 737288 | tf_op jit(solution)/shard_map/ppermute | solution.py:217
  50.4 1.5 %collective-permute-start.12 = (bf16[192,640]{1,0:T(8,128)(2,1)S(1)}, bf16[192,640]{1,0:T(8,128)(2,1)S(1)}, u32[]{:S(2)}, u32[]{:S(2)}) collective-permute-start(bf16[192,640]{1,0:T(8,128)(2,1)S(1)} %get-tuple-element.52), channel_id=1, source_target_pairs={{0,4},{1,5},{2,6},{3,7},{4,0},{5,1},{6,2},{7,3},{8,12},{9,13},{10,... | collective-permute-start | bytes 737288 | tf_op jit(solution)/shard_map/ppermute | solution.py:217
  51.9 0.9 collective-permute-start.13
  52.8 1.8 %second_matmul.2 = (bf16[192,896]{1,0:T(8,128)(2,1)S(1)}, bf16[192,896]{1,0:T(8,128)(2,1)S(1)}, bf16[192,896]{1,0:T(8,128)(2,1)S(1)}, bf16[192,896]{1,0:T(8,128)(2,1)S(1)}) custom-call(bf16[768,1024]{1,0:T(8,128)(2,1)S(1)} %get-tuple-element.49.refs_0_, bf16[1024,2048]{1,0:T(8,128)(2,1)S(1)} %bitcast.21, bf16[1024,2048]{1,0:T(8,128)(2,1)S(1)} %hold.3.refs_7_.refs_8_.refs_2_), custom_call_target="tpu_custom_call" | custom-call | tf_op jit(solution)/shard_map/second_matmul/pallas_call | solution.py:317
  54.6 1.2 %collective-permute-start.16 = (bf16[192,896]{1,0:T(8,128)(2,1)S(1)}, bf16[192,896]{1,0:T(8,128)(2,1)S(1)}, u32[]{:S(2)}, u32[]{:S(2)}) collective-permute-start(bf16[192,896]{1,0:T(8,128)(2,1)S(1)} %get-tuple-element.55), channel_id=1, source_target_pairs={{0,2},{1,3},{2,0},{3,1},{4,6},{5,7},{6,4},{7,5},{8,10},{9,11},{10,... | collective-permute-start | bytes 1032200 | tf_op jit(solution)/shard_map/ppermute | solution.py:217
  55.8 1.5 %collective-permute-start.17 = (bf16[192,896]{1,0:T(8,128)(2,1)S(1)}, bf16[192,896]{1,0:T(8,128)(2,1)S(1)}, u32[]{:S(2)}, u32[]{:S(2)}) collective-permute-start(bf16[192,896]{1,0:T(8,128)(2,1)S(1)} %get-tuple-element.56), channel_id=1, source_target_pairs={{0,4},{1,5},{2,6},{3,7},{4,0},{5,1},{6,2},{7,3},{8,12},{9,13},{10,... | collective-permute-start | bytes 1032200 | tf_op jit(solution)/shard_map/ppermute | solution.py:217
  57.3 0.9 collective-permute-done.11.refs_3_
  58.2 2.1 %collective-permute-start.18 = (bf16[192,896]{1,0:T(8,128)(2,1)S(1)}, bf16[192,896]{1,0:T(8,128)(2,1)S(1)}, u32[]{:S(2)}, u32[]{:S(2)}) collective-permute-start(bf16[192,896]{1,0:T(8,128)(2,1)S(1)} %get-tuple-element.57), channel_id=1, source_target_pairs={{0,6},{1,7},{2,4},{3,5},{4,2},{5,3},{6,0},{7,1},{8,14},{9,15},{10,... | collective-permute-start | bytes 1032200 | tf_op jit(solution)/shard_map/ppermute | solution.py:217
  60.3 1.7 %collective-permute-done.12.refs_4_ = bf16[192,640]{1,0:T(8,128)(2,1)S(1)} collective-permute-done((bf16[192,640]{1,0:T(8,128)(2,1)S(1)}, bf16[192,640]{1,0:T(8,128)(2,1)S(1)}, u32[]{:S(2)}, u32[]{:S(2)}) %collective-permute-start.12) | collective-permute-done | bytes 245792 | tf_op jit(solution)/shard_map/ppermute | solution.py:217
  62.0 2.8 %collective-permute-done.13.refs_5_ = bf16[192,640]{1,0:T(8,128)(2,1)S(1)} collective-permute-done((bf16[192,640]{1,0:T(8,128)(2,1)S(1)}, bf16[192,640]{1,0:T(8,128)(2,1)S(1)}, u32[]{:S(2)}, u32[]{:S(2)}) %collective-permute-start.13) | collective-permute-done | bytes 245792 | tf_op jit(solution)/shard_map/ppermute | solution.py:217
  64.7 0.5 combine.3
  65.2 2.8 %collective-permute-start.15 = (bf16[256,640]{1,0:T(8,128)(2,1)S(1)}, bf16[256,640]{1,0:T(8,128)(2,1)S(1)}, u32[]{:S(2)}, u32[]{:S(2)}) collective-permute-start(bf16[256,640]{1,0:T(8,128)(2,1)S(1)} %combine.3), channel_id=1, source_target_pairs={{0,8},{16,24},{1,9},{17,25},{2,10},{18,26},{3,11},{19,27},{4,12},{... | collective-permute-start | bytes 983048 | tf_op jit(solution)/shard_map/ppermute | solution.py:337
  68.0 1.5 %collective-permute-start.14 = (bf16[256,640]{1,0:T(8,128)(2,1)S(1)}, bf16[256,640]{1,0:T(8,128)(2,1)S(1)}, u32[]{:S(2)}, u32[]{:S(2)}) collective-permute-start(bf16[256,640]{1,0:T(8,128)(2,1)S(1)} %combine.3), channel_id=1, source_target_pairs={{0,24},{8,16},{16,8},{24,0},{1,25},{9,17},{17,9},{25,1},{2,26},{10... | collective-permute-start | bytes 983048 | tf_op jit(solution)/shard_map/ppermute | solution.py:336
  69.5 1.3 %collective-permute-done.16.refs_3_ = bf16[192,896]{1,0:T(8,128)(2,1)S(1)} collective-permute-done((bf16[192,896]{1,0:T(8,128)(2,1)S(1)}, bf16[192,896]{1,0:T(8,128)(2,1)S(1)}, u32[]{:S(2)}, u32[]{:S(2)}) %collective-permute-start.16) | collective-permute-done | bytes 344096 | tf_op jit(solution)/shard_map/ppermute | solution.py:217
  70.8 4.7 %collective-permute-done.17.refs_4_ = bf16[192,896]{1,0:T(8,128)(2,1)S(1)} collective-permute-done((bf16[192,896]{1,0:T(8,128)(2,1)S(1)}, bf16[192,896]{1,0:T(8,128)(2,1)S(1)}, u32[]{:S(2)}, u32[]{:S(2)}) %collective-permute-start.17) | collective-permute-done | bytes 344096 | tf_op jit(solution)/shard_map/ppermute | solution.py:217
  75.6 0.6 combine.4.refs_5_
  76.1 3.5 %collective-permute-start.25 = (bf16[256,896]{1,0:T(8,128)(2,1)S(1)}, bf16[256,896]{1,0:T(8,128)(2,1)S(1)}, u32[]{:S(2)}, u32[]{:S(2)}) collective-permute-start(bf16[256,896]{1,0:T(8,128)(2,1)S(1)} %combine.4.refs_5_), channel_id=1, source_target_pairs={{0,8},{16,24},{1,9},{17,25},{2,10},{18,26},{3,11},{19,27},{4,12},{... | collective-permute-start | bytes 1376264 | tf_op jit(solution)/shard_map/ppermute | solution.py:337
  79.7 1.4 %collective-permute-start.24 = (bf16[256,896]{1,0:T(8,128)(2,1)S(1)}, bf16[256,896]{1,0:T(8,128)(2,1)S(1)}, u32[]{:S(2)}, u32[]{:S(2)}) collective-permute-start(bf16[256,896]{1,0:T(8,128)(2,1)S(1)} %combine.4.refs_5_), channel_id=1, source_target_pairs={{0,24},{8,16},{16,8},{24,0},{1,25},{9,17},{17,9},{25,1},{2,26},{10... | collective-permute-start | bytes 1376264 | tf_op jit(solution)/shard_map/ppermute | solution.py:336
  81.1 1.0 second_matmul.3
  82.1 1.4 %collective-permute-start.19 = (bf16[192,512]{1,0:T(8,128)(2,1)S(1)}, bf16[192,512]{1,0:T(8,128)(2,1)S(1)}, u32[]{:S(2)}, u32[]{:S(2)}) collective-permute-start(bf16[192,512]{1,0:T(8,128)(2,1)S(1)} %get-tuple-element.59), channel_id=1, source_target_pairs={{0,2},{1,3},{2,0},{3,1},{4,6},{5,7},{6,4},{7,5},{8,10},{9,11},{10,... | collective-permute-start | bytes 589832 | tf_op jit(solution)/shard_map/ppermute | solution.py:217
  83.5 0.7 collective-permute-start.20
  84.2 1.4 %collective-permute-start.21 = (bf16[192,512]{1,0:T(8,128)(2,1)S(1)}, bf16[192,512]{1,0:T(8,128)(2,1)S(1)}, u32[]{:S(2)}, u32[]{:S(2)}) collective-permute-start(bf16[192,512]{1,0:T(8,128)(2,1)S(1)} %get-tuple-element.61), channel_id=1, source_target_pairs={{0,6},{1,7},{2,4},{3,5},{4,2},{5,3},{6,0},{7,1},{8,14},{9,15},{10,... | collective-permute-start | bytes 589832 | tf_op jit(solution)/shard_map/ppermute | solution.py:217
  85.6 2.2 %collective-permute-done.19.refs_3_ = bf16[192,512]{1,0:T(8,128)(2,1)S(1)} collective-permute-done((bf16[192,512]{1,0:T(8,128)(2,1)S(1)}, bf16[192,512]{1,0:T(8,128)(2,1)S(1)}, u32[]{:S(2)}, u32[]{:S(2)}) %collective-permute-start.19) | collective-permute-done | bytes 196640 | tf_op jit(solution)/shard_map/ppermute | solution.py:217
  87.8 1.3 %collective-permute-done.20.refs_4_ = bf16[192,512]{1,0:T(8,128)(2,1)S(1)} collective-permute-done((bf16[192,512]{1,0:T(8,128)(2,1)S(1)}, bf16[192,512]{1,0:T(8,128)(2,1)S(1)}, u32[]{:S(2)}, u32[]{:S(2)}) %collective-permute-start.20) | collective-permute-done | bytes 196640 | tf_op jit(solution)/shard_map/ppermute | solution.py:217
  89.1 2.1 %collective-permute-done.21.refs_5_ = bf16[192,512]{1,0:T(8,128)(2,1)S(1)} collective-permute-done((bf16[192,512]{1,0:T(8,128)(2,1)S(1)}, bf16[192,512]{1,0:T(8,128)(2,1)S(1)}, u32[]{:S(2)}, u32[]{:S(2)}) %collective-permute-start.21) | collective-permute-done | bytes 196640 | tf_op jit(solution)/shard_map/ppermute | solution.py:217
  91.2 0.4 combine.5
  91.6 3.7 %collective-permute-start.23 = (bf16[256,512]{1,0:T(8,128)(2,1)S(1)}, bf16[256,512]{1,0:T(8,128)(2,1)S(1)}, u32[]{:S(2)}, u32[]{:S(2)}) collective-permute-start(bf16[256,512]{1,0:T(8,128)(2,1)S(1)} %combine.5), channel_id=1, source_target_pairs={{0,8},{16,24},{1,9},{17,25},{2,10},{18,26},{3,11},{19,27},{4,12},{... | collective-permute-start | bytes 786440 | tf_op jit(solution)/shard_map/ppermute | solution.py:337
  95.3 0.1 collective-permute-start.22
  95.4 0.8 place.3
  96.3 4.1 %collective-permute-done.24.refs_1_ = bf16[256,896]{1,0:T(8,128)(2,1)S(1)} collective-permute-done((bf16[256,896]{1,0:T(8,128)(2,1)S(1)}, bf16[256,896]{1,0:T(8,128)(2,1)S(1)}, u32[]{:S(2)}, u32[]{:S(2)}) %collective-permute-start.24) | collective-permute-done | bytes 458784 | tf_op jit(solution)/shard_map/ppermute | solution.py:336
  100.4 0.9 place.4
  101.4 2.9 %collective-permute-done.23.refs_2_ = bf16[256,512]{1,0:T(8,128)(2,1)S(1)} collective-permute-done((bf16[256,512]{1,0:T(8,128)(2,1)S(1)}, bf16[256,512]{1,0:T(8,128)(2,1)S(1)}, u32[]{:S(2)}, u32[]{:S(2)}) %collective-permute-start.23) | collective-permute-done | bytes 262176 | tf_op jit(solution)/shard_map/ppermute | solution.py:337
  104.2 2.9 %collective-permute-done.22.refs_1_ = bf16[256,512]{1,0:T(8,128)(2,1)S(1)} collective-permute-done((bf16[256,512]{1,0:T(8,128)(2,1)S(1)}, bf16[256,512]{1,0:T(8,128)(2,1)S(1)}, u32[]{:S(2)}, u32[]{:S(2)}) %collective-permute-start.22) | collective-permute-done | bytes 262176 | tf_op jit(solution)/shard_map/ppermute | solution.py:336
  107.1 0.8 place.5
  (20 shorter events, 0.0 us)
Async XLA Ops:
  0.6 34.0 %copy-start.6 = (bf16[1,2048,8]{1,2,0:T(8,128)(2,1)S(1)}, bf16[1,2048,8]{1,2,0:T(8,128)(2,1)}, u32[]{:S(2)}) copy-start(bf16[1,2048,8]{1,2,0:T(8,128)(2,1)} %param.9) | copy-start | bytes 98308
  0.6 32.5 %collective-permute-start.3 = (bf16[2048,1024]{1,0:T(8,128)(2,1)}, bf16[2048,1024]{1,0:T(8,128)(2,1)}, u32[]{:S(2)}, u32[]{:S(2)}) collective-permute-start(bf16[2048,1024]{1,0:T(8,128)(2,1)} %bitcast.15), channel_id=1, source_target_pairs={{0,1},{1,0},{2,3},{3,2},{4,5},{5,4},{6,7},{7,6},{8,9},{9,8},{10,11... | collective-permute-start | bytes 12582920 | tf_op jit(solution)/shard_map/ppermute | solution.py:213
  1.2 33.5 %collective-permute-start.10 = (bf16[1024,2048]{1,0:T(8,128)(2,1)}, bf16[1024,2048]{1,0:T(8,128)(2,1)}, u32[]{:S(2)}, u32[]{:S(2)}) collective-permute-start(bf16[1024,2048]{1,0:T(8,128)(2,1)} %bitcast.19), channel_id=1, source_target_pairs={{0,1},{1,0},{2,3},{3,2},{4,5},{5,4},{6,7},{7,6},{8,9},{9,8},{10,11... | collective-permute-start | bytes 12582920 | tf_op jit(solution)/shard_map/ppermute | solution.py:213
  5.2 12.2 %collective-permute-start.7 = (bf16[192,768]{1,0:T(8,128)(2,1)}, bf16[192,768]{1,0:T(8,128)(2,1)S(1)}, u32[]{:S(2)}, u32[]{:S(2)}) collective-permute-start(bf16[192,768]{1,0:T(8,128)(2,1)} %get-tuple-element.46), channel_id=1, source_target_pairs={{0,2},{1,3},{2,0},{3,1},{4,6},{5,7},{6,4},{7,5},{8,10},{9,11},{10,... | collective-permute-start | bytes 884744 | tf_op jit(solution)/shard_map/ppermute | solution.py:217
  8.2 14.6 %collective-permute-start.8 = (bf16[192,768]{1,0:T(8,128)(2,1)}, bf16[192,768]{1,0:T(8,128)(2,1)S(1)}, u32[]{:S(2)}, u32[]{:S(2)}) collective-permute-start(bf16[192,768]{1,0:T(8,128)(2,1)} %get-tuple-element.47), channel_id=1, source_target_pairs={{0,4},{1,5},{2,6},{3,7},{4,0},{5,1},{6,2},{7,3},{8,12},{9,13},{10,... | collective-permute-start | bytes 884744 | tf_op jit(solution)/shard_map/ppermute | solution.py:217
  9.7 15.2 %collective-permute-start.9 = (bf16[192,768]{1,0:T(8,128)(2,1)}, bf16[192,768]{1,0:T(8,128)(2,1)S(1)}, u32[]{:S(2)}, u32[]{:S(2)}) collective-permute-start(bf16[192,768]{1,0:T(8,128)(2,1)} %get-tuple-element.48), channel_id=1, source_target_pairs={{0,6},{1,7},{2,4},{3,5},{4,2},{5,3},{6,0},{7,1},{8,14},{9,15},{10,... | collective-permute-start | bytes 884744 | tf_op jit(solution)/shard_map/ppermute | solution.py:217
  9.8 1.2 %copy-start.2 = (bf16[1,256,2048]{2,1,0:T(8,128)(2,1)S(1)}, bf16[1,256,2048]{2,1,0:T(8,128)(2,1)}, u32[]{:S(2)}) copy-start(bf16[1,256,2048]{2,1,0:T(8,128)(2,1)} %param.7) | copy-start | bytes 3145732
  11.0 1.2 %copy-start.3 = (bf16[1,256,2048]{2,1,0:T(8,128)(2,1)S(1)}, bf16[1,256,2048]{2,1,0:T(8,128)(2,1)}, u32[]{:S(2)}) copy-start(bf16[1,256,2048]{2,1,0:T(8,128)(2,1)} %param.11) | copy-start | bytes 3145732
  12.2 0.7 copy-start.5
  12.9 0.7 copy-start.7
  17.4 13.6 %collective-permute-start.4 = (bf16[192,1024]{1,0:T(8,128)(2,1)S(1)}, bf16[192,1024]{1,0:T(8,128)(2,1)S(1)}, u32[]{:S(2)}, u32[]{:S(2)}) collective-permute-start(bf16[192,1024]{1,0:T(8,128)(2,1)S(1)} %get-tuple-element.42), channel_id=1, source_target_pairs={{0,2},{1,3},{2,0},{3,1},{4,6},{5,7},{6,4},{7,5},{8,10},{9,11},{10,... | collective-permute-start | bytes 1179656 | tf_op jit(solution)/shard_map/ppermute | solution.py:217
  22.8 21.7 %collective-permute-start.5 = (bf16[192,1024]{1,0:T(8,128)(2,1)S(1)}, bf16[192,1024]{1,0:T(8,128)(2,1)S(1)}, u32[]{:S(2)}, u32[]{:S(2)}) collective-permute-start(bf16[192,1024]{1,0:T(8,128)(2,1)S(1)} %get-tuple-element.43), channel_id=1, source_target_pairs={{0,4},{1,5},{2,6},{3,7},{4,0},{5,1},{6,2},{7,3},{8,12},{9,13},{10,... | collective-permute-start | bytes 1179656 | tf_op jit(solution)/shard_map/ppermute | solution.py:217
  25.0 19.5 %collective-permute-start.6 = (bf16[192,1024]{1,0:T(8,128)(2,1)S(1)}, bf16[192,1024]{1,0:T(8,128)(2,1)S(1)}, u32[]{:S(2)}, u32[]{:S(2)}) collective-permute-start(bf16[192,1024]{1,0:T(8,128)(2,1)S(1)} %get-tuple-element.44), channel_id=1, source_target_pairs={{0,6},{1,7},{2,4},{3,5},{4,2},{5,3},{6,0},{7,1},{8,14},{9,15},{10,... | collective-permute-start | bytes 1179656 | tf_op jit(solution)/shard_map/ppermute | solution.py:217
  31.0 15.3 %collective-permute-start = (bf16[192,256]{1,0:T(8,128)(2,1)S(1)}, bf16[192,256]{1,0:T(8,128)(2,1)S(1)}, u32[]{:S(2)}, u32[]{:S(2)}) collective-permute-start(bf16[192,256]{1,0:T(8,128)(2,1)S(1)} %get-tuple-element.38), channel_id=1, source_target_pairs={{0,2},{1,3},{2,0},{3,1},{4,6},{5,7},{6,4},{7,5},{8,10},{9,11},{10,... | collective-permute-start | bytes 294920 | tf_op jit(solution)/shard_map/ppermute | solution.py:217
  33.1 13.2 %collective-permute-start.1 = (bf16[192,256]{1,0:T(8,128)(2,1)S(1)}, bf16[192,256]{1,0:T(8,128)(2,1)S(1)}, u32[]{:S(2)}, u32[]{:S(2)}) collective-permute-start(bf16[192,256]{1,0:T(8,128)(2,1)S(1)} %get-tuple-element.39), channel_id=1, source_target_pairs={{0,4},{1,5},{2,6},{3,7},{4,0},{5,1},{6,2},{7,3},{8,12},{9,13},{10,... | collective-permute-start | bytes 294920 | tf_op jit(solution)/shard_map/ppermute | solution.py:217
  34.6 11.7 %collective-permute-start.2 = (bf16[192,256]{1,0:T(8,128)(2,1)S(1)}, bf16[192,256]{1,0:T(8,128)(2,1)S(1)}, u32[]{:S(2)}, u32[]{:S(2)}) collective-permute-start(bf16[192,256]{1,0:T(8,128)(2,1)S(1)} %get-tuple-element.40), channel_id=1, source_target_pairs={{0,6},{1,7},{2,4},{3,5},{4,2},{5,3},{6,0},{7,1},{8,14},{9,15},{10,... | collective-permute-start | bytes 294920 | tf_op jit(solution)/shard_map/ppermute | solution.py:217
  38.8 3.5 %copy-start = (bf16[1,1,2048,1024]{3,2,1,0:T(8,128)(2,1)S(1)}, bf16[1,1,2048,1024]{3,2,1,0:T(8,128)(2,1)}, u32[]{:S(2)}) copy-start(bf16[1,1,2048,1024]{3,2,1,0:T(8,128)(2,1)} %param.12) | copy-start | bytes 12582916
  38.8 3.5 %copy-start.4 = (bf16[192,768]{1,0:T(8,128)(2,1)S(1)}, bf16[192,768]{1,0:T(8,128)(2,1)}, u32[]{:S(2)}) copy-start(bf16[192,768]{1,0:T(8,128)(2,1)} %get-tuple-element.45.refs_0_) | copy-start | bytes 884740
  44.5 2.2 %copy-start.1 = (bf16[1,1,1024,2048]{3,2,1,0:T(8,128)(2,1)S(1)}, bf16[1,1,1024,2048]{3,2,1,0:T(8,128)(2,1)}, u32[]{:S(2)}) copy-start(bf16[1,1,1024,2048]{3,2,1,0:T(8,128)(2,1)} %param.13) | copy-start | bytes 12582916
  49.2 9.0 %collective-permute-start.11 = (bf16[192,640]{1,0:T(8,128)(2,1)S(1)}, bf16[192,640]{1,0:T(8,128)(2,1)S(1)}, u32[]{:S(2)}, u32[]{:S(2)}) collective-permute-start(bf16[192,640]{1,0:T(8,128)(2,1)S(1)} %get-tuple-element.51), channel_id=1, source_target_pairs={{0,2},{1,3},{2,0},{3,1},{4,6},{5,7},{6,4},{7,5},{8,10},{9,11},{10,... | collective-permute-start | bytes 737288 | tf_op jit(solution)/shard_map/ppermute | solution.py:217
  50.4 11.6 %collective-permute-start.12 = (bf16[192,640]{1,0:T(8,128)(2,1)S(1)}, bf16[192,640]{1,0:T(8,128)(2,1)S(1)}, u32[]{:S(2)}, u32[]{:S(2)}) collective-permute-start(bf16[192,640]{1,0:T(8,128)(2,1)S(1)} %get-tuple-element.52), channel_id=1, source_target_pairs={{0,4},{1,5},{2,6},{3,7},{4,0},{5,1},{6,2},{7,3},{8,12},{9,13},{10,... | collective-permute-start | bytes 737288 | tf_op jit(solution)/shard_map/ppermute | solution.py:217
  51.9 12.8 %collective-permute-start.13 = (bf16[192,640]{1,0:T(8,128)(2,1)S(1)}, bf16[192,640]{1,0:T(8,128)(2,1)S(1)}, u32[]{:S(2)}, u32[]{:S(2)}) collective-permute-start(bf16[192,640]{1,0:T(8,128)(2,1)S(1)} %get-tuple-element.53), channel_id=1, source_target_pairs={{0,6},{1,7},{2,4},{3,5},{4,2},{5,3},{6,0},{7,1},{8,14},{9,15},{10,... | collective-permute-start | bytes 737288 | tf_op jit(solution)/shard_map/ppermute | solution.py:217
  54.6 16.3 %collective-permute-start.16 = (bf16[192,896]{1,0:T(8,128)(2,1)S(1)}, bf16[192,896]{1,0:T(8,128)(2,1)S(1)}, u32[]{:S(2)}, u32[]{:S(2)}) collective-permute-start(bf16[192,896]{1,0:T(8,128)(2,1)S(1)} %get-tuple-element.55), channel_id=1, source_target_pairs={{0,2},{1,3},{2,0},{3,1},{4,6},{5,7},{6,4},{7,5},{8,10},{9,11},{10,... | collective-permute-start | bytes 1032200 | tf_op jit(solution)/shard_map/ppermute | solution.py:217
  55.8 19.8 %collective-permute-start.17 = (bf16[192,896]{1,0:T(8,128)(2,1)S(1)}, bf16[192,896]{1,0:T(8,128)(2,1)S(1)}, u32[]{:S(2)}, u32[]{:S(2)}) collective-permute-start(bf16[192,896]{1,0:T(8,128)(2,1)S(1)} %get-tuple-element.56), channel_id=1, source_target_pairs={{0,4},{1,5},{2,6},{3,7},{4,0},{5,1},{6,2},{7,3},{8,12},{9,13},{10,... | collective-permute-start | bytes 1032200 | tf_op jit(solution)/shard_map/ppermute | solution.py:217
  58.2 17.3 %collective-permute-start.18 = (bf16[192,896]{1,0:T(8,128)(2,1)S(1)}, bf16[192,896]{1,0:T(8,128)(2,1)S(1)}, u32[]{:S(2)}, u32[]{:S(2)}) collective-permute-start(bf16[192,896]{1,0:T(8,128)(2,1)S(1)} %get-tuple-element.57), channel_id=1, source_target_pairs={{0,6},{1,7},{2,4},{3,5},{4,2},{5,3},{6,0},{7,1},{8,14},{9,15},{10,... | collective-permute-start | bytes 1032200 | tf_op jit(solution)/shard_map/ppermute | solution.py:217
  65.2 15.9 %collective-permute-start.15 = (bf16[256,640]{1,0:T(8,128)(2,1)S(1)}, bf16[256,640]{1,0:T(8,128)(2,1)S(1)}, u32[]{:S(2)}, u32[]{:S(2)}) collective-permute-start(bf16[256,640]{1,0:T(8,128)(2,1)S(1)} %combine.3), channel_id=1, source_target_pairs={{0,8},{16,24},{1,9},{17,25},{2,10},{18,26},{3,11},{19,27},{4,12},{... | collective-permute-start | bytes 983048 | tf_op jit(solution)/shard_map/ppermute | solution.py:337
  68.0 13.1 %collective-permute-start.14 = (bf16[256,640]{1,0:T(8,128)(2,1)S(1)}, bf16[256,640]{1,0:T(8,128)(2,1)S(1)}, u32[]{:S(2)}, u32[]{:S(2)}) collective-permute-start(bf16[256,640]{1,0:T(8,128)(2,1)S(1)} %combine.3), channel_id=1, source_target_pairs={{0,24},{8,16},{16,8},{24,0},{1,25},{9,17},{17,9},{25,1},{2,26},{10... | collective-permute-start | bytes 983048 | tf_op jit(solution)/shard_map/ppermute | solution.py:336
  76.1 20.1 %collective-permute-start.25 = (bf16[256,896]{1,0:T(8,128)(2,1)S(1)}, bf16[256,896]{1,0:T(8,128)(2,1)S(1)}, u32[]{:S(2)}, u32[]{:S(2)}) collective-permute-start(bf16[256,896]{1,0:T(8,128)(2,1)S(1)} %combine.4.refs_5_), channel_id=1, source_target_pairs={{0,8},{16,24},{1,9},{17,25},{2,10},{18,26},{3,11},{19,27},{4,12},{... | collective-permute-start | bytes 1376264 | tf_op jit(solution)/shard_map/ppermute | solution.py:337
  79.7 20.8 %collective-permute-start.24 = (bf16[256,896]{1,0:T(8,128)(2,1)S(1)}, bf16[256,896]{1,0:T(8,128)(2,1)S(1)}, u32[]{:S(2)}, u32[]{:S(2)}) collective-permute-start(bf16[256,896]{1,0:T(8,128)(2,1)S(1)} %combine.4.refs_5_), channel_id=1, source_target_pairs={{0,24},{8,16},{16,8},{24,0},{1,25},{9,17},{17,9},{25,1},{2,26},{10... | collective-permute-start | bytes 1376264 | tf_op jit(solution)/shard_map/ppermute | solution.py:336
  82.1 5.7 %collective-permute-start.19 = (bf16[192,512]{1,0:T(8,128)(2,1)S(1)}, bf16[192,512]{1,0:T(8,128)(2,1)S(1)}, u32[]{:S(2)}, u32[]{:S(2)}) collective-permute-start(bf16[192,512]{1,0:T(8,128)(2,1)S(1)} %get-tuple-element.59), channel_id=1, source_target_pairs={{0,2},{1,3},{2,0},{3,1},{4,6},{5,7},{6,4},{7,5},{8,10},{9,11},{10,... | collective-permute-start | bytes 589832 | tf_op jit(solution)/shard_map/ppermute | solution.py:217
  83.5 5.7 %collective-permute-start.20 = (bf16[192,512]{1,0:T(8,128)(2,1)S(1)}, bf16[192,512]{1,0:T(8,128)(2,1)S(1)}, u32[]{:S(2)}, u32[]{:S(2)}) collective-permute-start(bf16[192,512]{1,0:T(8,128)(2,1)S(1)} %get-tuple-element.60), channel_id=1, source_target_pairs={{0,4},{1,5},{2,6},{3,7},{4,0},{5,1},{6,2},{7,3},{8,12},{9,13},{10,... | collective-permute-start | bytes 589832 | tf_op jit(solution)/shard_map/ppermute | solution.py:217
  84.2 7.0 %collective-permute-start.21 = (bf16[192,512]{1,0:T(8,128)(2,1)S(1)}, bf16[192,512]{1,0:T(8,128)(2,1)S(1)}, u32[]{:S(2)}, u32[]{:S(2)}) collective-permute-start(bf16[192,512]{1,0:T(8,128)(2,1)S(1)} %get-tuple-element.61), channel_id=1, source_target_pairs={{0,6},{1,7},{2,4},{3,5},{4,2},{5,3},{6,0},{7,1},{8,14},{9,15},{10,... | collective-permute-start | bytes 589832 | tf_op jit(solution)/shard_map/ppermute | solution.py:217
  91.6 12.6 %collective-permute-start.23 = (bf16[256,512]{1,0:T(8,128)(2,1)S(1)}, bf16[256,512]{1,0:T(8,128)(2,1)S(1)}, u32[]{:S(2)}, u32[]{:S(2)}) collective-permute-start(bf16[256,512]{1,0:T(8,128)(2,1)S(1)} %combine.5), channel_id=1, source_target_pairs={{0,8},{16,24},{1,9},{17,25},{2,10},{18,26},{3,11},{19,27},{4,12},{... | collective-permute-start | bytes 786440 | tf_op jit(solution)/shard_map/ppermute | solution.py:337
  95.3 11.8 %collective-permute-start.22 = (bf16[256,512]{1,0:T(8,128)(2,1)S(1)}, bf16[256,512]{1,0:T(8,128)(2,1)S(1)}, u32[]{:S(2)}, u32[]{:S(2)}) collective-permute-start(bf16[256,512]{1,0:T(8,128)(2,1)S(1)} %combine.5), channel_id=1, source_target_pairs={{0,24},{8,16},{16,8},{24,0},{1,25},{9,17},{17,9},{25,1},{2,26},{10... | collective-permute-start | bytes 786440 | tf_op jit(solution)/shard_map/ppermute | solution.py:336
